TPU v7x, 1024 devices: a whole 4x4x32 slice. The times are simulated.
1024 devices in a mesh: gx: 16 (over y, x), gy: 64 (over z, core).
Axes of the slice: x: 4, y: 4, z: 32, core: 2. Of those that a mesh axis runs over, the one named last changes fastest.
Arguments:
- background: float32 [8, 1024, 2048], P(None, 'gy', 'gx'), may hold values from 1 to 12
- density: float32 [1024, 2048], P('gy', 'gx'), may hold values from 0 to 1
- design_tiles: int32 [8, 16], replicated, may hold values 0 or 1
- material_tiles: int32 [8, 16], replicated, may hold values from 0 to 3
- contrast: float32 [4], replicated, may hold values from 2 to 10
- source: float32 [3, 8, 1024, 2048], P(None, None, 'gy', 'gx'), may hold values from -18 to 18
- adjoint_source: float32 [3, 8, 1024, 2048], P(None, None, 'gy', 'gx'), may hold values from -18 to 18
- field_start: float32 [3, 8, 1024, 2048], P(None, None, 'gy', 'gx'), may hold values from -6 to 6
- adjoint_start: float32 [3, 8, 1024, 2048], P(None, None, 'gy', 'gx'), may hold values from -6 to 6
Outputs:
- field: float32 [3, 8, 1024, 2048], P(None, None, 'gy', 'gx')
- adjoint: float32 [3, 8, 1024, 2048], P(None, None, 'gy', 'gx')
- gradient: float32 [1024, 2048], P('gy', 'gx')
All inputs are finite; a program needn't handle non-finite values.
Results may differ from a plain program's by a relative error of at most 0.00019.
Values sent between devices are 32-bit elements; how exact they have to be, the bound alone decides.
No kernel may reach another device: no remote copies, remote signals or barrier semaphores. Data moves between devices by JAX's collectives and lax.ppermute only.
A program may use at most 32 MiB of HBM per device.

v0:
```python
import math

import jax
import jax.numpy as jnp
from jax import lax
from jax.sharding import PartitionSpec as P

ITERS = 4
RADIUS = 8
TILE = 128
MATERIALS = 4


wave_square = 0.5
relaxation = 0.5


def padded_2(value, sides, width):
    for axis, dim in sides:
        size, length = (lax.axis_size(axis), value.shape[dim])
        up = [(i, (i + 1) % size) for i in range(size - 1)]
        down = [(j, i) for i, j in up]
        last = lax.slice_in_dim(value, length - width, length, axis=dim)
        initial = lax.slice_in_dim(value, 0, width, axis=dim)
        before = lax.ppermute(last, axis, up)
        after = lax.ppermute(initial, axis, down)
        value = jnp.concatenate([before, value, after], axis=dim)
    return value


def cone_total():
    total = 0.0
    for row_shift in range(-RADIUS, RADIUS + 1):
        for col_shift in range(-RADIUS, RADIUS + 1):
            total = total + max(
                0.0, RADIUS + 1 - math.sqrt(row_shift * row_shift + col_shift * col_shift)
            )
    return total


def cone_filter(padded, rows, cols):
    row_shift = jnp.arange(2 * RADIUS + 1, dtype=jnp.float32)[:, None, None] - RADIUS
    col_shift = (
        jnp.arange(cols + 2 * RADIUS)[:, None] - jnp.arange(cols)[None, :] - RADIUS
    ).astype(jnp.float32)[None]
    distance = jnp.sqrt(row_shift * row_shift + col_shift * col_shift)
    table = jnp.where(jnp.abs(col_shift) <= RADIUS, jnp.maximum(0.0, RADIUS + 1 - distance), 0.0)
    slabs = jnp.stack([padded[offset : offset + rows] for offset in range(2 * RADIUS + 1)])
    result = jnp.einsum("krc,kcx->rx", slabs, table, precision=lax.Precision.HIGHEST)
    return result / cone_total()


def take_span(array, axis, chosen, others):
    index = [slice(None)] * array.ndim
    for other in (-3, -2, -1):
        index[other] = others
    index[axis] = chosen
    return array[tuple(index)]


def forward_diff(array, axis):
    return take_span(array, axis, slice(1, None), slice(None, -1)) - take_span(
        array, axis, slice(None, -1), slice(None, -1)
    )


def backward_diff(array, axis):
    return take_span(array, axis, slice(1, None), slice(1, None)) - take_span(
        array, axis, slice(None, -1), slice(1, None)
    )


def curl_curl(padded):
    along_x = padded[..., 0, :, :, :]
    along_y = padded[..., 1, :, :, :]
    along_z = padded[..., 2, :, :, :]
    magnet_x = forward_diff(along_z, -2) - forward_diff(along_y, -3)
    magnet_y = forward_diff(along_x, -3) - forward_diff(along_z, -1)
    magnet_z = forward_diff(along_y, -1) - forward_diff(along_x, -2)
    curl_x = backward_diff(magnet_z, -2) - backward_diff(magnet_y, -3)
    curl_y = backward_diff(magnet_x, -3) - backward_diff(magnet_z, -1)
    curl_z = backward_diff(magnet_y, -1) - backward_diff(magnet_x, -2)
    return jnp.stack([curl_x, curl_y, curl_z], axis=-4)


def relax_sweep(fields, padded, sources, permittivity):
    image = curl_curl(padded) + wave_square * permittivity * fields
    return fields + relaxation * (sources - image) / (4.0 + wave_square * permittivity)


def pad_depth(array):
    return jnp.pad(array, [(0, 0), (0, 0), (1, 1), (0, 0), (0, 0)])


def tile_spread(tile_gain, row_first, col_first, rows, cols):
    row_tile = jnp.floor_divide(row_first + jnp.arange(rows, dtype=jnp.int32), TILE)
    col_tile = jnp.floor_divide(col_first + jnp.arange(cols, dtype=jnp.int32), TILE)
    row_tile = jnp.where(row_first + jnp.arange(rows, dtype=jnp.int32) < 0, -1, row_tile)
    col_tile = jnp.where(col_first + jnp.arange(cols, dtype=jnp.int32) < 0, -1, col_tile)
    pick_rows = (
        row_tile[:, None] == jnp.arange(tile_gain.shape[0], dtype=jnp.int32)[None, :]
    ).astype(jnp.float32)
    pick_cols = (
        jnp.arange(tile_gain.shape[1], dtype=jnp.int32)[:, None] == col_tile[None, :]
    ).astype(jnp.float32)
    return jnp.dot(
        jnp.dot(pick_rows, tile_gain, precision=lax.Precision.HIGHEST),
        pick_cols,
        precision=lax.Precision.HIGHEST,
    )


def on_device(
    background,
    density,
    design_tiles,
    material_tiles,
    contrast,
    source,
    adjoint_source,
    field_start,
    adjoint_start,
):
    rows, cols = density.shape
    chosen = (
        material_tiles[:, :, None] == jnp.arange(MATERIALS, dtype=jnp.int32)[None, None, :]
    ).astype(jnp.float32)
    tile_gain = design_tiles.astype(jnp.float32) * jnp.sum(chosen * contrast[None, None, :], axis=2)
    row_first = lax.axis_index("gy") * rows
    col_first = lax.axis_index("gx") * cols
    gain = tile_spread(tile_gain, row_first, col_first, rows, cols)
    reach = RADIUS
    density_wide = padded_2(density, (("gx", 1), ("gy", 0)), reach)
    fields = jnp.stack([field_start, adjoint_start])
    sources = jnp.stack([source, adjoint_source])
    filtered = cone_filter(density_wide, rows, cols)
    permittivity = background + (gain * filtered)[None]
    for sweep_number in range(ITERS):
        forward_wide = padded_2(fields[0], (("gx", 3), ("gy", 2)), 1)
        adjoint_wide = padded_2(fields[1], (("gx", 3), ("gy", 2)), 1)
        padded = jnp.stack([forward_wide, adjoint_wide])
        fields = relax_sweep(fields, pad_depth(padded), sources, permittivity)
    field = fields[0]
    adjoint = fields[1]
    local = -wave_square * gain * jnp.sum(adjoint * field, axis=(0, 1))
    local_wide = padded_2(local, (("gx", 1), ("gy", 0)), RADIUS)
    gradient = cone_filter(local_wide, rows, cols)
    return (field, adjoint, gradient)


def solution(mesh):
    in_specs = (
        P(None, "gy", "gx"),
        P("gy", "gx"),
        P(),
        P(),
        P(),
        P(None, None, "gy", "gx"),
        P(None, None, "gy", "gx"),
        P(None, None, "gy", "gx"),
        P(None, None, "gy", "gx"),
    )
    out_specs = (P(None, None, "gy", "gx"), P(None, None, "gy", "gx"), P("gy", "gx"))
    return jax.shard_map(
        on_device, mesh=mesh, in_specs=in_specs, out_specs=out_specs, check_vma=False
    )
```

profile of v0, /device:TPU:902, one launch (start us, length us, event | category | flops | bytes accessed | tf_op | source)
XLA Modules:
  0.0 174.8 jit_solution(1463822514953364580)
XLA Ops:
  0.7 0.9 fusion.94
  1.6 3.4 %collective-permute-start.8 = (f32[16,8]{1,0:T(8,128)S(1)}, f32[16,8]{1,0:T(8,128)S(1)}, u32[]{:S(2)}, u32[]{:S(2)}) collective-permute-start(f32[16,8]{1,0:T(8,128)S(1)} %get-tuple-element.92), channel_id=1, source_target_pairs={{0,64},{64,128},{128,192},{192,256},{256,320},{320,384},{384,448},... | collective-permute-start | bytes 1544 | tf_op jit(solution)/shard_map/ppermute | solution.py:25
  5.0 2.4 %collective-permute-start.9 = (f32[16,8]{1,0:T(8,128)S(1)}, f32[16,8]{1,0:T(8,128)S(1)}, u32[]{:S(2)}, u32[]{:S(2)}) collective-permute-start(f32[16,8]{1,0:T(8,128)S(1)} %get-tuple-element.93), channel_id=1, source_target_pairs={{64,0},{128,64},{192,128},{256,192},{320,256},{384,320},{448,384},... | collective-permute-start | bytes 1544 | tf_op jit(solution)/shard_map/ppermute | solution.py:26
  7.4 1.1 fusion.89
  8.6 5.5 %collective-permute-start = (f32[3,8,16,1]{3,2,1,0:T(8,128)S(1)}, f32[3,8,16,1]{3,2,1,0:T(8,128)S(1)}, u32[]{:S(2)}, u32[]{:S(2)}) collective-permute-start(f32[3,8,16,1]{3,2,1,0:T(8,128)S(1)} %get-tuple-element.78), channel_id=1, source_target_pairs={{0,64},{64,128},{128,192},{192,256},{256,320},{320,384},{384,448},... | collective-permute-start | bytes 4616 | tf_op jit(solution)/shard_map/ppermute | solution.py:25
  14.1 1.9 %collective-permute-start.1 = (f32[3,8,16,1]{3,2,1,0:T(8,128)S(1)}, f32[3,8,16,1]{3,2,1,0:T(8,128)S(1)}, u32[]{:S(2)}, u32[]{:S(2)}) collective-permute-start(f32[3,8,16,1]{3,2,1,0:T(8,128)S(1)} %get-tuple-element.79), channel_id=1, source_target_pairs={{64,0},{128,64},{192,128},{256,192},{320,256},{384,320},{448,384},... | collective-permute-start | bytes 4616 | tf_op jit(solution)/shard_map/ppermute | solution.py:26
  16.0 1.1 fusion.90
  17.2 6.0 %collective-permute-start.4 = (f32[3,8,16,1]{3,2,1,0:T(8,128)S(1)}, f32[3,8,16,1]{3,2,1,0:T(8,128)S(1)}, u32[]{:S(2)}, u32[]{:S(2)}) collective-permute-start(f32[3,8,16,1]{3,2,1,0:T(8,128)S(1)} %get-tuple-element.80), channel_id=1, source_target_pairs={{0,64},{64,128},{128,192},{192,256},{256,320},{320,384},{384,448},... | collective-permute-start | bytes 4616 | tf_op jit(solution)/shard_map/ppermute | solution.py:25
  23.8 1.9 %collective-permute-start.5 = (f32[3,8,16,1]{3,2,1,0:T(8,128)S(1)}, f32[3,8,16,1]{3,2,1,0:T(8,128)S(1)}, u32[]{:S(2)}, u32[]{:S(2)}) collective-permute-start(f32[3,8,16,1]{3,2,1,0:T(8,128)S(1)} %get-tuple-element.81), channel_id=1, source_target_pairs={{64,0},{128,64},{192,128},{256,192},{320,256},{384,320},{448,384},... | collective-permute-start | bytes 4616 | tf_op jit(solution)/shard_map/ppermute | solution.py:26
  25.8 2.2 %collective-permute-start.11 = (f32[8,144]{1,0:T(8,128)S(1)}, f32[8,144]{1,0:T(8,128)S(1)}, u32[]{:S(2)}, u32[]{:S(2)}) collective-permute-start(f32[8,144]{1,0:T(8,128)S(1)} %get-tuple-element.88), channel_id=1, source_target_pairs={{1,0},{2,1},{3,2},{4,3},{5,4},{6,5},{7,6},{8,7},{9,8},{10,9},{11,1... | collective-permute-start | bytes 13832 | tf_op jit(solution)/shard_map/ppermute | solution.py:26
  28.0 2.2 %collective-permute-start.10 = (f32[8,144]{1,0:T(8,128)S(1)}, f32[8,144]{1,0:T(8,128)S(1)}, u32[]{:S(2)}, u32[]{:S(2)}) collective-permute-start(f32[8,144]{1,0:T(8,128)S(1)} %get-tuple-element.89), channel_id=1, source_target_pairs={{0,1},{1,2},{2,3},{3,4},{4,5},{5,6},{6,7},{7,8},{8,9},{9,10},{10,1... | collective-permute-start | bytes 13832 | tf_op jit(solution)/shard_map/ppermute | solution.py:25
  30.4 2.5 %collective-permute-start.2 = (f32[3,8,1,130]{3,2,1,0:T(1,128)S(1)}, f32[3,8,1,130]{3,2,1,0:T(1,128)S(1)}, u32[]{:S(2)}, u32[]{:S(2)}) collective-permute-start(f32[3,8,1,130]{3,2,1,0:T(1,128)S(1)} %get-tuple-element.32), channel_id=1, source_target_pairs={{0,1},{1,2},{2,3},{3,4},{4,5},{5,6},{6,7},{7,8},{8,9},{9,10},{10,1... | collective-permute-start | bytes 37448 | tf_op jit(solution)/shard_map/ppermute | solution.py:25
  33.0 4.4 %collective-permute-start.3 = (f32[3,8,1,130]{3,2,1,0:T(1,128)S(1)}, f32[3,8,1,130]{3,2,1,0:T(1,128)S(1)}, u32[]{:S(2)}, u32[]{:S(2)}) collective-permute-start(f32[3,8,1,130]{3,2,1,0:T(1,128)S(1)} %get-tuple-element.33), channel_id=1, source_target_pairs={{1,0},{2,1},{3,2},{4,3},{5,4},{6,5},{7,6},{8,7},{9,8},{10,9},{11,1... | collective-permute-start | bytes 37448 | tf_op jit(solution)/shard_map/ppermute | solution.py:26
  37.6 1.9 %collective-permute-start.6 = (f32[3,8,1,130]{3,2,1,0:T(1,128)S(1)}, f32[3,8,1,130]{3,2,1,0:T(1,128)S(1)}, u32[]{:S(2)}, u32[]{:S(2)}) collective-permute-start(f32[3,8,1,130]{3,2,1,0:T(1,128)S(1)} %get-tuple-element.34), channel_id=1, source_target_pairs={{0,1},{1,2},{2,3},{3,4},{4,5},{5,6},{6,7},{7,8},{8,9},{9,10},{10,1... | collective-permute-start | bytes 37448 | tf_op jit(solution)/shard_map/ppermute | solution.py:25
  39.5 4.9 %collective-permute-start.7 = (f32[3,8,1,130]{3,2,1,0:T(1,128)S(1)}, f32[3,8,1,130]{3,2,1,0:T(1,128)S(1)}, u32[]{:S(2)}, u32[]{:S(2)}) collective-permute-start(f32[3,8,1,130]{3,2,1,0:T(1,128)S(1)} %get-tuple-element.35), channel_id=1, source_target_pairs={{1,0},{2,1},{3,2},{4,3},{5,4},{6,5},{7,6},{8,7},{9,8},{10,9},{11,1... | collective-permute-start | bytes 37448 | tf_op jit(solution)/shard_map/ppermute | solution.py:26
  44.7 1.5 fusion.8
  46.6 0.3 maximum_bitcast_fusion.1
  47.2 0.3 fusion.30
  47.6 0.3 fusion.70
  47.9 0.6 copy-done.2
  48.8 6.0 %collective-permute-start.12 = (f32[3,8,16,1]{3,2,1,0:T(8,128)S(1)}, f32[3,8,16,1]{3,2,1,0:T(8,128)S(1)}, u32[]{:S(2)}, u32[]{:S(2)}) collective-permute-start(f32[3,8,16,1]{3,2,1,0:T(8,128)S(1)} %get-tuple-element.74), channel_id=1, source_target_pairs={{0,64},{64,128},{128,192},{192,256},{256,320},{320,384},{384,448},... | collective-permute-start | bytes 4616 | tf_op jit(solution)/shard_map/ppermute | solution.py:25
  54.9 1.9 %collective-permute-start.13 = (f32[3,8,16,1]{3,2,1,0:T(8,128)S(1)}, f32[3,8,16,1]{3,2,1,0:T(8,128)S(1)}, u32[]{:S(2)}, u32[]{:S(2)}) collective-permute-start(f32[3,8,16,1]{3,2,1,0:T(8,128)S(1)} %get-tuple-element.75), channel_id=1, source_target_pairs={{64,0},{128,64},{192,128},{256,192},{320,256},{384,320},{448,384},... | collective-permute-start | bytes 4616 | tf_op jit(solution)/shard_map/ppermute | solution.py:26
  56.9 6.0 %collective-permute-start.16 = (f32[3,8,16,1]{3,2,1,0:T(8,128)S(1)}, f32[3,8,16,1]{3,2,1,0:T(8,128)S(1)}, u32[]{:S(2)}, u32[]{:S(2)}) collective-permute-start(f32[3,8,16,1]{3,2,1,0:T(8,128)S(1)} %get-tuple-element.76), channel_id=1, source_target_pairs={{0,64},{64,128},{128,192},{192,256},{256,320},{320,384},{384,448},... | collective-permute-start | bytes 4616 | tf_op jit(solution)/shard_map/ppermute | solution.py:25
  63.0 1.9 %collective-permute-start.17 = (f32[3,8,16,1]{3,2,1,0:T(8,128)S(1)}, f32[3,8,16,1]{3,2,1,0:T(8,128)S(1)}, u32[]{:S(2)}, u32[]{:S(2)}) collective-permute-start(f32[3,8,16,1]{3,2,1,0:T(8,128)S(1)} %get-tuple-element.77), channel_id=1, source_target_pairs={{64,0},{128,64},{192,128},{256,192},{320,256},{384,320},{448,384},... | collective-permute-start | bytes 4616 | tf_op jit(solution)/shard_map/ppermute | solution.py:26
  65.1 1.9 %collective-permute-start.14 = (f32[3,8,1,130]{3,2,1,0:T(1,128)S(1)}, f32[3,8,1,130]{3,2,1,0:T(1,128)S(1)}, u32[]{:S(2)}, u32[]{:S(2)}) collective-permute-start(f32[3,8,1,130]{3,2,1,0:T(1,128)S(1)} %get-tuple-element.28), channel_id=1, source_target_pairs={{0,1},{1,2},{2,3},{3,4},{4,5},{5,6},{6,7},{7,8},{8,9},{9,10},{10,1... | collective-permute-start | bytes 37448 | tf_op jit(solution)/shard_map/ppermute | solution.py:25
  67.1 4.9 %collective-permute-start.15 = (f32[3,8,1,130]{3,2,1,0:T(1,128)S(1)}, f32[3,8,1,130]{3,2,1,0:T(1,128)S(1)}, u32[]{:S(2)}, u32[]{:S(2)}) collective-permute-start(f32[3,8,1,130]{3,2,1,0:T(1,128)S(1)} %get-tuple-element.29), channel_id=1, source_target_pairs={{1,0},{2,1},{3,2},{4,3},{5,4},{6,5},{7,6},{8,7},{9,8},{10,9},{11,1... | collective-permute-start | bytes 37448 | tf_op jit(solution)/shard_map/ppermute | solution.py:26
  71.9 0.7 collective-permute-done.17
  72.9 1.9 %collective-permute-start.18 = (f32[3,8,1,130]{3,2,1,0:T(1,128)S(1)}, f32[3,8,1,130]{3,2,1,0:T(1,128)S(1)}, u32[]{:S(2)}, u32[]{:S(2)}) collective-permute-start(f32[3,8,1,130]{3,2,1,0:T(1,128)S(1)} %get-tuple-element.30), channel_id=1, source_target_pairs={{0,1},{1,2},{2,3},{3,4},{4,5},{5,6},{6,7},{7,8},{8,9},{9,10},{10,1... | collective-permute-start | bytes 37448 | tf_op jit(solution)/shard_map/ppermute | solution.py:25
  74.8 4.9 %collective-permute-start.19 = (f32[3,8,1,130]{3,2,1,0:T(1,128)S(1)}, f32[3,8,1,130]{3,2,1,0:T(1,128)S(1)}, u32[]{:S(2)}, u32[]{:S(2)}) collective-permute-start(f32[3,8,1,130]{3,2,1,0:T(1,128)S(1)} %get-tuple-element.31), channel_id=1, source_target_pairs={{1,0},{2,1},{3,2},{4,3},{5,4},{6,5},{7,6},{8,7},{9,8},{10,9},{11,1... | collective-permute-start | bytes 37448 | tf_op jit(solution)/shard_map/ppermute | solution.py:26
  80.0 1.2 collective-permute-done.19
  81.7 0.3 fusion.27
  82.1 0.3 fusion.64
  82.7 5.3 %collective-permute-start.20 = (f32[3,8,16,1]{3,2,1,0:T(8,128)S(1)}, f32[3,8,16,1]{3,2,1,0:T(8,128)S(1)}, u32[]{:S(2)}, u32[]{:S(2)}) collective-permute-start(f32[3,8,16,1]{3,2,1,0:T(8,128)S(1)} %get-tuple-element.70), channel_id=1, source_target_pairs={{0,64},{64,128},{128,192},{192,256},{256,320},{320,384},{384,448},... | collective-permute-start | bytes 4616 | tf_op jit(solution)/shard_map/ppermute | solution.py:25
  88.1 1.9 %collective-permute-start.21 = (f32[3,8,16,1]{3,2,1,0:T(8,128)S(1)}, f32[3,8,16,1]{3,2,1,0:T(8,128)S(1)}, u32[]{:S(2)}, u32[]{:S(2)}) collective-permute-start(f32[3,8,16,1]{3,2,1,0:T(8,128)S(1)} %get-tuple-element.71), channel_id=1, source_target_pairs={{64,0},{128,64},{192,128},{256,192},{320,256},{384,320},{448,384},... | collective-permute-start | bytes 4616 | tf_op jit(solution)/shard_map/ppermute | solution.py:26
  90.1 6.0 %collective-permute-start.24 = (f32[3,8,16,1]{3,2,1,0:T(8,128)S(1)}, f32[3,8,16,1]{3,2,1,0:T(8,128)S(1)}, u32[]{:S(2)}, u32[]{:S(2)}) collective-permute-start(f32[3,8,16,1]{3,2,1,0:T(8,128)S(1)} %get-tuple-element.72), channel_id=1, source_target_pairs={{0,64},{64,128},{128,192},{192,256},{256,320},{320,384},{384,448},... | collective-permute-start | bytes 4616 | tf_op jit(solution)/shard_map/ppermute | solution.py:25
  96.1 1.9 %collective-permute-start.25 = (f32[3,8,16,1]{3,2,1,0:T(8,128)S(1)}, f32[3,8,16,1]{3,2,1,0:T(8,128)S(1)}, u32[]{:S(2)}, u32[]{:S(2)}) collective-permute-start(f32[3,8,16,1]{3,2,1,0:T(8,128)S(1)} %get-tuple-element.73), channel_id=1, source_target_pairs={{64,0},{128,64},{192,128},{256,192},{320,256},{384,320},{448,384},... | collective-permute-start | bytes 4616 | tf_op jit(solution)/shard_map/ppermute | solution.py:26
  98.3 1.9 %collective-permute-start.22 = (f32[3,8,1,130]{3,2,1,0:T(1,128)S(1)}, f32[3,8,1,130]{3,2,1,0:T(1,128)S(1)}, u32[]{:S(2)}, u32[]{:S(2)}) collective-permute-start(f32[3,8,1,130]{3,2,1,0:T(1,128)S(1)} %get-tuple-element.24), channel_id=1, source_target_pairs={{0,1},{1,2},{2,3},{3,4},{4,5},{5,6},{6,7},{7,8},{8,9},{9,10},{10,1... | collective-permute-start | bytes 37448 | tf_op jit(solution)/shard_map/ppermute | solution.py:25
  100.3 4.9 %collective-permute-start.23 = (f32[3,8,1,130]{3,2,1,0:T(1,128)S(1)}, f32[3,8,1,130]{3,2,1,0:T(1,128)S(1)}, u32[]{:S(2)}, u32[]{:S(2)}) collective-permute-start(f32[3,8,1,130]{3,2,1,0:T(1,128)S(1)} %get-tuple-element.25), channel_id=1, source_target_pairs={{1,0},{2,1},{3,2},{4,3},{5,4},{6,5},{7,6},{8,7},{9,8},{10,9},{11,1... | collective-permute-start | bytes 37448 | tf_op jit(solution)/shard_map/ppermute | solution.py:26
  105.1 0.7 collective-permute-done.25
  106.0 1.9 %collective-permute-start.26 = (f32[3,8,1,130]{3,2,1,0:T(1,128)S(1)}, f32[3,8,1,130]{3,2,1,0:T(1,128)S(1)}, u32[]{:S(2)}, u32[]{:S(2)}) collective-permute-start(f32[3,8,1,130]{3,2,1,0:T(1,128)S(1)} %get-tuple-element.26), channel_id=1, source_target_pairs={{0,1},{1,2},{2,3},{3,4},{4,5},{5,6},{6,7},{7,8},{8,9},{9,10},{10,1... | collective-permute-start | bytes 37448 | tf_op jit(solution)/shard_map/ppermute | solution.py:25
  108.0 4.9 %collective-permute-start.27 = (f32[3,8,1,130]{3,2,1,0:T(1,128)S(1)}, f32[3,8,1,130]{3,2,1,0:T(1,128)S(1)}, u32[]{:S(2)}, u32[]{:S(2)}) collective-permute-start(f32[3,8,1,130]{3,2,1,0:T(1,128)S(1)} %get-tuple-element.27), channel_id=1, source_target_pairs={{1,0},{2,1},{3,2},{4,3},{5,4},{6,5},{7,6},{8,7},{9,8},{10,9},{11,1... | collective-permute-start | bytes 37448 | tf_op jit(solution)/shard_map/ppermute | solution.py:26
  113.2 1.2 collective-permute-done.27
  114.9 0.3 fusion.24
  115.2 0.3 fusion.58
  115.8 5.3 %collective-permute-start.28 = (f32[3,8,16,1]{3,2,1,0:T(8,128)S(1)}, f32[3,8,16,1]{3,2,1,0:T(8,128)S(1)}, u32[]{:S(2)}, u32[]{:S(2)}) collective-permute-start(f32[3,8,16,1]{3,2,1,0:T(8,128)S(1)} %get-tuple-element.66), channel_id=1, source_target_pairs={{0,64},{64,128},{128,192},{192,256},{256,320},{320,384},{384,448},... | collective-permute-start | bytes 4616 | tf_op jit(solution)/shard_map/ppermute | solution.py:25
  121.2 1.9 %collective-permute-start.29 = (f32[3,8,16,1]{3,2,1,0:T(8,128)S(1)}, f32[3,8,16,1]{3,2,1,0:T(8,128)S(1)}, u32[]{:S(2)}, u32[]{:S(2)}) collective-permute-start(f32[3,8,16,1]{3,2,1,0:T(8,128)S(1)} %get-tuple-element.67), channel_id=1, source_target_pairs={{64,0},{128,64},{192,128},{256,192},{320,256},{384,320},{448,384},... | collective-permute-start | bytes 4616 | tf_op jit(solution)/shard_map/ppermute | solution.py:26
  123.2 6.0 %collective-permute-start.32 = (f32[3,8,16,1]{3,2,1,0:T(8,128)S(1)}, f32[3,8,16,1]{3,2,1,0:T(8,128)S(1)}, u32[]{:S(2)}, u32[]{:S(2)}) collective-permute-start(f32[3,8,16,1]{3,2,1,0:T(8,128)S(1)} %get-tuple-element.68), channel_id=1, source_target_pairs={{0,64},{64,128},{128,192},{192,256},{256,320},{320,384},{384,448},... | collective-permute-start | bytes 4616 | tf_op jit(solution)/shard_map/ppermute | solution.py:25
  129.2 1.9 %collective-permute-start.33 = (f32[3,8,16,1]{3,2,1,0:T(8,128)S(1)}, f32[3,8,16,1]{3,2,1,0:T(8,128)S(1)}, u32[]{:S(2)}, u32[]{:S(2)}) collective-permute-start(f32[3,8,16,1]{3,2,1,0:T(8,128)S(1)} %get-tuple-element.69), channel_id=1, source_target_pairs={{64,0},{128,64},{192,128},{256,192},{320,256},{384,320},{448,384},... | collective-permute-start | bytes 4616 | tf_op jit(solution)/shard_map/ppermute | solution.py:26
  131.4 1.9 %collective-permute-start.30 = (f32[3,8,1,130]{3,2,1,0:T(1,128)S(1)}, f32[3,8,1,130]{3,2,1,0:T(1,128)S(1)}, u32[]{:S(2)}, u32[]{:S(2)}) collective-permute-start(f32[3,8,1,130]{3,2,1,0:T(1,128)S(1)} %get-tuple-element.20), channel_id=1, source_target_pairs={{0,1},{1,2},{2,3},{3,4},{4,5},{5,6},{6,7},{7,8},{8,9},{9,10},{10,1... | collective-permute-start | bytes 37448 | tf_op jit(solution)/shard_map/ppermute | solution.py:25
  133.3 4.9 %collective-permute-start.31 = (f32[3,8,1,130]{3,2,1,0:T(1,128)S(1)}, f32[3,8,1,130]{3,2,1,0:T(1,128)S(1)}, u32[]{:S(2)}, u32[]{:S(2)}) collective-permute-start(f32[3,8,1,130]{3,2,1,0:T(1,128)S(1)} %get-tuple-element.21), channel_id=1, source_target_pairs={{1,0},{2,1},{3,2},{4,3},{5,4},{6,5},{7,6},{8,7},{9,8},{10,9},{11,1... | collective-permute-start | bytes 37448 | tf_op jit(solution)/shard_map/ppermute | solution.py:26
  138.2 0.7 collective-permute-done.33
  139.1 1.9 %collective-permute-start.34 = (f32[3,8,1,130]{3,2,1,0:T(1,128)S(1)}, f32[3,8,1,130]{3,2,1,0:T(1,128)S(1)}, u32[]{:S(2)}, u32[]{:S(2)}) collective-permute-start(f32[3,8,1,130]{3,2,1,0:T(1,128)S(1)} %get-tuple-element.22), channel_id=1, source_target_pairs={{0,1},{1,2},{2,3},{3,4},{4,5},{5,6},{6,7},{7,8},{8,9},{9,10},{10,1... | collective-permute-start | bytes 37448 | tf_op jit(solution)/shard_map/ppermute | solution.py:25
  141.1 5.0 %collective-permute-start.35 = (f32[3,8,1,130]{3,2,1,0:T(1,128)S(1)}, f32[3,8,1,130]{3,2,1,0:T(1,128)S(1)}, u32[]{:S(2)}, u32[]{:S(2)}) collective-permute-start(f32[3,8,1,130]{3,2,1,0:T(1,128)S(1)} %get-tuple-element.23), channel_id=1, source_target_pairs={{1,0},{2,1},{3,2},{4,3},{5,4},{6,5},{7,6},{8,7},{9,8},{10,9},{11,1... | collective-permute-start | bytes 37448 | tf_op jit(solution)/shard_map/ppermute | solution.py:26
  146.4 1.0 collective-permute-done.35
  148.0 0.3 fusion.21
  148.3 0.3 fusion.52
  148.7 0.8 multiply_reduce_fusion
  149.6 5.3 %collective-permute-start.36 = (f32[16,8]{1,0:T(8,128)S(1)}, f32[16,8]{1,0:T(8,128)S(1)}, u32[]{:S(2)}, u32[]{:S(2)}) collective-permute-start(f32[16,8]{1,0:T(8,128)S(1)} %get-tuple-element.90), channel_id=1, source_target_pairs={{0,64},{64,128},{128,192},{192,256},{256,320},{320,384},{384,448},... | collective-permute-start | bytes 1544 | tf_op jit(solution)/shard_map/ppermute | solution.py:25
  155.0 1.9 %collective-permute-start.37 = (f32[16,8]{1,0:T(8,128)S(1)}, f32[16,8]{1,0:T(8,128)S(1)}, u32[]{:S(2)}, u32[]{:S(2)}) collective-permute-start(f32[16,8]{1,0:T(8,128)S(1)} %get-tuple-element.91), channel_id=1, source_target_pairs={{64,0},{128,64},{192,128},{256,192},{320,256},{384,320},{448,384},... | collective-permute-start | bytes 1544 | tf_op jit(solution)/shard_map/ppermute | solution.py:26
  156.9 5.7 %collective-permute-done.37 = f32[16,8]{1,0:T(8,128)S(1)} collective-permute-done((f32[16,8]{1,0:T(8,128)S(1)}, f32[16,8]{1,0:T(8,128)S(1)}, u32[]{:S(2)}, u32[]{:S(2)}) %collective-permute-start.37) | collective-permute-done | bytes 544 | tf_op jit(solution)/shard_map/ppermute | solution.py:26
  162.7 3.4 %collective-permute-start.39 = (f32[8,144]{1,0:T(8,128)S(1)}, f32[8,144]{1,0:T(8,128)S(1)}, u32[]{:S(2)}, u32[]{:S(2)}) collective-permute-start(f32[8,144]{1,0:T(8,128)S(1)} %get-tuple-element.86), channel_id=1, source_target_pairs={{1,0},{2,1},{3,2},{4,3},{5,4},{6,5},{7,6},{8,7},{9,8},{10,9},{11,1... | collective-permute-start | bytes 13832 | tf_op jit(solution)/shard_map/ppermute | solution.py:26
  166.1 1.9 %collective-permute-start.38 = (f32[8,144]{1,0:T(8,128)S(1)}, f32[8,144]{1,0:T(8,128)S(1)}, u32[]{:S(2)}, u32[]{:S(2)}) collective-permute-start(f32[8,144]{1,0:T(8,128)S(1)} %get-tuple-element.87), channel_id=1, source_target_pairs={{0,1},{1,2},{2,3},{3,4},{4,5},{5,6},{6,7},{7,8},{8,9},{9,10},{10,1... | collective-permute-start | bytes 13832 | tf_op jit(solution)/shard_map/ppermute | solution.py:25
  168.0 4.2 %collective-permute-done.38 = f32[8,144]{1,0:T(8,128)S(1)} collective-permute-done((f32[8,144]{1,0:T(8,128)S(1)}, f32[8,144]{1,0:T(8,128)S(1)}, u32[]{:S(2)}, u32[]{:S(2)}) %collective-permute-start.38) | collective-permute-done | bytes 4640 | tf_op jit(solution)/shard_map/ppermute | solution.py:25
  172.7 2.1 %fusion.6 = f32[16,128]{1,0:T(8,128)} fusion(f32[17,16,144]{2,1,0:T(8,128)S(1)} %constant_dynamic-update-slice_fusion.17, f32[144,128]{1,0:T(8,128)S(1)} %convert_multiply_fusion, f32[17]{0:T(128)S(1)} %add_multiply_fusion.1, pred[144,128]{1,0:T(8,128)(4,1)S(1)} %abs_compare_fusion), kind=kOutput, calls=%fused_computation.15 | convolution fusion | flops 61417472 | bytes 257092 | tf_op jit(solution)/shard_map/krc,kcx->rx/dot_general | solution.py:49
  (136 shorter events, 7.6 us)
Async XLA Ops:
  0.6 25.1 %copy-start.4 = (f32[16,128]{1,0:T(8,128)S(1)}, f32[16,128]{1,0:T(8,128)}, u32[]{:S(2)}) copy-start(f32[16,128]{1,0:T(8,128)} %param.10) | copy-start | bytes 24580
  0.6 29.5 %copy-start.1 = (f32[3,8,16,128]{3,2,1,0:T(8,128)S(1)}, f32[3,8,16,128]{3,2,1,0:T(8,128)}, u32[]{:S(2)}) copy-start(f32[3,8,16,128]{3,2,1,0:T(8,128)} %param.16) | copy-start | bytes 589828
  0.7 36.7 %copy-start = (f32[3,8,16,128]{3,2,1,0:T(8,128)S(1)}, f32[3,8,16,128]{3,2,1,0:T(8,128)}, u32[]{:S(2)}) copy-start(f32[3,8,16,128]{3,2,1,0:T(8,128)} %param.17) | copy-start | bytes 589828
  0.7 22.7 %copy-start.7 = (f32[4]{0:T(128)S(1)}, f32[4]{0:T(128)}, u32[]{:S(2)}) copy-start(f32[4]{0:T(128)} %param.13) | copy-start | bytes 52
  0.7 22.7 %copy-start.6 = (s32[8,16]{1,0:T(8,128)S(1)}, s32[8,16]{1,0:T(8,128)}, u32[]{:S(2)}) copy-start(s32[8,16]{1,0:T(8,128)} %param.12) | copy-start | bytes 1540
  0.7 22.7 %copy-start.8 = (s32[8,16]{1,0:T(8,128)S(1)}, s32[8,16]{1,0:T(8,128)}, u32[]{:S(2)}) copy-start(s32[8,16]{1,0:T(8,128)} %param.11) | copy-start | bytes 1540
  1.6 22.2 %collective-permute-start.8 = (f32[16,8]{1,0:T(8,128)S(1)}, f32[16,8]{1,0:T(8,128)S(1)}, u32[]{:S(2)}, u32[]{:S(2)}) collective-permute-start(f32[16,8]{1,0:T(8,128)S(1)} %get-tuple-element.92), channel_id=1, source_target_pairs={{0,64},{64,128},{128,192},{192,256},{256,320},{320,384},{384,448},... | collective-permute-start | bytes 1544 | tf_op jit(solution)/shard_map/ppermute | solution.py:25
  5.0 20.7 %collective-permute-start.9 = (f32[16,8]{1,0:T(8,128)S(1)}, f32[16,8]{1,0:T(8,128)S(1)}, u32[]{:S(2)}, u32[]{:S(2)}) collective-permute-start(f32[16,8]{1,0:T(8,128)S(1)} %get-tuple-element.93), channel_id=1, source_target_pairs={{64,0},{128,64},{192,128},{256,192},{320,256},{384,320},{448,384},... | collective-permute-start | bytes 1544 | tf_op jit(solution)/shard_map/ppermute | solution.py:26
  8.6 19.4 %collective-permute-start = (f32[3,8,16,1]{3,2,1,0:T(8,128)S(1)}, f32[3,8,16,1]{3,2,1,0:T(8,128)S(1)}, u32[]{:S(2)}, u32[]{:S(2)}) collective-permute-start(f32[3,8,16,1]{3,2,1,0:T(8,128)S(1)} %get-tuple-element.78), channel_id=1, source_target_pairs={{0,64},{64,128},{128,192},{192,256},{256,320},{320,384},{384,448},... | collective-permute-start | bytes 4616 | tf_op jit(solution)/shard_map/ppermute | solution.py:25
  14.1 16.0 %collective-permute-start.1 = (f32[3,8,16,1]{3,2,1,0:T(8,128)S(1)}, f32[3,8,16,1]{3,2,1,0:T(8,128)S(1)}, u32[]{:S(2)}, u32[]{:S(2)}) collective-permute-start(f32[3,8,16,1]{3,2,1,0:T(8,128)S(1)} %get-tuple-element.79), channel_id=1, source_target_pairs={{64,0},{128,64},{192,128},{256,192},{320,256},{384,320},{448,384},... | collective-permute-start | bytes 4616 | tf_op jit(solution)/shard_map/ppermute | solution.py:26
  17.2 15.8 %collective-permute-start.4 = (f32[3,8,16,1]{3,2,1,0:T(8,128)S(1)}, f32[3,8,16,1]{3,2,1,0:T(8,128)S(1)}, u32[]{:S(2)}, u32[]{:S(2)}) collective-permute-start(f32[3,8,16,1]{3,2,1,0:T(8,128)S(1)} %get-tuple-element.80), channel_id=1, source_target_pairs={{0,64},{64,128},{128,192},{192,256},{256,320},{320,384},{384,448},... | collective-permute-start | bytes 4616 | tf_op jit(solution)/shard_map/ppermute | solution.py:25
  23.8 13.6 %collective-permute-start.5 = (f32[3,8,16,1]{3,2,1,0:T(8,128)S(1)}, f32[3,8,16,1]{3,2,1,0:T(8,128)S(1)}, u32[]{:S(2)}, u32[]{:S(2)}) collective-permute-start(f32[3,8,16,1]{3,2,1,0:T(8,128)S(1)} %get-tuple-element.81), channel_id=1, source_target_pairs={{64,0},{128,64},{192,128},{256,192},{320,256},{384,320},{448,384},... | collective-permute-start | bytes 4616 | tf_op jit(solution)/shard_map/ppermute | solution.py:26
  25.8 13.7 %collective-permute-start.11 = (f32[8,144]{1,0:T(8,128)S(1)}, f32[8,144]{1,0:T(8,128)S(1)}, u32[]{:S(2)}, u32[]{:S(2)}) collective-permute-start(f32[8,144]{1,0:T(8,128)S(1)} %get-tuple-element.88), channel_id=1, source_target_pairs={{1,0},{2,1},{3,2},{4,3},{5,4},{6,5},{7,6},{8,7},{9,8},{10,9},{11,1... | collective-permute-start | bytes 13832 | tf_op jit(solution)/shard_map/ppermute | solution.py:26
  28.0 16.4 %collective-permute-start.10 = (f32[8,144]{1,0:T(8,128)S(1)}, f32[8,144]{1,0:T(8,128)S(1)}, u32[]{:S(2)}, u32[]{:S(2)}) collective-permute-start(f32[8,144]{1,0:T(8,128)S(1)} %get-tuple-element.89), channel_id=1, source_target_pairs={{0,1},{1,2},{2,3},{3,4},{4,5},{5,6},{6,7},{7,8},{8,9},{9,10},{10,1... | collective-permute-start | bytes 13832 | tf_op jit(solution)/shard_map/ppermute | solution.py:25
  30.4 15.9 %collective-permute-start.2 = (f32[3,8,1,130]{3,2,1,0:T(1,128)S(1)}, f32[3,8,1,130]{3,2,1,0:T(1,128)S(1)}, u32[]{:S(2)}, u32[]{:S(2)}) collective-permute-start(f32[3,8,1,130]{3,2,1,0:T(1,128)S(1)} %get-tuple-element.32), channel_id=1, source_target_pairs={{0,1},{1,2},{2,3},{3,4},{4,5},{5,6},{6,7},{7,8},{8,9},{9,10},{10,1... | collective-permute-start | bytes 37448 | tf_op jit(solution)/shard_map/ppermute | solution.py:25
  32.9 13.3 %copy-start.5 = (f32[8,16,128]{2,1,0:T(8,128)S(1)}, f32[8,16,128]{2,1,0:T(8,128)}, u32[]{:S(2)}) copy-start(f32[8,16,128]{2,1,0:T(8,128)} %param.9) | copy-start | bytes 196612
  33.0 13.3 %collective-permute-start.3 = (f32[3,8,1,130]{3,2,1,0:T(1,128)S(1)}, f32[3,8,1,130]{3,2,1,0:T(1,128)S(1)}, u32[]{:S(2)}, u32[]{:S(2)}) collective-permute-start(f32[3,8,1,130]{3,2,1,0:T(1,128)S(1)} %get-tuple-element.33), channel_id=1, source_target_pairs={{1,0},{2,1},{3,2},{4,3},{5,4},{6,5},{7,6},{8,7},{9,8},{10,9},{11,1... | collective-permute-start | bytes 37448 | tf_op jit(solution)/shard_map/ppermute | solution.py:26
  37.6 9.0 %collective-permute-start.6 = (f32[3,8,1,130]{3,2,1,0:T(1,128)S(1)}, f32[3,8,1,130]{3,2,1,0:T(1,128)S(1)}, u32[]{:S(2)}, u32[]{:S(2)}) collective-permute-start(f32[3,8,1,130]{3,2,1,0:T(1,128)S(1)} %get-tuple-element.34), channel_id=1, source_target_pairs={{0,1},{1,2},{2,3},{3,4},{4,5},{5,6},{6,7},{7,8},{8,9},{9,10},{10,1... | collective-permute-start | bytes 37448 | tf_op jit(solution)/shard_map/ppermute | solution.py:25
  39.5 7.1 %collective-permute-start.7 = (f32[3,8,1,130]{3,2,1,0:T(1,128)S(1)}, f32[3,8,1,130]{3,2,1,0:T(1,128)S(1)}, u32[]{:S(2)}, u32[]{:S(2)}) collective-permute-start(f32[3,8,1,130]{3,2,1,0:T(1,128)S(1)} %get-tuple-element.35), channel_id=1, source_target_pairs={{1,0},{2,1},{3,2},{4,3},{5,4},{6,5},{7,6},{8,7},{9,8},{10,9},{11,1... | collective-permute-start | bytes 37448 | tf_op jit(solution)/shard_map/ppermute | solution.py:26
  47.5 0.9 copy-start.2
  47.6 1.0 copy-start.3
  48.8 16.1 %collective-permute-start.12 = (f32[3,8,16,1]{3,2,1,0:T(8,128)S(1)}, f32[3,8,16,1]{3,2,1,0:T(8,128)S(1)}, u32[]{:S(2)}, u32[]{:S(2)}) collective-permute-start(f32[3,8,16,1]{3,2,1,0:T(8,128)S(1)} %get-tuple-element.74), channel_id=1, source_target_pairs={{0,64},{64,128},{128,192},{192,256},{256,320},{320,384},{384,448},... | collective-permute-start | bytes 4616 | tf_op jit(solution)/shard_map/ppermute | solution.py:25
  54.9 10.0 %collective-permute-start.13 = (f32[3,8,16,1]{3,2,1,0:T(8,128)S(1)}, f32[3,8,16,1]{3,2,1,0:T(8,128)S(1)}, u32[]{:S(2)}, u32[]{:S(2)}) collective-permute-start(f32[3,8,16,1]{3,2,1,0:T(8,128)S(1)} %get-tuple-element.75), channel_id=1, source_target_pairs={{64,0},{128,64},{192,128},{256,192},{320,256},{384,320},{448,384},... | collective-permute-start | bytes 4616 | tf_op jit(solution)/shard_map/ppermute | solution.py:26
  56.9 15.0 %collective-permute-start.16 = (f32[3,8,16,1]{3,2,1,0:T(8,128)S(1)}, f32[3,8,16,1]{3,2,1,0:T(8,128)S(1)}, u32[]{:S(2)}, u32[]{:S(2)}) collective-permute-start(f32[3,8,16,1]{3,2,1,0:T(8,128)S(1)} %get-tuple-element.76), channel_id=1, source_target_pairs={{0,64},{64,128},{128,192},{192,256},{256,320},{320,384},{384,448},... | collective-permute-start | bytes 4616 | tf_op jit(solution)/shard_map/ppermute | solution.py:25
  63.0 9.7 %collective-permute-start.17 = (f32[3,8,16,1]{3,2,1,0:T(8,128)S(1)}, f32[3,8,16,1]{3,2,1,0:T(8,128)S(1)}, u32[]{:S(2)}, u32[]{:S(2)}) collective-permute-start(f32[3,8,16,1]{3,2,1,0:T(8,128)S(1)} %get-tuple-element.77), channel_id=1, source_target_pairs={{64,0},{128,64},{192,128},{256,192},{320,256},{384,320},{448,384},... | collective-permute-start | bytes 4616 | tf_op jit(solution)/shard_map/ppermute | solution.py:26
  65.1 14.5 %collective-permute-start.14 = (f32[3,8,1,130]{3,2,1,0:T(1,128)S(1)}, f32[3,8,1,130]{3,2,1,0:T(1,128)S(1)}, u32[]{:S(2)}, u32[]{:S(2)}) collective-permute-start(f32[3,8,1,130]{3,2,1,0:T(1,128)S(1)} %get-tuple-element.28), channel_id=1, source_target_pairs={{0,1},{1,2},{2,3},{3,4},{4,5},{5,6},{6,7},{7,8},{8,9},{9,10},{10,1... | collective-permute-start | bytes 37448 | tf_op jit(solution)/shard_map/ppermute | solution.py:25
  67.1 12.6 %collective-permute-start.15 = (f32[3,8,1,130]{3,2,1,0:T(1,128)S(1)}, f32[3,8,1,130]{3,2,1,0:T(1,128)S(1)}, u32[]{:S(2)}, u32[]{:S(2)}) collective-permute-start(f32[3,8,1,130]{3,2,1,0:T(1,128)S(1)} %get-tuple-element.29), channel_id=1, source_target_pairs={{1,0},{2,1},{3,2},{4,3},{5,4},{6,5},{7,6},{8,7},{9,8},{10,9},{11,1... | collective-permute-start | bytes 37448 | tf_op jit(solution)/shard_map/ppermute | solution.py:26
  72.9 7.1 %collective-permute-start.18 = (f32[3,8,1,130]{3,2,1,0:T(1,128)S(1)}, f32[3,8,1,130]{3,2,1,0:T(1,128)S(1)}, u32[]{:S(2)}, u32[]{:S(2)}) collective-permute-start(f32[3,8,1,130]{3,2,1,0:T(1,128)S(1)} %get-tuple-element.30), channel_id=1, source_target_pairs={{0,1},{1,2},{2,3},{3,4},{4,5},{5,6},{6,7},{7,8},{8,9},{9,10},{10,1... | collective-permute-start | bytes 37448 | tf_op jit(solution)/shard_map/ppermute | solution.py:25
  74.8 6.4 %collective-permute-start.19 = (f32[3,8,1,130]{3,2,1,0:T(1,128)S(1)}, f32[3,8,1,130]{3,2,1,0:T(1,128)S(1)}, u32[]{:S(2)}, u32[]{:S(2)}) collective-permute-start(f32[3,8,1,130]{3,2,1,0:T(1,128)S(1)} %get-tuple-element.31), channel_id=1, source_target_pairs={{1,0},{2,1},{3,2},{4,3},{5,4},{6,5},{7,6},{8,7},{9,8},{10,9},{11,1... | collective-permute-start | bytes 37448 | tf_op jit(solution)/shard_map/ppermute | solution.py:26
  82.7 15.4 %collective-permute-start.20 = (f32[3,8,16,1]{3,2,1,0:T(8,128)S(1)}, f32[3,8,16,1]{3,2,1,0:T(8,128)S(1)}, u32[]{:S(2)}, u32[]{:S(2)}) collective-permute-start(f32[3,8,16,1]{3,2,1,0:T(8,128)S(1)} %get-tuple-element.70), channel_id=1, source_target_pairs={{0,64},{64,128},{128,192},{192,256},{256,320},{320,384},{384,448},... | collective-permute-start | bytes 4616 | tf_op jit(solution)/shard_map/ppermute | solution.py:25
  88.1 10.0 %collective-permute-start.21 = (f32[3,8,16,1]{3,2,1,0:T(8,128)S(1)}, f32[3,8,16,1]{3,2,1,0:T(8,128)S(1)}, u32[]{:S(2)}, u32[]{:S(2)}) collective-permute-start(f32[3,8,16,1]{3,2,1,0:T(8,128)S(1)} %get-tuple-element.71), channel_id=1, source_target_pairs={{64,0},{128,64},{192,128},{256,192},{320,256},{384,320},{448,384},... | collective-permute-start | bytes 4616 | tf_op jit(solution)/shard_map/ppermute | solution.py:26
  90.1 15.0 %collective-permute-start.24 = (f32[3,8,16,1]{3,2,1,0:T(8,128)S(1)}, f32[3,8,16,1]{3,2,1,0:T(8,128)S(1)}, u32[]{:S(2)}, u32[]{:S(2)}) collective-permute-start(f32[3,8,16,1]{3,2,1,0:T(8,128)S(1)} %get-tuple-element.72), channel_id=1, source_target_pairs={{0,64},{64,128},{128,192},{192,256},{256,320},{320,384},{384,448},... | collective-permute-start | bytes 4616 | tf_op jit(solution)/shard_map/ppermute | solution.py:25
  96.1 9.7 %collective-permute-start.25 = (f32[3,8,16,1]{3,2,1,0:T(8,128)S(1)}, f32[3,8,16,1]{3,2,1,0:T(8,128)S(1)}, u32[]{:S(2)}, u32[]{:S(2)}) collective-permute-start(f32[3,8,16,1]{3,2,1,0:T(8,128)S(1)} %get-tuple-element.73), channel_id=1, source_target_pairs={{64,0},{128,64},{192,128},{256,192},{320,256},{384,320},{448,384},... | collective-permute-start | bytes 4616 | tf_op jit(solution)/shard_map/ppermute | solution.py:26
  98.3 14.5 %collective-permute-start.22 = (f32[3,8,1,130]{3,2,1,0:T(1,128)S(1)}, f32[3,8,1,130]{3,2,1,0:T(1,128)S(1)}, u32[]{:S(2)}, u32[]{:S(2)}) collective-permute-start(f32[3,8,1,130]{3,2,1,0:T(1,128)S(1)} %get-tuple-element.24), channel_id=1, source_target_pairs={{0,1},{1,2},{2,3},{3,4},{4,5},{5,6},{6,7},{7,8},{8,9},{9,10},{10,1... | collective-permute-start | bytes 37448 | tf_op jit(solution)/shard_map/ppermute | solution.py:25
  100.3 12.6 %collective-permute-start.23 = (f32[3,8,1,130]{3,2,1,0:T(1,128)S(1)}, f32[3,8,1,130]{3,2,1,0:T(1,128)S(1)}, u32[]{:S(2)}, u32[]{:S(2)}) collective-permute-start(f32[3,8,1,130]{3,2,1,0:T(1,128)S(1)} %get-tuple-element.25), channel_id=1, source_target_pairs={{1,0},{2,1},{3,2},{4,3},{5,4},{6,5},{7,6},{8,7},{9,8},{10,9},{11,1... | collective-permute-start | bytes 37448 | tf_op jit(solution)/shard_map/ppermute | solution.py:26
  106.0 7.1 %collective-permute-start.26 = (f32[3,8,1,130]{3,2,1,0:T(1,128)S(1)}, f32[3,8,1,130]{3,2,1,0:T(1,128)S(1)}, u32[]{:S(2)}, u32[]{:S(2)}) collective-permute-start(f32[3,8,1,130]{3,2,1,0:T(1,128)S(1)} %get-tuple-element.26), channel_id=1, source_target_pairs={{0,1},{1,2},{2,3},{3,4},{4,5},{5,6},{6,7},{7,8},{8,9},{9,10},{10,1... | collective-permute-start | bytes 37448 | tf_op jit(solution)/shard_map/ppermute | solution.py:25
  108.0 6.4 %collective-permute-start.27 = (f32[3,8,1,130]{3,2,1,0:T(1,128)S(1)}, f32[3,8,1,130]{3,2,1,0:T(1,128)S(1)}, u32[]{:S(2)}, u32[]{:S(2)}) collective-permute-start(f32[3,8,1,130]{3,2,1,0:T(1,128)S(1)} %get-tuple-element.27), channel_id=1, source_target_pairs={{1,0},{2,1},{3,2},{4,3},{5,4},{6,5},{7,6},{8,7},{9,8},{10,9},{11,1... | collective-permute-start | bytes 37448 | tf_op jit(solution)/shard_map/ppermute | solution.py:26
  115.8 15.4 %collective-permute-start.28 = (f32[3,8,16,1]{3,2,1,0:T(8,128)S(1)}, f32[3,8,16,1]{3,2,1,0:T(8,128)S(1)}, u32[]{:S(2)}, u32[]{:S(2)}) collective-permute-start(f32[3,8,16,1]{3,2,1,0:T(8,128)S(1)} %get-tuple-element.66), channel_id=1, source_target_pairs={{0,64},{64,128},{128,192},{192,256},{256,320},{320,384},{384,448},... | collective-permute-start | bytes 4616 | tf_op jit(solution)/shard_map/ppermute | solution.py:25
  121.2 10.0 %collective-permute-start.29 = (f32[3,8,16,1]{3,2,1,0:T(8,128)S(1)}, f32[3,8,16,1]{3,2,1,0:T(8,128)S(1)}, u32[]{:S(2)}, u32[]{:S(2)}) collective-permute-start(f32[3,8,16,1]{3,2,1,0:T(8,128)S(1)} %get-tuple-element.67), channel_id=1, source_target_pairs={{64,0},{128,64},{192,128},{256,192},{320,256},{384,320},{448,384},... | collective-permute-start | bytes 4616 | tf_op jit(solution)/shard_map/ppermute | solution.py:26
  123.2 15.0 %collective-permute-start.32 = (f32[3,8,16,1]{3,2,1,0:T(8,128)S(1)}, f32[3,8,16,1]{3,2,1,0:T(8,128)S(1)}, u32[]{:S(2)}, u32[]{:S(2)}) collective-permute-start(f32[3,8,16,1]{3,2,1,0:T(8,128)S(1)} %get-tuple-element.68), channel_id=1, source_target_pairs={{0,64},{64,128},{128,192},{192,256},{256,320},{320,384},{384,448},... | collective-permute-start | bytes 4616 | tf_op jit(solution)/shard_map/ppermute | solution.py:25
  129.2 9.7 %collective-permute-start.33 = (f32[3,8,16,1]{3,2,1,0:T(8,128)S(1)}, f32[3,8,16,1]{3,2,1,0:T(8,128)S(1)}, u32[]{:S(2)}, u32[]{:S(2)}) collective-permute-start(f32[3,8,16,1]{3,2,1,0:T(8,128)S(1)} %get-tuple-element.69), channel_id=1, source_target_pairs={{64,0},{128,64},{192,128},{256,192},{320,256},{384,320},{448,384},... | collective-permute-start | bytes 4616 | tf_op jit(solution)/shard_map/ppermute | solution.py:26
  131.4 14.7 %collective-permute-start.30 = (f32[3,8,1,130]{3,2,1,0:T(1,128)S(1)}, f32[3,8,1,130]{3,2,1,0:T(1,128)S(1)}, u32[]{:S(2)}, u32[]{:S(2)}) collective-permute-start(f32[3,8,1,130]{3,2,1,0:T(1,128)S(1)} %get-tuple-element.20), channel_id=1, source_target_pairs={{0,1},{1,2},{2,3},{3,4},{4,5},{5,6},{6,7},{7,8},{8,9},{9,10},{10,1... | collective-permute-start | bytes 37448 | tf_op jit(solution)/shard_map/ppermute | solution.py:25
  133.3 12.8 %collective-permute-start.31 = (f32[3,8,1,130]{3,2,1,0:T(1,128)S(1)}, f32[3,8,1,130]{3,2,1,0:T(1,128)S(1)}, u32[]{:S(2)}, u32[]{:S(2)}) collective-permute-start(f32[3,8,1,130]{3,2,1,0:T(1,128)S(1)} %get-tuple-element.21), channel_id=1, source_target_pairs={{1,0},{2,1},{3,2},{4,3},{5,4},{6,5},{7,6},{8,7},{9,8},{10,9},{11,1... | collective-permute-start | bytes 37448 | tf_op jit(solution)/shard_map/ppermute | solution.py:26
  139.1 7.3 %collective-permute-start.34 = (f32[3,8,1,130]{3,2,1,0:T(1,128)S(1)}, f32[3,8,1,130]{3,2,1,0:T(1,128)S(1)}, u32[]{:S(2)}, u32[]{:S(2)}) collective-permute-start(f32[3,8,1,130]{3,2,1,0:T(1,128)S(1)} %get-tuple-element.22), channel_id=1, source_target_pairs={{0,1},{1,2},{2,3},{3,4},{4,5},{5,6},{6,7},{7,8},{8,9},{9,10},{10,1... | collective-permute-start | bytes 37448 | tf_op jit(solution)/shard_map/ppermute | solution.py:25
  141.1 6.4 %collective-permute-start.35 = (f32[3,8,1,130]{3,2,1,0:T(1,128)S(1)}, f32[3,8,1,130]{3,2,1,0:T(1,128)S(1)}, u32[]{:S(2)}, u32[]{:S(2)}) collective-permute-start(f32[3,8,1,130]{3,2,1,0:T(1,128)S(1)} %get-tuple-element.23), channel_id=1, source_target_pairs={{1,0},{2,1},{3,2},{4,3},{5,4},{6,5},{7,6},{8,7},{9,8},{10,9},{11,1... | collective-permute-start | bytes 37448 | tf_op jit(solution)/shard_map/ppermute | solution.py:26
  149.6 7.3 %collective-permute-start.36 = (f32[16,8]{1,0:T(8,128)S(1)}, f32[16,8]{1,0:T(8,128)S(1)}, u32[]{:S(2)}, u32[]{:S(2)}) collective-permute-start(f32[16,8]{1,0:T(8,128)S(1)} %get-tuple-element.90), channel_id=1, source_target_pairs={{0,64},{64,128},{128,192},{192,256},{256,320},{320,384},{384,448},... | collective-permute-start | bytes 1544 | tf_op jit(solution)/shard_map/ppermute | solution.py:25
  155.0 7.7 %collective-permute-start.37 = (f32[16,8]{1,0:T(8,128)S(1)}, f32[16,8]{1,0:T(8,128)S(1)}, u32[]{:S(2)}, u32[]{:S(2)}) collective-permute-start(f32[16,8]{1,0:T(8,128)S(1)} %get-tuple-element.91), channel_id=1, source_target_pairs={{64,0},{128,64},{192,128},{256,192},{320,256},{384,320},{448,384},... | collective-permute-start | bytes 1544 | tf_op jit(solution)/shard_map/ppermute | solution.py:26
  162.7 5.4 %collective-permute-start.39 = (f32[8,144]{1,0:T(8,128)S(1)}, f32[8,144]{1,0:T(8,128)S(1)}, u32[]{:S(2)}, u32[]{:S(2)}) collective-permute-start(f32[8,144]{1,0:T(8,128)S(1)} %get-tuple-element.86), channel_id=1, source_target_pairs={{1,0},{2,1},{3,2},{4,3},{5,4},{6,5},{7,6},{8,7},{9,8},{10,9},{11,1... | collective-permute-start | bytes 13832 | tf_op jit(solution)/shard_map/ppermute | solution.py:26
  166.1 6.2 %collective-permute-start.38 = (f32[8,144]{1,0:T(8,128)S(1)}, f32[8,144]{1,0:T(8,128)S(1)}, u32[]{:S(2)}, u32[]{:S(2)}) collective-permute-start(f32[8,144]{1,0:T(8,128)S(1)} %get-tuple-element.87), channel_id=1, source_target_pairs={{0,1},{1,2},{2,3},{3,4},{4,5},{5,6},{6,7},{7,8},{8,9},{9,10},{10,1... | collective-permute-start | bytes 13832 | tf_op jit(solution)/shard_map/ppermute | solution.py:25
where the time goes:
time: 176 us; the launch traced here: 175 us
  starting transfers between devices  139 us (79%)
  waiting for transfers between devices  15.4 us (9%)
  other arithmetic  9.12 us (5%)
  local copies, waits for them, and re-layouts  5.43 us (3%)
  matrix products  3.92 us (2%)
  between operations  1.9 us (1%)
    ppermute x20, starting transfers between devices, padded_2(): before = lax.ppermute(last, axis, up)  75.2 us
    ppermute x20, starting transfers between devices, padded_2(): after = lax.ppermute(initial, axis, down)  63.8 us
    ppermute x20, waiting for transfers between devices, padded_2(): after = lax.ppermute(initial, axis, down)  11.1 us
    ppermute x20, waiting for transfers between devices, padded_2(): before = lax.ppermute(last, axis, up)  4.29 us
    slice x10, local copies, waits for them, and re-layouts, padded_2(): last = lax.slice_in_dim(value, length - width, length, axis=dim)  3.9 us
    dot_general x2, matrix products, cone_filter(): jnp.einsum('krc,kcx->rx', slabs, table, precision=lax.Precision.HIGHEST)  3.61 us
  transfers between devices with their start and end apart: 40, of which 8 were waited for; matrix products, arithmetic and copies ran while one was open for 5% of the time, Pallas kernels for 0%

commit v1 on v0

v1 whole, which is shorter than its diff:
```python
import functools
import math

import jax
import jax.numpy as jnp
from jax import lax
from jax.experimental import pallas as pl
from jax.experimental.pallas import tpu as pltpu
from jax.sharding import PartitionSpec as P

ITERS = 4
RADIUS = 8
TILE = 128
Z = 8
ROWS = 16
LANES = 128
HALO = 4
WRAP = ROWS + 8
GROUPS = 13
WIDTH = 16
SMEM = pltpu.SMEM
VMEM = pltpu.VMEM
LIMIT = 48 * 1024 * 1024


def cone_weight(row_shift, col_shift):
    return max(0.0, RADIUS + 1 - math.sqrt(row_shift * row_shift + col_shift * col_shift))


def cone_total():
    span = range(-RADIUS, RADIUS + 1)
    return math.fsum(cone_weight(a, b) for a in span for b in span)


def lanes_of(rows):
    return lax.broadcasted_iota(jnp.int32, (rows, LANES), 1)


def rows_of(rows):
    return lax.broadcasted_iota(jnp.int32, (rows, LANES), 0)


def turn(value, shift, axis):
    size = value.shape[axis]
    return pltpu.roll(value, shift % size, axis)


def cone(rows_at, rows):
    total = cone_total()
    paired = [rows_at(0)]
    for a in range(1, RADIUS + 1):
        paired.append(rows_at(a) + rows_at(-a))
    result = None
    for b in range(RADIUS + 1):
        column = None
        for a in range(RADIUS + 1):
            weight = cone_weight(a, b)
            if weight > 0.0:
                term = paired[a] * (weight / total)
                column = term if column is None else column + term
        if b > 0:
            column = turn(column, b, 1) + turn(column, -b, 1)
        result = column if result is None else result + column
    return result


def pack_kernel(field, adjoint, source, adjoint_source, background, density, right, left, up, down):
    lane = lanes_of(ROWS)
    low = rows_of(8) < 4
    for g in range(GROUPS):
        planes = background if g == 12 else (field, adjoint, source, adjoint_source)[g // 3].at[g % 3]
        to_right = to_left = None
        for z in range(Z):
            plane = planes[z]
            here_right = turn(plane, 16 * z + 12, 1)
            here_left = turn(plane, 16 * z + 4, 1)
            if z == 0:
                to_right, to_left = here_right, here_left
            else:
                chosen = lane >= 16 * z
                to_right = jnp.where(chosen, here_right, to_right)
                to_left = jnp.where(chosen, here_left, to_left)
        right[g] = to_right
        left[g] = to_left
        for pair in range(Z // 2):
            k = g * (Z // 2) + pair
            down[k] = jnp.where(low, planes[2 * pair, 0:8], turn(planes[2 * pair + 1, 0:8], 4, 0))
            up[k] = jnp.where(low, turn(planes[2 * pair + 1, 8:16], 4, 0), planes[2 * pair, 8:16])
    right[GROUPS] = density[...]
    left[GROUPS] = density[...]
    for part in range(2):
        up[4 * GROUPS + part] = density[8 * part : 8 * part + 8]
        down[4 * GROUPS + part] = density[8 * part : 8 * part + 8]


def strip_kernel(own_right, own_left, from_left, from_right, strips, side, up, down):
    col = lax.axis_index("gx")
    first, last = col == 0, col == lax.axis_size("gx") - 1
    lane = lanes_of(ROWS)
    within = lane % 16
    half = lane % 32 < 16
    low = rows_of(8) < 4
    for g in range(GROUPS):
        here_right = jnp.where(within >= HALO, jnp.where(last, 0.0, from_right[g]), own_left[g])
        here_left = jnp.where(within < 12, jnp.where(first, 0.0, from_left[g]), own_right[g])
        even = jnp.where(half, here_right, turn(here_left, 16, 1))
        odd = jnp.where(half, turn(here_right, -16, 1), here_left)
        strips[g, 0] = even
        strips[g, 1] = odd
        down[g] = jnp.where(low, even[0:8], turn(odd[0:8], 4, 0))
        up[g] = jnp.where(low, turn(odd[8:16], 4, 0), even[8:16])
    beside = jnp.where(
        lane < 64, jnp.where(last, 0.0, from_right[GROUPS]), jnp.where(first, 0.0, from_left[GROUPS])
    )
    side[...] = beside
    for part in range(2):
        up[GROUPS + part] = beside[8 * part : 8 * part + 8]
        down[GROUPS + part] = beside[8 * part : 8 * part + 8]


def unpack(above, below, low, odd):
    if odd:
        return turn(jnp.where(low, below, above), 4, 0)
    return jnp.where(low, above, below)


def main_kernel(
    design, material, contrast, field, adjoint, source, adjoint_source, background, density,
    above, below, strips, side, strip_above, strip_below,
    field_out, adjoint_out, local_up, local_down,
    fields, drive, rate, keep, strip_fields, strip_drive, strip_rate, strip_keep, wide,
):
    col, row = lax.axis_index("gx"), lax.axis_index("gy")
    cols, rows = lax.axis_size("gx"), lax.axis_size("gy")
    first_row, last_row = row == 0, row == rows - 1
    low = rows_of(8) < 4
    lane8, lane24, row24 = lanes_of(8), lanes_of(WRAP), rows_of(WRAP)
    outside8 = (low & last_row) | (jnp.logical_not(low) & first_row)
    outside = ((row24 >= 16) & (row24 < 20) & last_row) | ((row24 >= 20) & first_row)
    j = lane24 % 32
    outside_strip = outside | ((j >= HALO) & (j < 16) & (col == cols - 1)) | ((j >= 16) & (j < 28) & (col == 0))

    tiles_y, tiles_x = design.shape

    def gain_at(first, tile_x):
        tile_y = jnp.clip(first, 0, tiles_y * TILE - 1) // TILE
        tile_x = jnp.clip(tile_x, 0, tiles_x - 1)
        return design[tile_y, tile_x].astype(jnp.float32) * contrast[material[tile_y, tile_x]]

    def gain_rows(tile_x):
        here = gain_at(row * ROWS, tile_x)
        up = gain_at(row * ROWS + ROWS, tile_x)
        down = gain_at(row * ROWS - HALO, tile_x)
        return here, jnp.where(row24 < 16, here, jnp.where(row24 < 20, up, down))

    here_main, gain_main = gain_rows(col)
    here_right, gain_right = gain_rows(col + 1)
    here_left, gain_left = gain_rows(col - 1)

    wide[0:8, 0:LANES] = jnp.where(first_row, 0.0, below[52])
    wide[8:16, 0:LANES] = jnp.where(first_row, 0.0, below[53])
    wide[0:8, LANES : 2 * LANES] = jnp.where(first_row, 0.0, strip_below[13])
    wide[8:16, LANES : 2 * LANES] = jnp.where(first_row, 0.0, strip_below[14])
    wide[16:32, 0:LANES] = density[...]
    wide[16:32, LANES : 2 * LANES] = side[...]
    wide[32:40, 0:LANES] = jnp.where(last_row, 0.0, above[52])
    wide[40:48, 0:LANES] = jnp.where(last_row, 0.0, above[53])
    wide[32:40, LANES : 2 * LANES] = jnp.where(last_row, 0.0, strip_above[13])
    wide[40:48, LANES : 2 * LANES] = jnp.where(last_row, 0.0, strip_above[14])
    filtered = cone(lambda a: wide[8 + a : 40 + a], 32)
    low2 = lax.broadcasted_iota(jnp.int32, (8, 2 * LANES), 0) < 4
    filtered = jnp.concatenate(
        [filtered[8:24], jnp.where(low2, filtered[24:32], filtered[0:8])], axis=0
    )
    design_main = gain_main * filtered[:, :LANES]
    beside = filtered[:, LANES:]
    block = filtered[:, :LANES]
    right_side = jnp.where(lane24 < HALO, turn(block, HALO, 1), turn(beside, HALO, 1))
    left_side = jnp.where(lane24 < 28, turn(beside, 28, 1), turn(block, 28, 1))
    quarter = jnp.where(lane24 < 16, right_side * gain_right, left_side * gain_left)
    quarter = jnp.where((lane24 < HALO) | (lane24 >= 28), turn_edges(right_side, left_side, lane24) * gain_main, quarter)
    quarter = jnp.where(lane24 < 32, quarter, 0.0)
    quarter = quarter + turn(quarter, 32, 1)
    design_strip = quarter + turn(quarter, 64, 1)

    def whole(inner, halo):
        return jnp.concatenate([inner, halo], axis=0)

    for z in range(Z):
        k = 48 + z // 2
        halo = unpack(above[k], below[k], low, z % 2)
        step = 0.5 / (4.0 + 0.5 * (whole(background[z], halo) + design_main))
        step = jnp.where(outside, 0.0, step)
        rate[z] = step
        keep[z] = 0.5 + 4.0 * step
    for t in range(2):
        halo = unpack(strip_above[12], strip_below[12], low, t)
        step = 0.5 / (4.0 + 0.5 * (whole(strips[12, t], halo) + design_strip))
        step = jnp.where(outside_strip, 0.0, step)
        strip_rate[t] = step
        strip_keep[t] = 0.5 + 4.0 * step

    starts = (field, adjoint)
    sources = (source, adjoint_source)
    for f in range(2):
        for c in range(3):
            g = 3 * f + c
            for z in range(Z):
                k = 4 * g + z // 2
                halo = jnp.where(outside8, 0.0, unpack(above[k], below[k], low, z % 2))
                fields[f, c, z] = whole(starts[f][c, z], halo)
                k = 4 * (6 + g) + z // 2
                halo = unpack(above[k], below[k], low, z % 2)
                drive[f, c, z] = rate[z] * whole(sources[f][c, z], halo)
            for t in range(2):
                halo = jnp.where(outside8, 0.0, unpack(strip_above[g], strip_below[g], low, t))
                strip_fields[f, c, t] = whole(strips[g, t], halo)
                halo = unpack(strip_above[6 + g], strip_below[6 + g], low, t)
                strip_drive[f, c, t] = strip_rate[t] * whole(strips[6 + g, t], halo)

    at_last, at_first = lane24 == LANES - 1, lane24 == 0

    def ahead_y(value):
        return turn(value, -1, 0)

    def behind_y(value):
        return turn(value, 1, 0)

    def sweep(_, carry):
        for f in range(2):
            ex, ey, ez = ([strip_fields[f, c, t] for t in range(2)] for c in range(3))

            def above_z(pair):
                return pair[1], jnp.where(lane24 < 96, turn(pair[0], -32, 1), 0.0)

            ex_z, ey_z = above_z(ex), above_z(ey)
            hx, hy, hz = [], [], []
            for t in range(2):
                hx.append((ahead_y(ez[t]) - ez[t]) - (ey_z[t] - ey[t]))
                hy.append((ex_z[t] - ex[t]) - (turn(ez[t], -1, 1) - ez[t]))
                hz.append((turn(ey[t], -1, 1) - ey[t]) - (ahead_y(ex[t]) - ex[t]))
            bottom = lane24 < 32
            hx_z = (jnp.where(bottom, -ey[0], turn(hx[1], 32, 1)), hx[0])
            hy_z = (jnp.where(bottom, ex[0], turn(hy[1], 32, 1)), hy[0])
            for t in range(2):
                curl_x = (hz[t] - behind_y(hz[t])) - (hy[t] - hy_z[t])
                curl_y = (hx[t] - hx_z[t]) - (hz[t] - turn(hz[t], 1, 1))
                curl_z = (hy[t] - turn(hy[t], 1, 1)) - (hx[t] - behind_y(hx[t]))
                step, kept = strip_rate[t], strip_keep[t]
                strip_fields[f, 0, t] = kept * ex[t] + strip_drive[f, 0, t] - step * curl_x
                strip_fields[f, 1, t] = kept * ey[t] + strip_drive[f, 1, t] - step * curl_y
                strip_fields[f, 2, t] = kept * ez[t] + strip_drive[f, 2, t] - step * curl_z

            def ahead_x(value, strip, z):
                return jnp.where(at_last, turn(strip[z % 2], 123 - 32 * (z // 2), 1), turn(value, -1, 1))

            def behind_x(value, strip, z):
                return jnp.where(at_first, turn(strip[z % 2], -(32 * (z // 2) + 27), 1), turn(value, 1, 1))

            mx, my, mz = fields[f, 0, 0], fields[f, 1, 0], fields[f, 2, 0]
            gx_before, gy_before = -my, mx
            for z in range(Z):
                if z < Z - 1:
                    nx, ny, nz = fields[f, 0, z + 1], fields[f, 1, z + 1], fields[f, 2, z + 1]
                else:
                    nx = ny = nz = jnp.zeros_like(mx)
                gx = (ahead_y(mz) - mz) - (ny - my)
                gy = (nx - mx) - (ahead_x(mz, ez, z) - mz)
                gz = (ahead_x(my, ey, z) - my) - (ahead_y(mx) - mx)
                curl_x = (gz - behind_y(gz)) - (gy - gy_before)
                curl_y = (gx - gx_before) - (gz - behind_x(gz, hz, z))
                curl_z = (gy - behind_x(gy, hy, z)) - (gx - behind_y(gx))
                step, kept = rate[z], keep[z]
                fields[f, 0, z] = kept * mx + drive[f, 0, z] - step * curl_x
                fields[f, 1, z] = kept * my + drive[f, 1, z] - step * curl_y
                fields[f, 2, z] = kept * mz + drive[f, 2, z] - step * curl_z
                gx_before, gy_before = gx, gy
                mx, my, mz = nx, ny, nz
        return carry

    lax.fori_loop(0, ITERS, sweep, 0)

    product = jnp.zeros((ROWS, LANES), jnp.float32)
    strip_product = jnp.zeros((ROWS, LANES), jnp.float32)
    for c in range(3):
        for z in range(Z):
            forward, backward = fields[0, c, z, 0:ROWS], fields[1, c, z, 0:ROWS]
            field_out[c, z] = forward
            adjoint_out[c, z] = backward
            product = product + forward * backward
        for t in range(2):
            strip_product = strip_product + strip_fields[0, c, t, 0:ROWS] * strip_fields[1, c, t, 0:ROWS]
    strip_product = strip_product + turn(strip_product, 64, 1)
    strip_product = strip_product + turn(strip_product, 32, 1)
    local = product * (-0.5 * here_main)
    lane = lanes_of(ROWS)
    local_side = jnp.where(
        lane < 64, turn(strip_product, -4, 1) * (-0.5 * here_right), turn(strip_product, 100, 1) * (-0.5 * here_left)
    )
    local_down[:, 0:LANES] = local[0:8]
    local_down[:, LANES : 2 * LANES] = local_side[0:8]
    local_up[:, 0:LANES] = local[8:16]
    local_up[:, LANES : 2 * LANES] = local_side[8:16]


def turn_edges(right_side, left_side, lane):
    return jnp.where(lane < 16, right_side, left_side)


def gradient_kernel(own_up, own_down, above, below, gradient, wide):
    row = lax.axis_index("gy")
    wide[0:8] = jnp.where(row == 0, 0.0, below[...])
    wide[8:16] = own_down[...]
    wide[16:24] = own_up[...]
    wide[24:32] = jnp.where(row == lax.axis_size("gy") - 1, 0.0, above[...])
    gradient[...] = cone(lambda a: wide[8 + a : 24 + a], ROWS)[:, :LANES]


def ring(axis, step):
    size = lax.axis_size(axis)
    return [(i, (i + step) % size) for i in range(size)]


def shape(*dims):
    return jax.ShapeDtypeStruct(dims, jnp.float32)


def call(kernel, outs, smem=0, scratch=()):
    def run(*operands):
        spaces = [SMEM] * smem + [VMEM] * (len(operands) - smem)
        return pl.pallas_call(
            kernel,
            out_shape=outs,
            in_specs=[pl.BlockSpec(memory_space=space) for space in spaces],
            out_specs=jax.tree.map(lambda _: pl.BlockSpec(memory_space=VMEM), outs),
            scratch_shapes=[pltpu.VMEM(dims, jnp.float32) for dims in scratch],
            compiler_params=pltpu.CompilerParams(vmem_limit_bytes=LIMIT),
        )(*operands)

    return run


def on_device(background, density, design_tiles, material_tiles, contrast, source, adjoint_source, field_start, adjoint_start):
    packed = 4 * GROUPS + 2
    right, left, up, down = call(
        pack_kernel,
        [shape(GROUPS + 1, ROWS, LANES), shape(GROUPS + 1, ROWS, LANES), shape(packed, 8, LANES), shape(packed, 8, LANES)],
    )(field_start, adjoint_start, source, adjoint_source, background, density)
    from_left = lax.ppermute(right, "gx", ring("gx", 1))
    from_right = lax.ppermute(left, "gx", ring("gx", -1))
    below = lax.ppermute(up, "gy", ring("gy", 1))
    above = lax.ppermute(down, "gy", ring("gy", -1))
    strips, side, strip_up, strip_down = call(
        strip_kernel,
        [shape(GROUPS, 2, ROWS, LANES), shape(ROWS, LANES), shape(GROUPS + 2, 8, LANES), shape(GROUPS + 2, 8, LANES)],
    )(right, left, from_left, from_right)
    strip_below = lax.ppermute(strip_up, "gy", ring("gy", 1))
    strip_above = lax.ppermute(strip_down, "gy", ring("gy", -1))
    block = shape(3, Z, ROWS, LANES)
    field, adjoint, local_up, local_down = call(
        main_kernel,
        [block, block, shape(8, 2 * LANES), shape(8, 2 * LANES)],
        smem=3,
        scratch=(
            (2, 3, Z, WRAP, LANES),
            (2, 3, Z, WRAP, LANES),
            (Z, WRAP, LANES),
            (Z, WRAP, LANES),
            (2, 3, 2, WRAP, LANES),
            (2, 3, 2, WRAP, LANES),
            (2, WRAP, LANES),
            (2, WRAP, LANES),
            (48, 2 * LANES),
        ),
    )(
        design_tiles, material_tiles, contrast, field_start, adjoint_start, source, adjoint_source, background, density,
        above, below, strips, side, strip_above, strip_below,
    )
    local_below = lax.ppermute(local_up, "gy", ring("gy", 1))
    local_above = lax.ppermute(local_down, "gy", ring("gy", -1))
    gradient = call(gradient_kernel, shape(ROWS, LANES), scratch=((32, 2 * LANES),))(
        local_up, local_down, local_above, local_below
    )
    return (field, adjoint, gradient)


def solution(mesh):
    in_specs = (
        P(None, "gy", "gx"),
        P("gy", "gx"),
        P(),
        P(),
        P(),
        P(None, None, "gy", "gx"),
        P(None, None, "gy", "gx"),
        P(None, None, "gy", "gx"),
        P(None, None, "gy", "gx"),
    )
    out_specs = (P(None, None, "gy", "gx"), P(None, None, "gy", "gx"), P("gy", "gx"))
    return jax.shard_map(on_device, mesh=mesh, in_specs=in_specs, out_specs=out_specs, check_vma=False)
```

time: 176 us -> 55.9 us (0.32)
  the two profiles are of different devices: /device:TPU:902 before, /device:TPU:6 now
where the time goes in v1:
time: 55.9 us; the launch traced here: 55.5 us
  starting transfers between devices  26.9 us (48%)
  waiting for transfers between devices  12.6 us (23%)
  Pallas kernels  9.43 us (17%)
  local copies, waits for them, and re-layouts  5.86 us (10%)
  between operations  0.78 us (1%)
    ppermute x1, starting transfers between devices, on_device(): above = lax.ppermute(down, 'gy', ring('gy', -1))  16.2 us
    pallas_call x4, Pallas kernels, run(): pl.pallas_call(kernel, out_shape=outs, in_specs=[pl.BlockSpec(memory_spac...  9.43 us
    unnamed x28, local copies, waits for them, and re-layouts  5.86 us
    ppermute x1, waiting for transfers between devices, on_device(): from_right = lax.ppermute(left, 'gx', ring('gx', -1))  5.7 us
    ppermute x1, starting transfers between devices, on_device(): from_left = lax.ppermute(right, 'gx', ring('gx', 1))  3.39 us
    ppermute x1, waiting for transfers between devices, on_device(): strip_below = lax.ppermute(strip_up, 'gy', ring('gy', 1))  2.99 us
    ppermute x1, starting transfers between devices, on_device(): local_above = lax.ppermute(local_down, 'gy', ring('gy', -1))  2.95 us
    ppermute x1, starting transfers between devices, on_device(): from_right = lax.ppermute(left, 'gx', ring('gx', -1))  2.57 us
  transfers between devices with their start and end apart: 8, of which 5 were waited for; matrix products, arithmetic and copies ran while one was open for 0% of the time, Pallas kernels for 0%

profile of v1, /device:TPU:6, one launch (start us, length us, event | category | flops | bytes accessed | tf_op | source)
XLA Modules:
  0.0 55.5 jit_solution(9639279573950762817)
XLA Ops:
  0.6 0.0 copy-start
  0.6 0.9 %copy-done = f32[3,8,16,128]{3,2,1,0:T(8,128)S(1)} copy-done((f32[3,8,16,128]{3,2,1,0:T(8,128)S(1)}, f32[3,8,16,128]{3,2,1,0:T(8,128)}, u32[]{:S(2)}) %copy-start) | copy-done | bytes 196632
  1.6 0.0 copy-start.2
  1.6 0.9 %copy-done.2 = f32[3,8,16,128]{3,2,1,0:T(8,128)S(1)} copy-done((f32[3,8,16,128]{3,2,1,0:T(8,128)S(1)}, f32[3,8,16,128]{3,2,1,0:T(8,128)}, u32[]{:S(2)}) %copy-start.2) | copy-done | bytes 196632
  2.5 0.0 copy-start.4
  2.5 0.9 %copy-done.4 = f32[3,8,16,128]{3,2,1,0:T(8,128)S(1)} copy-done((f32[3,8,16,128]{3,2,1,0:T(8,128)S(1)}, f32[3,8,16,128]{3,2,1,0:T(8,128)}, u32[]{:S(2)}) %copy-start.4) | copy-done | bytes 196632
  3.4 0.0 copy-start.6
  3.4 0.9 %copy-done.6 = f32[3,8,16,128]{3,2,1,0:T(8,128)S(1)} copy-done((f32[3,8,16,128]{3,2,1,0:T(8,128)S(1)}, f32[3,8,16,128]{3,2,1,0:T(8,128)}, u32[]{:S(2)}) %copy-start.6) | copy-done | bytes 196632
  4.3 0.0 copy-start.8
  4.3 0.8 %copy-done.8 = f32[8,16,128]{2,1,0:T(8,128)S(1)} copy-done((f32[8,16,128]{2,1,0:T(8,128)S(1)}, f32[8,16,128]{2,1,0:T(8,128)}, u32[]{:S(2)}) %copy-start.8) | copy-done | bytes 65560
  5.2 0.0 copy-start.10
  5.2 0.7 %copy-done.10 = f32[16,128]{1,0:T(8,128)S(1)} copy-done((f32[16,128]{1,0:T(8,128)S(1)}, f32[16,128]{1,0:T(8,128)}, u32[]{:S(2)}) %copy-start.10) | copy-done | bytes 8216
  5.9 0.0 copy-start.5
  5.9 0.0 copy-start.7
  5.9 0.5 shard_map.112
  6.4 16.2 %collective-permute-start = (f32[54,8,128]{2,1,0:T(8,128)S(1)}, f32[54,8,128]{2,1,0:T(8,128)S(1)}, u32[]{:S(2)}, u32[]{:S(2)}) collective-permute-start(f32[54,8,128]{2,1,0:T(8,128)S(1)} %get-tuple-element.15), channel_id=1, source_target_pairs={{0,63},{1,0},{2,1},{3,2},{4,3},{5,4},{6,5},{7,6},{8,7},{9,8},{10,9... | collective-permute-start | bytes 663560 | tf_op jit(solution)/shard_map/ppermute | solution.py:352
  22.6 0.0 collective-permute-start.1
  22.6 3.4 %collective-permute-start.2 = (f32[14,16,128]{2,1,0:T(8,128)S(1)}, f32[14,16,128]{2,1,0:T(8,128)S(1)}, u32[]{:S(2)}, u32[]{:S(2)}) collective-permute-start(f32[14,16,128]{2,1,0:T(8,128)S(1)} %get-tuple-element.17.own_right), channel_id=1, source_target_pairs={{0,64},{64,128},{128,192},{192,256},{256,320},{320,384},{384,448},... | collective-permute-start | bytes 344072 | tf_op jit(solution)/shard_map/ppermute | solution.py:349
  26.0 0.0 copy-start.12
  26.0 0.0 copy-start.1
  26.0 0.0 copy-start.3
  26.0 0.0 copy-start.9
  26.1 2.6 %collective-permute-start.3 = (f32[14,16,128]{2,1,0:T(8,128)S(1)}, f32[14,16,128]{2,1,0:T(8,128)S(1)}, u32[]{:S(2)}, u32[]{:S(2)}) collective-permute-start(f32[14,16,128]{2,1,0:T(8,128)S(1)} %get-tuple-element.18.own_left), channel_id=1, source_target_pairs={{0,960},{64,0},{128,64},{192,128},{256,192},{320,256},{384,320},{4... | collective-permute-start | bytes 344072 | tf_op jit(solution)/shard_map/ppermute | solution.py:350
  28.6 0.6 %collective-permute-done.2.from_left = f32[14,16,128]{2,1,0:T(8,128)S(1)} collective-permute-done((f32[14,16,128]{2,1,0:T(8,128)S(1)}, f32[14,16,128]{2,1,0:T(8,128)S(1)}, u32[]{:S(2)}, u32[]{:S(2)}) %collective-permute-start.2) | collective-permute-done | bytes 114720 | tf_op jit(solution)/shard_map/ppermute | solution.py:349
  29.3 5.7 %collective-permute-done.3.from_right = f32[14,16,128]{2,1,0:T(8,128)S(1)} collective-permute-done((f32[14,16,128]{2,1,0:T(8,128)S(1)}, f32[14,16,128]{2,1,0:T(8,128)S(1)}, u32[]{:S(2)}, u32[]{:S(2)}) %collective-permute-start.3) | collective-permute-done | bytes 114720 | tf_op jit(solution)/shard_map/ppermute | solution.py:350
  35.0 0.1 shard_map.113
  35.1 0.0 copy-start.11
  35.1 1.7 %collective-permute-start.4 = (f32[15,8,128]{2,1,0:T(8,128)S(1)}, f32[15,8,128]{2,1,0:T(8,128)S(1)}, u32[]{:S(2)}, u32[]{:S(2)}) collective-permute-start(f32[15,8,128]{2,1,0:T(8,128)S(1)} %get-tuple-element.21), channel_id=1, source_target_pairs={{0,63},{1,0},{2,1},{3,2},{4,3},{5,4},{6,5},{7,6},{8,7},{9,8},{10,9... | collective-permute-start | bytes 184328 | tf_op jit(solution)/shard_map/ppermute | solution.py:358
  36.9 0.0 collective-permute-start.5
  36.9 1.9 %collective-permute-done.4.strip_above = f32[15,8,128]{2,1,0:T(8,128)S(1)} collective-permute-done((f32[15,8,128]{2,1,0:T(8,128)S(1)}, f32[15,8,128]{2,1,0:T(8,128)S(1)}, u32[]{:S(2)}, u32[]{:S(2)}) %collective-permute-start.4) | collective-permute-done | bytes 61472 | tf_op jit(solution)/shard_map/ppermute | solution.py:358
  38.7 3.0 %collective-permute-done.5.strip_below = f32[15,8,128]{2,1,0:T(8,128)S(1)} collective-permute-done((f32[15,8,128]{2,1,0:T(8,128)S(1)}, f32[15,8,128]{2,1,0:T(8,128)S(1)}, u32[]{:S(2)}, u32[]{:S(2)}) %collective-permute-start.5) | collective-permute-done | bytes 61472 | tf_op jit(solution)/shard_map/ppermute | solution.py:357
  41.7 0.0 collective-permute-done.above
  41.7 0.0 collective-permute-done.1.below
  41.7 0.0 copy-start.13
  41.7 0.0 copy-done.5
  41.7 0.0 copy-done.7
  41.8 0.0 copy-done.12
  41.8 0.0 copy-done.1
  41.8 0.0 copy-done.3
  41.8 0.0 copy-done.9
  41.8 0.0 copy-done.11
  41.8 0.6 %copy-done.13 = f32[4]{0:T(128)S(1)} copy-done((f32[4]{0:T(128)S(1)}, f32[4]{0:T(128)}, u32[]{:S(2)}) %copy-start.13) | copy-done | bytes 40
  42.4 8.0 %shard_map.114 = (f32[3,8,16,128]{3,2,1,0:T(8,128)}, f32[3,8,16,128]{3,2,1,0:T(8,128)}, f32[8,256]{1,0:T(8,128)S(1)}, f32[8,256]{1,0:T(8,128)S(1)}) custom-call(s32[8,16]{1,0:T(8,128)S(1)} %copy-done.11, s32[8,16]{1,0:T(8,128)S(1)} %copy-done.12, f32[4]{0:T(128)S(1)} %copy-done.13, f32[3,8,16,128]{3,2,1,0:T(8,128)S(1)} %copy-done.1, ...), custom_call_target="tpu_custom_call" | custom-call | tf_op jit(solution)/shard_map/pallas_call | solution.py:331
  50.4 0.0 collective-permute-start.7
  50.4 3.0 %collective-permute-start.6 = (f32[8,256]{1,0:T(8,128)S(1)}, f32[8,256]{1,0:T(8,128)S(1)}, u32[]{:S(2)}, u32[]{:S(2)}) collective-permute-start(f32[8,256]{1,0:T(8,128)S(1)} %get-tuple-element.26.own_down), channel_id=1, source_target_pairs={{0,63},{1,0},{2,1},{3,2},{4,3},{5,4},{6,5},{7,6},{8,7},{9,8},{10,9... | collective-permute-start | bytes 24584 | tf_op jit(solution)/shard_map/ppermute | solution.py:380
  53.3 1.3 %collective-permute-done.7.below = f32[8,256]{1,0:T(8,128)S(1)} collective-permute-done((f32[8,256]{1,0:T(8,128)S(1)}, f32[8,256]{1,0:T(8,128)S(1)}, u32[]{:S(2)}, u32[]{:S(2)}) %collective-permute-start.7) | collective-permute-done | bytes 8224 | tf_op jit(solution)/shard_map/ppermute | solution.py:379
  54.6 0.0 collective-permute-done.6.above
  54.7 0.8 %shard_map.115 = f32[16,128]{1,0:T(8,128)} custom-call(f32[8,256]{1,0:T(8,128)S(1)} %get-tuple-element.25.own_up, f32[8,256]{1,0:T(8,128)S(1)} %get-tuple-element.26.own_down, f32[8,256]{1,0:T(8,128)S(1)} %collective-permute-done.6.above, f32[8,256]{1,0:T(8,128)S(1)} %collective-permute-done.7.below), custom_call_target="tpu_custom_call" | custom-call | tf_op jit(solution)/shard_map/pallas_call | solution.py:331
Async XLA Ops:
  0.6 0.9 %copy-start = (f32[3,8,16,128]{3,2,1,0:T(8,128)S(1)}, f32[3,8,16,128]{3,2,1,0:T(8,128)}, u32[]{:S(2)}) copy-start(f32[3,8,16,128]{3,2,1,0:T(8,128)} %field.3) | copy-start | bytes 589828
  1.6 0.9 %copy-start.2 = (f32[3,8,16,128]{3,2,1,0:T(8,128)S(1)}, f32[3,8,16,128]{3,2,1,0:T(8,128)}, u32[]{:S(2)}) copy-start(f32[3,8,16,128]{3,2,1,0:T(8,128)} %adjoint.3) | copy-start | bytes 589828
  2.5 0.9 %copy-start.4 = (f32[3,8,16,128]{3,2,1,0:T(8,128)S(1)}, f32[3,8,16,128]{3,2,1,0:T(8,128)}, u32[]{:S(2)}) copy-start(f32[3,8,16,128]{3,2,1,0:T(8,128)} %source.3) | copy-start | bytes 589828
  3.4 0.9 %copy-start.6 = (f32[3,8,16,128]{3,2,1,0:T(8,128)S(1)}, f32[3,8,16,128]{3,2,1,0:T(8,128)}, u32[]{:S(2)}) copy-start(f32[3,8,16,128]{3,2,1,0:T(8,128)} %adjoint_source.3) | copy-start | bytes 589828
  4.3 0.8 %copy-start.8 = (f32[8,16,128]{2,1,0:T(8,128)S(1)}, f32[8,16,128]{2,1,0:T(8,128)}, u32[]{:S(2)}) copy-start(f32[8,16,128]{2,1,0:T(8,128)} %background.3) | copy-start | bytes 196612
  5.2 0.7 %copy-start.10 = (f32[16,128]{1,0:T(8,128)S(1)}, f32[16,128]{1,0:T(8,128)}, u32[]{:S(2)}) copy-start(f32[16,128]{1,0:T(8,128)} %density.3) | copy-start | bytes 24580
  5.9 35.9 %copy-start.5 = (f32[3,8,16,128]{3,2,1,0:T(8,128)S(1)}, f32[3,8,16,128]{3,2,1,0:T(8,128)}, u32[]{:S(2)}) copy-start(f32[3,8,16,128]{3,2,1,0:T(8,128)} %source.3) | copy-start | bytes 589828
  5.9 35.9 %copy-start.7 = (f32[3,8,16,128]{3,2,1,0:T(8,128)S(1)}, f32[3,8,16,128]{3,2,1,0:T(8,128)}, u32[]{:S(2)}) copy-start(f32[3,8,16,128]{3,2,1,0:T(8,128)} %adjoint_source.3) | copy-start | bytes 589828
  6.4 35.3 %collective-permute-start = (f32[54,8,128]{2,1,0:T(8,128)S(1)}, f32[54,8,128]{2,1,0:T(8,128)S(1)}, u32[]{:S(2)}, u32[]{:S(2)}) collective-permute-start(f32[54,8,128]{2,1,0:T(8,128)S(1)} %get-tuple-element.15), channel_id=1, source_target_pairs={{0,63},{1,0},{2,1},{3,2},{4,3},{5,4},{6,5},{7,6},{8,7},{9,8},{10,9... | collective-permute-start | bytes 663560 | tf_op jit(solution)/shard_map/ppermute | solution.py:352
  22.6 19.1 %collective-permute-start.1 = (f32[54,8,128]{2,1,0:T(8,128)S(1)}, f32[54,8,128]{2,1,0:T(8,128)S(1)}, u32[]{:S(2)}, u32[]{:S(2)}) collective-permute-start(f32[54,8,128]{2,1,0:T(8,128)S(1)} %get-tuple-element.16), channel_id=1, source_target_pairs={{0,1},{1,2},{2,3},{3,4},{4,5},{5,6},{6,7},{7,8},{8,9},{9,10},{10,1... | collective-permute-start | bytes 663560 | tf_op jit(solution)/shard_map/ppermute | solution.py:351
  22.6 6.7 %collective-permute-start.2 = (f32[14,16,128]{2,1,0:T(8,128)S(1)}, f32[14,16,128]{2,1,0:T(8,128)S(1)}, u32[]{:S(2)}, u32[]{:S(2)}) collective-permute-start(f32[14,16,128]{2,1,0:T(8,128)S(1)} %get-tuple-element.17.own_right), channel_id=1, source_target_pairs={{0,64},{64,128},{128,192},{192,256},{256,320},{320,384},{384,448},... | collective-permute-start | bytes 344072 | tf_op jit(solution)/shard_map/ppermute | solution.py:349
  26.0 15.7 %copy-start.12 = (s32[8,16]{1,0:T(8,128)S(1)}, s32[8,16]{1,0:T(8,128)}, u32[]{:S(2)}) copy-start(s32[8,16]{1,0:T(8,128)} %material.1) | copy-start | bytes 1540
  26.0 15.7 %copy-start.1 = (f32[3,8,16,128]{3,2,1,0:T(8,128)S(1)}, f32[3,8,16,128]{3,2,1,0:T(8,128)}, u32[]{:S(2)}) copy-start(f32[3,8,16,128]{3,2,1,0:T(8,128)} %field.3) | copy-start | bytes 589828
  26.0 15.7 %copy-start.3 = (f32[3,8,16,128]{3,2,1,0:T(8,128)S(1)}, f32[3,8,16,128]{3,2,1,0:T(8,128)}, u32[]{:S(2)}) copy-start(f32[3,8,16,128]{3,2,1,0:T(8,128)} %adjoint.3) | copy-start | bytes 589828
  26.0 15.7 %copy-start.9 = (f32[8,16,128]{2,1,0:T(8,128)S(1)}, f32[8,16,128]{2,1,0:T(8,128)}, u32[]{:S(2)}) copy-start(f32[8,16,128]{2,1,0:T(8,128)} %background.3) | copy-start | bytes 196612
  26.1 8.9 %collective-permute-start.3 = (f32[14,16,128]{2,1,0:T(8,128)S(1)}, f32[14,16,128]{2,1,0:T(8,128)S(1)}, u32[]{:S(2)}, u32[]{:S(2)}) collective-permute-start(f32[14,16,128]{2,1,0:T(8,128)S(1)} %get-tuple-element.18.own_left), channel_id=1, source_target_pairs={{0,960},{64,0},{128,64},{192,128},{256,192},{320,256},{384,320},{4... | collective-permute-start | bytes 344072 | tf_op jit(solution)/shard_map/ppermute | solution.py:350
  35.1 6.7 %copy-start.11 = (s32[8,16]{1,0:T(8,128)S(1)}, s32[8,16]{1,0:T(8,128)}, u32[]{:S(2)}) copy-start(s32[8,16]{1,0:T(8,128)} %design.1) | copy-start | bytes 1540
  35.1 3.6 %collective-permute-start.4 = (f32[15,8,128]{2,1,0:T(8,128)S(1)}, f32[15,8,128]{2,1,0:T(8,128)S(1)}, u32[]{:S(2)}, u32[]{:S(2)}) collective-permute-start(f32[15,8,128]{2,1,0:T(8,128)S(1)} %get-tuple-element.21), channel_id=1, source_target_pairs={{0,63},{1,0},{2,1},{3,2},{4,3},{5,4},{6,5},{7,6},{8,7},{9,8},{10,9... | collective-permute-start | bytes 184328 | tf_op jit(solution)/shard_map/ppermute | solution.py:358
  36.9 4.9 %collective-permute-start.5 = (f32[15,8,128]{2,1,0:T(8,128)S(1)}, f32[15,8,128]{2,1,0:T(8,128)S(1)}, u32[]{:S(2)}, u32[]{:S(2)}) collective-permute-start(f32[15,8,128]{2,1,0:T(8,128)S(1)} %get-tuple-element.22), channel_id=1, source_target_pairs={{0,1},{1,2},{2,3},{3,4},{4,5},{5,6},{6,7},{7,8},{8,9},{9,10},{10,1... | collective-permute-start | bytes 184328 | tf_op jit(solution)/shard_map/ppermute | solution.py:357
  41.7 0.7 %copy-start.13 = (f32[4]{0:T(128)S(1)}, f32[4]{0:T(128)}, u32[]{:S(2)}) copy-start(f32[4]{0:T(128)} %contrast.1) | copy-start | bytes 52
  50.4 4.3 %collective-permute-start.7 = (f32[8,256]{1,0:T(8,128)S(1)}, f32[8,256]{1,0:T(8,128)S(1)}, u32[]{:S(2)}, u32[]{:S(2)}) collective-permute-start(f32[8,256]{1,0:T(8,128)S(1)} %get-tuple-element.25.own_up), channel_id=1, source_target_pairs={{0,1},{1,2},{2,3},{3,4},{4,5},{5,6},{6,7},{7,8},{8,9},{9,10},{10,1... | collective-permute-start | bytes 24584 | tf_op jit(solution)/shard_map/ppermute | solution.py:379
  50.4 4.3 %collective-permute-start.6 = (f32[8,256]{1,0:T(8,128)S(1)}, f32[8,256]{1,0:T(8,128)S(1)}, u32[]{:S(2)}, u32[]{:S(2)}) collective-permute-start(f32[8,256]{1,0:T(8,128)S(1)} %get-tuple-element.26.own_down), channel_id=1, source_target_pairs={{0,63},{1,0},{2,1},{3,2},{4,3},{5,4},{6,5},{7,6},{8,7},{9,8},{10,9... | collective-permute-start | bytes 24584 | tf_op jit(solution)/shard_map/ppermute | solution.py:380

commit v2 on v1

--- a/solution.py
+++ b/solution.py
@@ -17,8 +17,6 @@
 HALO = 4
 WRAP = ROWS + 8
 GROUPS = 13
-WIDTH = 16
-SMEM = pltpu.SMEM
 VMEM = pltpu.VMEM
 LIMIT = 48 * 1024 * 1024
 
@@ -64,10 +62,23 @@
     return result
 
 
-def pack_kernel(field, adjoint, source, adjoint_source, background, density, right, left, up, down):
+def edge_kernel(
+    design_in, material_in, contrast_in, field_in, adjoint_in, source_in, adjoint_source_in, background_in, density_in,
+    right, left, gains,
+    design, material, contrast, field, adjoint, source, adjoint_source, background, density, done,
+):
+    arrays = (
+        (field_in, field), (adjoint_in, adjoint), (source_in, source), (adjoint_source_in, adjoint_source),
+        (background_in, background), (density_in, density),
+        (design_in, design), (material_in, material), (contrast_in, contrast),
+    )
+    copies = [pltpu.make_async_copy(here, there, done.at[i]) for i, (here, there) in enumerate(arrays)]
+    for copy in copies:
+        copy.start()
     lane = lanes_of(ROWS)
-    low = rows_of(8) < 4
     for g in range(GROUPS):
+        if g % 3 == 0:
+            copies[g // 3].wait()
         planes = background if g == 12 else (field, adjoint, source, adjoint_source)[g // 3].at[g % 3]
         to_right = to_left = None
         for z in range(Z):
@@ -82,12 +93,36 @@
                 to_left = jnp.where(chosen, here_left, to_left)
         right[g] = to_right
         left[g] = to_left
+    for copy in copies[5:]:
+        copy.wait()
+    right[GROUPS] = density[...]
+    left[GROUPS] = density[...]
+
+    col, row = lax.axis_index("gx"), lax.axis_index("gy")
+    row24 = rows_of(WRAP)
+    tiles_y, tiles_x = design.shape
+
+    def gain_at(first, tile_x):
+        tile_y = jnp.clip(first, 0, tiles_y * TILE - 1) // TILE
+        tile_x = jnp.clip(tile_x, 0, tiles_x - 1)
+        return design[tile_y, tile_x].astype(jnp.float32) * contrast[material[tile_y, tile_x]]
+
+    for k in range(3):
+        tile_x = col + (0, 1, -1)[k]
+        here = gain_at(row * ROWS, tile_x)
+        up = gain_at(row * ROWS + ROWS, tile_x)
+        down = gain_at(row * ROWS - HALO, tile_x)
+        gains[k] = jnp.where(row24 < 16, here, jnp.where(row24 < 20, up, down))
+
+
+def rows_kernel(field, adjoint, source, adjoint_source, background, density, sent, up, down):
+    low = rows_of(8) < 4
+    for g in range(GROUPS):
+        planes = background if g == 12 else (field, adjoint, source, adjoint_source)[g // 3].at[g % 3]
         for pair in range(Z // 2):
             k = g * (Z // 2) + pair
             down[k] = jnp.where(low, planes[2 * pair, 0:8], turn(planes[2 * pair + 1, 0:8], 4, 0))
             up[k] = jnp.where(low, turn(planes[2 * pair + 1, 8:16], 4, 0), planes[2 * pair, 8:16])
-    right[GROUPS] = density[...]
-    left[GROUPS] = density[...]
     for part in range(2):
         up[4 * GROUPS + part] = density[8 * part : 8 * part + 8]
         down[4 * GROUPS + part] = density[8 * part : 8 * part + 8]
@@ -125,37 +160,21 @@
 
 
 def main_kernel(
-    design, material, contrast, field, adjoint, source, adjoint_source, background, density,
+    gains, field, adjoint, source, adjoint_source, background, density,
     above, below, strips, side, strip_above, strip_below,
     field_out, adjoint_out, local_up, local_down,
-    fields, drive, rate, keep, strip_fields, strip_drive, strip_rate, strip_keep, wide,
+    fields, sources, curls, rate, keep, strip_fields, strip_sources, strip_curls, strip_rate, strip_keep, wide,
 ):
     col, row = lax.axis_index("gx"), lax.axis_index("gy")
     cols, rows = lax.axis_size("gx"), lax.axis_size("gy")
     first_row, last_row = row == 0, row == rows - 1
     low = rows_of(8) < 4
-    lane8, lane24, row24 = lanes_of(8), lanes_of(WRAP), rows_of(WRAP)
+    lane24, row24 = lanes_of(WRAP), rows_of(WRAP)
     outside8 = (low & last_row) | (jnp.logical_not(low) & first_row)
     outside = ((row24 >= 16) & (row24 < 20) & last_row) | ((row24 >= 20) & first_row)
     j = lane24 % 32
     outside_strip = outside | ((j >= HALO) & (j < 16) & (col == cols - 1)) | ((j >= 16) & (j < 28) & (col == 0))
-
-    tiles_y, tiles_x = design.shape
-
-    def gain_at(first, tile_x):
-        tile_y = jnp.clip(first, 0, tiles_y * TILE - 1) // TILE
-        tile_x = jnp.clip(tile_x, 0, tiles_x - 1)
-        return design[tile_y, tile_x].astype(jnp.float32) * contrast[material[tile_y, tile_x]]
-
-    def gain_rows(tile_x):
-        here = gain_at(row * ROWS, tile_x)
-        up = gain_at(row * ROWS + ROWS, tile_x)
-        down = gain_at(row * ROWS - HALO, tile_x)
-        return here, jnp.where(row24 < 16, here, jnp.where(row24 < 20, up, down))
-
-    here_main, gain_main = gain_rows(col)
-    here_right, gain_right = gain_rows(col + 1)
-    here_left, gain_left = gain_rows(col - 1)
+    gain_main, gain_right, gain_left = gains[0], gains[1], gains[2]
 
     wide[0:8, 0:LANES] = jnp.where(first_row, 0.0, below[52])
     wide[8:16, 0:LANES] = jnp.where(first_row, 0.0, below[53])
@@ -200,23 +219,23 @@
         strip_rate[t] = step
         strip_keep[t] = 0.5 + 4.0 * step
 
-    starts = (field, adjoint)
-    sources = (source, adjoint_source)
-    for f in range(2):
+    starts = (field, adjoint, source, adjoint_source)
+    for f in range(4):
         for c in range(3):
             g = 3 * f + c
             for z in range(Z):
                 k = 4 * g + z // 2
-                halo = jnp.where(outside8, 0.0, unpack(above[k], below[k], low, z % 2))
-                fields[f, c, z] = whole(starts[f][c, z], halo)
-                k = 4 * (6 + g) + z // 2
                 halo = unpack(above[k], below[k], low, z % 2)
-                drive[f, c, z] = rate[z] * whole(sources[f][c, z], halo)
+                if f < 2:
+                    fields[f, c, z] = whole(starts[f][c, z], jnp.where(outside8, 0.0, halo))
+                else:
+                    sources[f - 2, c, z] = whole(starts[f][c, z], halo)
             for t in range(2):
-                halo = jnp.where(outside8, 0.0, unpack(strip_above[g], strip_below[g], low, t))
-                strip_fields[f, c, t] = whole(strips[g, t], halo)
-                halo = unpack(strip_above[6 + g], strip_below[6 + g], low, t)
-                strip_drive[f, c, t] = strip_rate[t] * whole(strips[6 + g, t], halo)
+                halo = unpack(strip_above[g], strip_below[g], low, t)
+                if f < 2:
+                    strip_fields[f, c, t] = whole(strips[g, t], jnp.where(outside8, 0.0, halo))
+                else:
+                    strip_sources[f - 2, c, t] = whole(strips[g, t], halo)
 
     at_last, at_first = lane24 == LANES - 1, lane24 == 0
 
@@ -225,57 +244,65 @@
 
     def behind_y(value):
         return turn(value, 1, 0)
+
+    def ahead_x(value, strip, z):
+        return jnp.where(at_last, turn(strip[z % 2], 123 - 32 * (z // 2), 1), turn(value, -1, 1))
+
+    def behind_x(value, strip, z):
+        return jnp.where(at_first, turn(strip[z % 2], -(32 * (z // 2) + 27), 1), turn(value, 1, 1))
 
     def sweep(_, carry):
         for f in range(2):
             ex, ey, ez = ([strip_fields[f, c, t] for t in range(2)] for c in range(3))
-
-            def above_z(pair):
-                return pair[1], jnp.where(lane24 < 96, turn(pair[0], -32, 1), 0.0)
-
-            ex_z, ey_z = above_z(ex), above_z(ey)
-            hx, hy, hz = [], [], []
             for t in range(2):
-                hx.append((ahead_y(ez[t]) - ez[t]) - (ey_z[t] - ey[t]))
-                hy.append((ex_z[t] - ex[t]) - (turn(ez[t], -1, 1) - ez[t]))
-                hz.append((turn(ey[t], -1, 1) - ey[t]) - (ahead_y(ex[t]) - ex[t]))
-            bottom = lane24 < 32
-            hx_z = (jnp.where(bottom, -ey[0], turn(hx[1], 32, 1)), hx[0])
-            hy_z = (jnp.where(bottom, ex[0], turn(hy[1], 32, 1)), hy[0])
+                if t == 0:
+                    ex_z, ey_z = ex[1], ey[1]
+                else:
+                    ex_z = jnp.where(lane24 < 96, turn(ex[0], -32, 1), 0.0)
+                    ey_z = jnp.where(lane24 < 96, turn(ey[0], -32, 1), 0.0)
+                strip_curls[f, 0, t] = (ahead_y(ez[t]) - ez[t]) - (ey_z - ey[t])
+                strip_curls[f, 1, t] = (ex_z - ex[t]) - (turn(ez[t], -1, 1) - ez[t])
+                strip_curls[f, 2, t] = (turn(ey[t], -1, 1) - ey[t]) - (ahead_y(ex[t]) - ex[t])
+            for z in range(Z):
+                ex, ey, ez = (fields[f, c, z] for c in range(3))
+                if z < Z - 1:
+                    ex_z, ey_z = fields[f, 0, z + 1], fields[f, 1, z + 1]
+                else:
+                    ex_z = ey_z = jnp.zeros_like(ex)
+                curls[f, 0, z] = (ahead_y(ez) - ez) - (ey_z - ey)
+                curls[f, 1, z] = (ex_z - ex) - (ahead_x(ez, strip_fields.at[f, 2], z) - ez)
+                curls[f, 2, z] = (ahead_x(ey, strip_fields.at[f, 1], z) - ey) - (ahead_y(ex) - ex)
+        bottom = lane24 < 32
+        for f in range(2):
             for t in range(2):
-                curl_x = (hz[t] - behind_y(hz[t])) - (hy[t] - hy_z[t])
-                curl_y = (hx[t] - hx_z[t]) - (hz[t] - turn(hz[t], 1, 1))
-                curl_z = (hy[t] - turn(hy[t], 1, 1)) - (hx[t] - behind_y(hx[t]))
+                ex, ey, ez = (strip_fields[f, c, t] for c in range(3))
+                hx, hy, hz = (strip_curls[f, c, t] for c in range(3))
+                if t == 1:
+                    hx_z, hy_z = strip_curls[f, 0, 0], strip_curls[f, 1, 0]
+                else:
+                    hx_z = jnp.where(bottom, -ey, turn(strip_curls[f, 0, 1], 32, 1))
+                    hy_z = jnp.where(bottom, ex, turn(strip_curls[f, 1, 1], 32, 1))
+                curl_x = (hz - behind_y(hz)) - (hy - hy_z)
+                curl_y = (hx - hx_z) - (hz - turn(hz, 1, 1))
+                curl_z = (hy - turn(hy, 1, 1)) - (hx - behind_y(hx))
                 step, kept = strip_rate[t], strip_keep[t]
-                strip_fields[f, 0, t] = kept * ex[t] + strip_drive[f, 0, t] - step * curl_x
-                strip_fields[f, 1, t] = kept * ey[t] + strip_drive[f, 1, t] - step * curl_y
-                strip_fields[f, 2, t] = kept * ez[t] + strip_drive[f, 2, t] - step * curl_z
-
-            def ahead_x(value, strip, z):
-                return jnp.where(at_last, turn(strip[z % 2], 123 - 32 * (z // 2), 1), turn(value, -1, 1))
-
-            def behind_x(value, strip, z):
-                return jnp.where(at_first, turn(strip[z % 2], -(32 * (z // 2) + 27), 1), turn(value, 1, 1))
-
-            mx, my, mz = fields[f, 0, 0], fields[f, 1, 0], fields[f, 2, 0]
-            gx_before, gy_before = -my, mx
+                strip_fields[f, 0, t] = kept * ex + step * (strip_sources[f, 0, t] - curl_x)
+                strip_fields[f, 1, t] = kept * ey + step * (strip_sources[f, 1, t] - curl_y)
+                strip_fields[f, 2, t] = kept * ez + step * (strip_sources[f, 2, t] - curl_z)
             for z in range(Z):
-                if z < Z - 1:
-                    nx, ny, nz = fields[f, 0, z + 1], fields[f, 1, z + 1], fields[f, 2, z + 1]
-                else:
-                    nx = ny = nz = jnp.zeros_like(mx)
-                gx = (ahead_y(mz) - mz) - (ny - my)
-                gy = (nx - mx) - (ahead_x(mz, ez, z) - mz)
-                gz = (ahead_x(my, ey, z) - my) - (ahead_y(mx) - mx)
-                curl_x = (gz - behind_y(gz)) - (gy - gy_before)
-                curl_y = (gx - gx_before) - (gz - behind_x(gz, hz, z))
-                curl_z = (gy - behind_x(gy, hy, z)) - (gx - behind_y(gx))
+                ex, ey, ez = (fields[f, c, z] for c in range(3))
+                hx, hy, hz = (curls[f, c, z] for c in range(3))
+                if z > 0:
+                    hx_z, hy_z = curls[f, 0, z - 1], curls[f, 1, z - 1]
+                else:
+                    hx_z, hy_z = -ey, ex
+                curl_x = (hz - behind_y(hz)) - (hy - hy_z)
+                curl_y = (hx - hx_z) - (hz - behind_x(hz, strip_curls.at[f, 2], z))
+                curl_z = (hy - behind_x(hy, strip_curls.at[f, 1], z)) - (hx - behind_y(hx))
                 step, kept = rate[z], keep[z]
-                fields[f, 0, z] = kept * mx + drive[f, 0, z] - step * curl_x
-                fields[f, 1, z] = kept * my + drive[f, 1, z] - step * curl_y
-                fields[f, 2, z] = kept * mz + drive[f, 2, z] - step * curl_z
-                gx_before, gy_before = gx, gy
-                mx, my, mz = nx, ny, nz
+                fields[f, 0, z] = kept * ex + step * (sources[f, 0, z] - curl_x)
+                fields[f, 1, z] = kept * ey + step * (sources[f, 1, z] - curl_y)
+                fields[f, 2, z] = kept * ez + step * (sources[f, 2, z] - curl_z)
         return carry
 
     lax.fori_loop(0, ITERS, sweep, 0)
@@ -292,10 +319,11 @@
             strip_product = strip_product + strip_fields[0, c, t, 0:ROWS] * strip_fields[1, c, t, 0:ROWS]
     strip_product = strip_product + turn(strip_product, 64, 1)
     strip_product = strip_product + turn(strip_product, 32, 1)
-    local = product * (-0.5 * here_main)
+    local = product * (-0.5 * gain_main[0:ROWS])
     lane = lanes_of(ROWS)
     local_side = jnp.where(
-        lane < 64, turn(strip_product, -4, 1) * (-0.5 * here_right), turn(strip_product, 100, 1) * (-0.5 * here_left)
+        lane < 64, turn(strip_product, -4, 1) * (-0.5 * gain_right[0:ROWS]),
+        turn(strip_product, 100, 1) * (-0.5 * gain_left[0:ROWS]),
     )
     local_down[:, 0:LANES] = local[0:8]
     local_down[:, LANES : 2 * LANES] = local_side[0:8]
@@ -325,60 +353,62 @@
     return jax.ShapeDtypeStruct(dims, jnp.float32)
 
 
-def call(kernel, outs, smem=0, scratch=()):
+def call(kernel, outs, space=VMEM, scratch=()):
     def run(*operands):
-        spaces = [SMEM] * smem + [VMEM] * (len(operands) - smem)
         return pl.pallas_call(
             kernel,
             out_shape=outs,
-            in_specs=[pl.BlockSpec(memory_space=space) for space in spaces],
+            in_specs=[pl.BlockSpec(memory_space=space)] * len(operands),
             out_specs=jax.tree.map(lambda _: pl.BlockSpec(memory_space=VMEM), outs),
-            scratch_shapes=[pltpu.VMEM(dims, jnp.float32) for dims in scratch],
+            scratch_shapes=scratch,
             compiler_params=pltpu.CompilerParams(vmem_limit_bytes=LIMIT),
         )(*operands)
 
     return run
 
 
+def room(*dims):
+    return pltpu.VMEM(dims, jnp.float32)
+
+
 def on_device(background, density, design_tiles, material_tiles, contrast, source, adjoint_source, field_start, adjoint_start):
-    packed = 4 * GROUPS + 2
-    right, left, up, down = call(
-        pack_kernel,
-        [shape(GROUPS + 1, ROWS, LANES), shape(GROUPS + 1, ROWS, LANES), shape(packed, 8, LANES), shape(packed, 8, LANES)],
-    )(field_start, adjoint_start, source, adjoint_source, background, density)
+    inner = (field_start, adjoint_start, source, adjoint_source, background, density)
+    tiles = (design_tiles, material_tiles, contrast)
+    edges = shape(GROUPS + 1, ROWS, LANES)
+    right, left, gains = call(
+        edge_kernel,
+        [edges, edges, shape(3, WRAP, LANES)],
+        space=pl.ANY,
+        scratch=[pltpu.SMEM(a.shape, a.dtype) for a in tiles]
+        + [room(*a.shape) for a in inner]
+        + [pltpu.SemaphoreType.DMA((9,))],
+    )(*tiles, *inner)
     from_left = lax.ppermute(right, "gx", ring("gx", 1))
     from_right = lax.ppermute(left, "gx", ring("gx", -1))
+    rows = shape(4 * GROUPS + 2, 8, LANES)
+    up, down = call(rows_kernel, [rows, rows])(*inner, from_left)
     below = lax.ppermute(up, "gy", ring("gy", 1))
     above = lax.ppermute(down, "gy", ring("gy", -1))
+    corner = shape(GROUPS + 2, 8, LANES)
     strips, side, strip_up, strip_down = call(
-        strip_kernel,
-        [shape(GROUPS, 2, ROWS, LANES), shape(ROWS, LANES), shape(GROUPS + 2, 8, LANES), shape(GROUPS + 2, 8, LANES)],
+        strip_kernel, [shape(GROUPS, 2, ROWS, LANES), shape(ROWS, LANES), corner, corner]
     )(right, left, from_left, from_right)
     strip_below = lax.ppermute(strip_up, "gy", ring("gy", 1))
     strip_above = lax.ppermute(strip_down, "gy", ring("gy", -1))
-    block = shape(3, Z, ROWS, LANES)
+    block, part = shape(3, Z, ROWS, LANES), shape(8, 2 * LANES)
+    planes, sheets = (2, 3, Z, WRAP, LANES), (2, 3, 2, WRAP, LANES)
     field, adjoint, local_up, local_down = call(
         main_kernel,
-        [block, block, shape(8, 2 * LANES), shape(8, 2 * LANES)],
-        smem=3,
-        scratch=(
-            (2, 3, Z, WRAP, LANES),
-            (2, 3, Z, WRAP, LANES),
-            (Z, WRAP, LANES),
-            (Z, WRAP, LANES),
-            (2, 3, 2, WRAP, LANES),
-            (2, 3, 2, WRAP, LANES),
-            (2, WRAP, LANES),
-            (2, WRAP, LANES),
-            (48, 2 * LANES),
-        ),
-    )(
-        design_tiles, material_tiles, contrast, field_start, adjoint_start, source, adjoint_source, background, density,
-        above, below, strips, side, strip_above, strip_below,
-    )
+        [block, block, part, part],
+        scratch=[
+            room(*planes), room(*planes), room(*planes), room(Z, WRAP, LANES), room(Z, WRAP, LANES),
+            room(*sheets), room(*sheets), room(*sheets), room(2, WRAP, LANES), room(2, WRAP, LANES),
+            room(48, 2 * LANES),
+        ],
+    )(gains, *inner, above, below, strips, side, strip_above, strip_below)
     local_below = lax.ppermute(local_up, "gy", ring("gy", 1))
     local_above = lax.ppermute(local_down, "gy", ring("gy", -1))
-    gradient = call(gradient_kernel, shape(ROWS, LANES), scratch=((32, 2 * LANES),))(
+    gradient = call(gradient_kernel, shape(ROWS, LANES), scratch=[room(32, 2 * LANES)])(
         local_up, local_down, local_above, local_below
     )
     return (field, adjoint, gradient)

time: 55.9 us -> 59.2 us (1.059)
  the two profiles are of different devices: /device:TPU:6 before, /device:TPU:30 now
where the time goes in v2:
time: 59.2 us; the launch traced here: 58.8 us
  starting transfers between devices  28.1 us (47%)
  waiting for transfers between devices  15.8 us (27%)
  local copies, waits for them, and re-layouts  7.29 us (12%)
  Pallas kernels  6.83 us (12%)
  between operations  0.73 us (1%)
    ppermute x1, starting transfers between devices, on_device(): from_left = lax.ppermute(right, 'gx', ring('gx', 1))  14.7 us
    unnamed x30, local copies, waits for them, and re-layouts  7.29 us
    ppermute x1, waiting for transfers between devices, on_device(): from_right = lax.ppermute(left, 'gx', ring('gx', -1))  7.26 us
    pallas_call x5, Pallas kernels, run(): pl.pallas_call(kernel, out_shape=outs, in_specs=[pl.BlockSpec(memory_spac...  6.83 us
    ppermute x1, starting transfers between devices, on_device(): above = lax.ppermute(down, 'gy', ring('gy', -1))  5.09 us
    ppermute x1, waiting for transfers between devices, on_device(): strip_below = lax.ppermute(strip_up, 'gy', ring('gy', 1))  2.99 us
    ppermute x1, starting transfers between devices, on_device(): local_above = lax.ppermute(local_down, 'gy', ring('gy', -1))  2.95 us
    ppermute x1, starting transfers between devices, on_device(): from_right = lax.ppermute(left, 'gx', ring('gx', -1))  2.73 us
  transfers between devices with their start and end apart: 8, of which 5 were waited for; matrix products, arithmetic and copies ran while one was open for 0% of the time, Pallas kernels for 0%

profile of v2, /device:TPU:30, one launch (start us, length us, event | category | flops | bytes accessed | tf_op | source)
XLA Modules:
  0.0 58.8 jit_solution(12596160012589121754)
XLA Ops:
  0.6 0.0 copy-start
  0.6 0.9 %copy-done = f32[3,8,16,128]{3,2,1,0:T(8,128)S(1)} copy-done((f32[3,8,16,128]{3,2,1,0:T(8,128)S(1)}, f32[3,8,16,128]{3,2,1,0:T(8,128)}, u32[]{:S(2)}) %copy-start) | copy-done | bytes 196632
  1.6 0.0 copy-start.2
  1.6 0.9 %copy-done.2 = f32[3,8,16,128]{3,2,1,0:T(8,128)S(1)} copy-done((f32[3,8,16,128]{3,2,1,0:T(8,128)S(1)}, f32[3,8,16,128]{3,2,1,0:T(8,128)}, u32[]{:S(2)}) %copy-start.2) | copy-done | bytes 196632
  2.5 0.0 copy-start.4
  2.5 0.9 %copy-done.4 = f32[3,8,16,128]{3,2,1,0:T(8,128)S(1)} copy-done((f32[3,8,16,128]{3,2,1,0:T(8,128)S(1)}, f32[3,8,16,128]{3,2,1,0:T(8,128)}, u32[]{:S(2)}) %copy-start.4) | copy-done | bytes 196632
  3.4 0.0 copy-start.6
  3.4 0.9 %copy-done.6 = f32[3,8,16,128]{3,2,1,0:T(8,128)S(1)} copy-done((f32[3,8,16,128]{3,2,1,0:T(8,128)S(1)}, f32[3,8,16,128]{3,2,1,0:T(8,128)}, u32[]{:S(2)}) %copy-start.6) | copy-done | bytes 196632
  4.3 0.0 copy-start.8
  4.3 0.8 %copy-done.8 = f32[8,16,128]{2,1,0:T(8,128)S(1)} copy-done((f32[8,16,128]{2,1,0:T(8,128)S(1)}, f32[8,16,128]{2,1,0:T(8,128)}, u32[]{:S(2)}) %copy-start.8) | copy-done | bytes 65560
  5.2 0.0 copy-start.10
  5.2 0.7 %copy-done.10 = f32[16,128]{1,0:T(8,128)S(1)} copy-done((f32[16,128]{1,0:T(8,128)S(1)}, f32[16,128]{1,0:T(8,128)}, u32[]{:S(2)}) %copy-start.10) | copy-done | bytes 8216
  5.9 0.0 copy-start.12
  5.9 0.7 %copy-done.12 = s32[8,16]{1,0:T(8,128)S(1)} copy-done((s32[8,16]{1,0:T(8,128)S(1)}, s32[8,16]{1,0:T(8,128)}, u32[]{:S(2)}) %copy-start.12) | copy-done | bytes 536
  6.6 0.0 copy-start.13
  6.6 0.7 %copy-done.13 = s32[8,16]{1,0:T(8,128)S(1)} copy-done((s32[8,16]{1,0:T(8,128)S(1)}, s32[8,16]{1,0:T(8,128)}, u32[]{:S(2)}) %copy-start.13) | copy-done | bytes 536
  7.3 0.0 copy-start.14
  7.3 0.7 %copy-done.14 = f32[4]{0:T(128)S(1)} copy-done((f32[4]{0:T(128)S(1)}, f32[4]{0:T(128)}, u32[]{:S(2)}) %copy-start.14) | copy-done | bytes 40
  7.9 0.0 copy-start.1
  7.9 0.0 copy-start.3
  7.9 0.0 copy-start.5
  7.9 0.0 copy-start.7
  7.9 0.0 copy-start.9
  7.9 2.0 %shard_map.112 = (f32[14,16,128]{2,1,0:T(8,128)S(1)}, f32[14,16,128]{2,1,0:T(8,128)S(1)}, f32[3,24,128]{2,1,0:T(8,128)S(1)}) custom-call(s32[8,16]{1,0:T(8,128)S(1)} %copy-done.12, s32[8,16]{1,0:T(8,128)S(1)} %copy-done.13, f32[4]{0:T(128)S(1)} %copy-done.14, f32[3,8,16,128]{3,2,1,0:T(8,128)S(1)} %copy-done, f32[3,8,16,128]{3,2,1,0:T(8,128)S(1)} %copy-done.2, ...), custom_call_target="tpu_custom_call" | custom-call | tf_op jit(solution)/shard_map/pallas_call | solution.py:358
  10.0 14.7 %collective-permute-start = (f32[14,16,128]{2,1,0:T(8,128)S(1)}, f32[14,16,128]{2,1,0:T(8,128)S(1)}, u32[]{:S(2)}, u32[]{:S(2)}) collective-permute-start(f32[14,16,128]{2,1,0:T(8,128)S(1)} %get-tuple-element.17.own_right), channel_id=1, source_target_pairs={{0,64},{64,128},{128,192},{192,256},{256,320},{320,384},{384,448},... | collective-permute-start | bytes 344072 | tf_op jit(solution)/shard_map/ppermute | solution.py:386
  24.7 2.3 %collective-permute-done.sent.from_left = f32[14,16,128]{2,1,0:T(8,128)S(1)} collective-permute-done((f32[14,16,128]{2,1,0:T(8,128)S(1)}, f32[14,16,128]{2,1,0:T(8,128)S(1)}, u32[]{:S(2)}, u32[]{:S(2)}) %collective-permute-start) | collective-permute-done | bytes 114720 | tf_op jit(solution)/shard_map/ppermute | solution.py:386
  27.0 0.0 copy-done.1
  27.0 0.0 copy-done.3
  27.0 0.0 copy-done.5
  27.0 0.0 copy-done.7
  27.0 0.0 copy-done.9
  27.1 5.1 %collective-permute-start.1 = (f32[54,8,128]{2,1,0:T(8,128)S(1)}, f32[54,8,128]{2,1,0:T(8,128)S(1)}, u32[]{:S(2)}, u32[]{:S(2)}) collective-permute-start(f32[54,8,128]{2,1,0:T(8,128)S(1)} %get-tuple-element.18), channel_id=1, source_target_pairs={{0,63},{1,0},{2,1},{3,2},{4,3},{5,4},{6,5},{7,6},{8,7},{9,8},{10,9... | collective-permute-start | bytes 663560 | tf_op jit(solution)/shard_map/ppermute | solution.py:391
  32.2 0.0 collective-permute-start.2
  32.2 2.7 %collective-permute-start.3 = (f32[14,16,128]{2,1,0:T(8,128)S(1)}, f32[14,16,128]{2,1,0:T(8,128)S(1)}, u32[]{:S(2)}, u32[]{:S(2)}) collective-permute-start(f32[14,16,128]{2,1,0:T(8,128)S(1)} %get-tuple-element.20.own_left), channel_id=1, source_target_pairs={{0,960},{64,0},{128,64},{192,128},{256,192},{320,256},{384,320},{4... | collective-permute-start | bytes 344072 | tf_op jit(solution)/shard_map/ppermute | solution.py:387
  34.9 7.3 %collective-permute-done.3.from_right = f32[14,16,128]{2,1,0:T(8,128)S(1)} collective-permute-done((f32[14,16,128]{2,1,0:T(8,128)S(1)}, f32[14,16,128]{2,1,0:T(8,128)S(1)}, u32[]{:S(2)}, u32[]{:S(2)}) %collective-permute-start.3) | collective-permute-done | bytes 114720 | tf_op jit(solution)/shard_map/ppermute | solution.py:387
  42.2 0.1 shard_map.114
  42.3 0.0 copy-start.11
  42.3 2.6 %collective-permute-start.4 = (f32[15,8,128]{2,1,0:T(8,128)S(1)}, f32[15,8,128]{2,1,0:T(8,128)S(1)}, u32[]{:S(2)}, u32[]{:S(2)}) collective-permute-start(f32[15,8,128]{2,1,0:T(8,128)S(1)} %get-tuple-element.23), channel_id=1, source_target_pairs={{0,63},{1,0},{2,1},{3,2},{4,3},{5,4},{6,5},{7,6},{8,7},{9,8},{10,9... | collective-permute-start | bytes 184328 | tf_op jit(solution)/shard_map/ppermute | solution.py:397
  45.0 0.0 collective-permute-start.5
  45.0 1.9 %collective-permute-done.4.strip_above = f32[15,8,128]{2,1,0:T(8,128)S(1)} collective-permute-done((f32[15,8,128]{2,1,0:T(8,128)S(1)}, f32[15,8,128]{2,1,0:T(8,128)S(1)}, u32[]{:S(2)}, u32[]{:S(2)}) %collective-permute-start.4) | collective-permute-done | bytes 61472 | tf_op jit(solution)/shard_map/ppermute | solution.py:397
  46.8 3.0 %collective-permute-done.5.strip_below = f32[15,8,128]{2,1,0:T(8,128)S(1)} collective-permute-done((f32[15,8,128]{2,1,0:T(8,128)S(1)}, f32[15,8,128]{2,1,0:T(8,128)S(1)}, u32[]{:S(2)}, u32[]{:S(2)}) %collective-permute-start.5) | collective-permute-done | bytes 61472 | tf_op jit(solution)/shard_map/ppermute | solution.py:396
  49.8 0.0 collective-permute-done.1.above
  49.8 0.0 collective-permute-done.2.below
  49.8 0.0 copy-done.11
  49.8 3.8 %shard_map.115 = (f32[3,8,16,128]{3,2,1,0:T(8,128)}, f32[3,8,16,128]{3,2,1,0:T(8,128)}, f32[8,256]{1,0:T(8,128)S(1)}, f32[8,256]{1,0:T(8,128)S(1)}) custom-call(f32[3,24,128]{2,1,0:T(8,128)S(1)} %get-tuple-element.16.gains, f32[3,8,16,128]{3,2,1,0:T(8,128)S(1)} %copy-done.1, f32[3,8,16,128]{3,2,1,0:T(8,128)S(1)} %copy-done.3, ...), custom_call_target="tpu_custom_call" | custom-call | tf_op jit(solution)/shard_map/pallas_call | solution.py:358
  53.6 0.0 collective-permute-start.7
  53.6 3.0 %collective-permute-start.6 = (f32[8,256]{1,0:T(8,128)S(1)}, f32[8,256]{1,0:T(8,128)S(1)}, u32[]{:S(2)}, u32[]{:S(2)}) collective-permute-start(f32[8,256]{1,0:T(8,128)S(1)} %get-tuple-element.28.own_down), channel_id=1, source_target_pairs={{0,63},{1,0},{2,1},{3,2},{4,3},{5,4},{6,5},{7,6},{8,7},{9,8},{10,9... | collective-permute-start | bytes 24584 | tf_op jit(solution)/shard_map/ppermute | solution.py:410
  56.5 1.3 %collective-permute-done.7.below = f32[8,256]{1,0:T(8,128)S(1)} collective-permute-done((f32[8,256]{1,0:T(8,128)S(1)}, f32[8,256]{1,0:T(8,128)S(1)}, u32[]{:S(2)}, u32[]{:S(2)}) %collective-permute-start.7) | collective-permute-done | bytes 8224 | tf_op jit(solution)/shard_map/ppermute | solution.py:409
  57.9 0.0 collective-permute-done.6.above
  57.9 0.8 %shard_map.116 = f32[16,128]{1,0:T(8,128)} custom-call(f32[8,256]{1,0:T(8,128)S(1)} %get-tuple-element.27.own_up, f32[8,256]{1,0:T(8,128)S(1)} %get-tuple-element.28.own_down, f32[8,256]{1,0:T(8,128)S(1)} %collective-permute-done.6.above, f32[8,256]{1,0:T(8,128)S(1)} %collective-permute-done.7.below), custom_call_target="tpu_custom_call" | custom-call | tf_op jit(solution)/shard_map/pallas_call | solution.py:358
  (1 shorter events, 0.0 us)
Async XLA Ops:
  0.6 0.9 %copy-start = (f32[3,8,16,128]{3,2,1,0:T(8,128)S(1)}, f32[3,8,16,128]{3,2,1,0:T(8,128)}, u32[]{:S(2)}) copy-start(f32[3,8,16,128]{3,2,1,0:T(8,128)} %field.3) | copy-start | bytes 589828
  1.6 0.9 %copy-start.2 = (f32[3,8,16,128]{3,2,1,0:T(8,128)S(1)}, f32[3,8,16,128]{3,2,1,0:T(8,128)}, u32[]{:S(2)}) copy-start(f32[3,8,16,128]{3,2,1,0:T(8,128)} %adjoint.3) | copy-start | bytes 589828
  2.5 0.9 %copy-start.4 = (f32[3,8,16,128]{3,2,1,0:T(8,128)S(1)}, f32[3,8,16,128]{3,2,1,0:T(8,128)}, u32[]{:S(2)}) copy-start(f32[3,8,16,128]{3,2,1,0:T(8,128)} %source.3) | copy-start | bytes 589828
  3.4 0.9 %copy-start.6 = (f32[3,8,16,128]{3,2,1,0:T(8,128)S(1)}, f32[3,8,16,128]{3,2,1,0:T(8,128)}, u32[]{:S(2)}) copy-start(f32[3,8,16,128]{3,2,1,0:T(8,128)} %adjoint_source.3) | copy-start | bytes 589828
  4.3 0.8 %copy-start.8 = (f32[8,16,128]{2,1,0:T(8,128)S(1)}, f32[8,16,128]{2,1,0:T(8,128)}, u32[]{:S(2)}) copy-start(f32[8,16,128]{2,1,0:T(8,128)} %background.3) | copy-start | bytes 196612
  5.2 0.7 %copy-start.10 = (f32[16,128]{1,0:T(8,128)S(1)}, f32[16,128]{1,0:T(8,128)}, u32[]{:S(2)}) copy-start(f32[16,128]{1,0:T(8,128)} %density.3) | copy-start | bytes 24580
  5.9 0.7 %copy-start.12 = (s32[8,16]{1,0:T(8,128)S(1)}, s32[8,16]{1,0:T(8,128)}, u32[]{:S(2)}) copy-start(s32[8,16]{1,0:T(8,128)} %design_in.1) | copy-start | bytes 1540
  6.6 0.7 %copy-start.13 = (s32[8,16]{1,0:T(8,128)S(1)}, s32[8,16]{1,0:T(8,128)}, u32[]{:S(2)}) copy-start(s32[8,16]{1,0:T(8,128)} %material_in.1) | copy-start | bytes 1540
  7.3 0.7 %copy-start.14 = (f32[4]{0:T(128)S(1)}, f32[4]{0:T(128)}, u32[]{:S(2)}) copy-start(f32[4]{0:T(128)} %contrast_in.1) | copy-start | bytes 52
  7.9 19.1 %copy-start.1 = (f32[3,8,16,128]{3,2,1,0:T(8,128)S(1)}, f32[3,8,16,128]{3,2,1,0:T(8,128)}, u32[]{:S(2)}) copy-start(f32[3,8,16,128]{3,2,1,0:T(8,128)} %field.3) | copy-start | bytes 589828
  7.9 19.1 %copy-start.3 = (f32[3,8,16,128]{3,2,1,0:T(8,128)S(1)}, f32[3,8,16,128]{3,2,1,0:T(8,128)}, u32[]{:S(2)}) copy-start(f32[3,8,16,128]{3,2,1,0:T(8,128)} %adjoint.3) | copy-start | bytes 589828
  7.9 19.1 %copy-start.5 = (f32[3,8,16,128]{3,2,1,0:T(8,128)S(1)}, f32[3,8,16,128]{3,2,1,0:T(8,128)}, u32[]{:S(2)}) copy-start(f32[3,8,16,128]{3,2,1,0:T(8,128)} %source.3) | copy-start | bytes 589828
  7.9 19.1 %copy-start.7 = (f32[3,8,16,128]{3,2,1,0:T(8,128)S(1)}, f32[3,8,16,128]{3,2,1,0:T(8,128)}, u32[]{:S(2)}) copy-start(f32[3,8,16,128]{3,2,1,0:T(8,128)} %adjoint_source.3) | copy-start | bytes 589828
  7.9 19.1 %copy-start.9 = (f32[8,16,128]{2,1,0:T(8,128)S(1)}, f32[8,16,128]{2,1,0:T(8,128)}, u32[]{:S(2)}) copy-start(f32[8,16,128]{2,1,0:T(8,128)} %background.3) | copy-start | bytes 196612
  10.0 17.0 %collective-permute-start = (f32[14,16,128]{2,1,0:T(8,128)S(1)}, f32[14,16,128]{2,1,0:T(8,128)S(1)}, u32[]{:S(2)}, u32[]{:S(2)}) collective-permute-start(f32[14,16,128]{2,1,0:T(8,128)S(1)} %get-tuple-element.17.own_right), channel_id=1, source_target_pairs={{0,64},{64,128},{128,192},{192,256},{256,320},{320,384},{384,448},... | collective-permute-start | bytes 344072 | tf_op jit(solution)/shard_map/ppermute | solution.py:386
  27.1 22.7 %collective-permute-start.1 = (f32[54,8,128]{2,1,0:T(8,128)S(1)}, f32[54,8,128]{2,1,0:T(8,128)S(1)}, u32[]{:S(2)}, u32[]{:S(2)}) collective-permute-start(f32[54,8,128]{2,1,0:T(8,128)S(1)} %get-tuple-element.18), channel_id=1, source_target_pairs={{0,63},{1,0},{2,1},{3,2},{4,3},{5,4},{6,5},{7,6},{8,7},{9,8},{10,9... | collective-permute-start | bytes 663560 | tf_op jit(solution)/shard_map/ppermute | solution.py:391
  32.2 17.6 %collective-permute-start.2 = (f32[54,8,128]{2,1,0:T(8,128)S(1)}, f32[54,8,128]{2,1,0:T(8,128)S(1)}, u32[]{:S(2)}, u32[]{:S(2)}) collective-permute-start(f32[54,8,128]{2,1,0:T(8,128)S(1)} %get-tuple-element.19), channel_id=1, source_target_pairs={{0,1},{1,2},{2,3},{3,4},{4,5},{5,6},{6,7},{7,8},{8,9},{9,10},{10,1... | collective-permute-start | bytes 663560 | tf_op jit(solution)/shard_map/ppermute | solution.py:390
  32.2 10.0 %collective-permute-start.3 = (f32[14,16,128]{2,1,0:T(8,128)S(1)}, f32[14,16,128]{2,1,0:T(8,128)S(1)}, u32[]{:S(2)}, u32[]{:S(2)}) collective-permute-start(f32[14,16,128]{2,1,0:T(8,128)S(1)} %get-tuple-element.20.own_left), channel_id=1, source_target_pairs={{0,960},{64,0},{128,64},{192,128},{256,192},{320,256},{384,320},{4... | collective-permute-start | bytes 344072 | tf_op jit(solution)/shard_map/ppermute | solution.py:387
  42.3 7.5 %copy-start.11 = (f32[16,128]{1,0:T(8,128)S(1)}, f32[16,128]{1,0:T(8,128)}, u32[]{:S(2)}) copy-start(f32[16,128]{1,0:T(8,128)} %density.3) | copy-start | bytes 24580
  42.3 4.5 %collective-permute-start.4 = (f32[15,8,128]{2,1,0:T(8,128)S(1)}, f32[15,8,128]{2,1,0:T(8,128)S(1)}, u32[]{:S(2)}, u32[]{:S(2)}) collective-permute-start(f32[15,8,128]{2,1,0:T(8,128)S(1)} %get-tuple-element.23), channel_id=1, source_target_pairs={{0,63},{1,0},{2,1},{3,2},{4,3},{5,4},{6,5},{7,6},{8,7},{9,8},{10,9... | collective-permute-start | bytes 184328 | tf_op jit(solution)/shard_map/ppermute | solution.py:397
  45.0 4.9 %collective-permute-start.5 = (f32[15,8,128]{2,1,0:T(8,128)S(1)}, f32[15,8,128]{2,1,0:T(8,128)S(1)}, u32[]{:S(2)}, u32[]{:S(2)}) collective-permute-start(f32[15,8,128]{2,1,0:T(8,128)S(1)} %get-tuple-element.24), channel_id=1, source_target_pairs={{0,1},{1,2},{2,3},{3,4},{4,5},{5,6},{6,7},{7,8},{8,9},{9,10},{10,1... | collective-permute-start | bytes 184328 | tf_op jit(solution)/shard_map/ppermute | solution.py:396
  53.6 4.3 %collective-permute-start.7 = (f32[8,256]{1,0:T(8,128)S(1)}, f32[8,256]{1,0:T(8,128)S(1)}, u32[]{:S(2)}, u32[]{:S(2)}) collective-permute-start(f32[8,256]{1,0:T(8,128)S(1)} %get-tuple-element.27.own_up), channel_id=1, source_target_pairs={{0,1},{1,2},{2,3},{3,4},{4,5},{5,6},{6,7},{7,8},{8,9},{9,10},{10,1... | collective-permute-start | bytes 24584 | tf_op jit(solution)/shard_map/ppermute | solution.py:409
  53.6 4.3 %collective-permute-start.6 = (f32[8,256]{1,0:T(8,128)S(1)}, f32[8,256]{1,0:T(8,128)S(1)}, u32[]{:S(2)}, u32[]{:S(2)}) collective-permute-start(f32[8,256]{1,0:T(8,128)S(1)} %get-tuple-element.28.own_down), channel_id=1, source_target_pairs={{0,63},{1,0},{2,1},{3,2},{4,3},{5,4},{6,5},{7,6},{8,7},{9,8},{10,9... | collective-permute-start | bytes 24584 | tf_op jit(solution)/shard_map/ppermute | solution.py:410

commit v3 on v2

--- a/solution.py
+++ b/solution.py
@@ -62,10 +62,10 @@
     return result
 
 
-def edge_kernel(
+def pack_kernel(
     design_in, material_in, contrast_in, field_in, adjoint_in, source_in, adjoint_source_in, background_in, density_in,
-    right, left, gains,
-    design, material, contrast, field, adjoint, source, adjoint_source, background, density, done,
+    right, left, up, down, gains, field, adjoint, source, adjoint_source, background, density,
+    design, material, contrast, done,
 ):
     arrays = (
         (field_in, field), (adjoint_in, adjoint), (source_in, source), (adjoint_source_in, adjoint_source),
@@ -76,6 +76,7 @@
     for copy in copies:
         copy.start()
     lane = lanes_of(ROWS)
+    low = rows_of(8) < 4
     for g in range(GROUPS):
         if g % 3 == 0:
             copies[g // 3].wait()
@@ -93,10 +94,17 @@
                 to_left = jnp.where(chosen, here_left, to_left)
         right[g] = to_right
         left[g] = to_left
+        for pair in range(Z // 2):
+            k = g * (Z // 2) + pair
+            down[k] = jnp.where(low, planes[2 * pair, 0:8], turn(planes[2 * pair + 1, 0:8], 4, 0))
+            up[k] = jnp.where(low, turn(planes[2 * pair + 1, 8:16], 4, 0), planes[2 * pair, 8:16])
     for copy in copies[5:]:
         copy.wait()
     right[GROUPS] = density[...]
     left[GROUPS] = density[...]
+    for part in range(2):
+        up[4 * GROUPS + part] = density[8 * part : 8 * part + 8]
+        down[4 * GROUPS + part] = density[8 * part : 8 * part + 8]
 
     col, row = lax.axis_index("gx"), lax.axis_index("gy")
     row24 = rows_of(WRAP)
@@ -113,19 +121,6 @@
         up = gain_at(row * ROWS + ROWS, tile_x)
         down = gain_at(row * ROWS - HALO, tile_x)
         gains[k] = jnp.where(row24 < 16, here, jnp.where(row24 < 20, up, down))
-
-
-def rows_kernel(field, adjoint, source, adjoint_source, background, density, sent, up, down):
-    low = rows_of(8) < 4
-    for g in range(GROUPS):
-        planes = background if g == 12 else (field, adjoint, source, adjoint_source)[g // 3].at[g % 3]
-        for pair in range(Z // 2):
-            k = g * (Z // 2) + pair
-            down[k] = jnp.where(low, planes[2 * pair, 0:8], turn(planes[2 * pair + 1, 0:8], 4, 0))
-            up[k] = jnp.where(low, turn(planes[2 * pair + 1, 8:16], 4, 0), planes[2 * pair, 8:16])
-    for part in range(2):
-        up[4 * GROUPS + part] = density[8 * part : 8 * part + 8]
-        down[4 * GROUPS + part] = density[8 * part : 8 * part + 8]
 
 
 def strip_kernel(own_right, own_left, from_left, from_right, strips, side, up, down):
@@ -374,19 +369,15 @@
 def on_device(background, density, design_tiles, material_tiles, contrast, source, adjoint_source, field_start, adjoint_start):
     inner = (field_start, adjoint_start, source, adjoint_source, background, density)
     tiles = (design_tiles, material_tiles, contrast)
-    edges = shape(GROUPS + 1, ROWS, LANES)
-    right, left, gains = call(
-        edge_kernel,
-        [edges, edges, shape(3, WRAP, LANES)],
-        space=pl.ANY,
-        scratch=[pltpu.SMEM(a.shape, a.dtype) for a in tiles]
-        + [room(*a.shape) for a in inner]
-        + [pltpu.SemaphoreType.DMA((9,))],
-    )(*tiles, *inner)
+    edges, rows = shape(GROUPS + 1, ROWS, LANES), shape(4 * GROUPS + 2, 8, LANES)
+    right, left, up, down, gains, *inner = call(
+        pack_kernel,
+        [edges, edges, rows, rows, shape(3, WRAP, LANES)] + [shape(*a.shape) for a in inner],
+        space=pltpu.HBM,
+        scratch=[pltpu.SMEM(a.shape, a.dtype) for a in tiles] + [pltpu.SemaphoreType.DMA((9,))],
+    )(*[pltpu.with_memory_space_constraint(a, pltpu.HBM) for a in (*tiles, *inner)])
     from_left = lax.ppermute(right, "gx", ring("gx", 1))
     from_right = lax.ppermute(left, "gx", ring("gx", -1))
-    rows = shape(4 * GROUPS + 2, 8, LANES)
-    up, down = call(rows_kernel, [rows, rows])(*inner, from_left)
     below = lax.ppermute(up, "gy", ring("gy", 1))
     above = lax.ppermute(down, "gy", ring("gy", -1))
     corner = shape(GROUPS + 2, 8, LANES)

time: 59.2 us -> 46.8 us (0.79)
  the two profiles are of different devices: /device:TPU:30 before, /device:TPU:6 now
where the time goes in v3:
time: 46.8 us; the launch traced here: 46.6 us
  starting transfers between devices  26.7 us (57%)
  waiting for transfers between devices  12.6 us (27%)
  Pallas kernels  6.61 us (14%)
  between operations  0.67 us (1%)
    ppermute x1, starting transfers between devices, on_device(): above = lax.ppermute(down, 'gy', ring('gy', -1))  16.2 us
    pallas_call x4, Pallas kernels, run(): pl.pallas_call(kernel, out_shape=outs, in_specs=[pl.BlockSpec(memory_spac...  6.61 us
    ppermute x1, waiting for transfers between devices, on_device(): from_right = lax.ppermute(left, 'gx', ring('gx', -1))  5.52 us
    ppermute x1, starting transfers between devices, on_device(): from_left = lax.ppermute(right, 'gx', ring('gx', 1))  3.39 us
    ppermute x1, waiting for transfers between devices, on_device(): strip_below = lax.ppermute(strip_up, 'gy', ring('gy', 1))  2.99 us
    ppermute x1, starting transfers between devices, on_device(): local_above = lax.ppermute(local_down, 'gy', ring('gy', -1))  2.95 us
    ppermute x1, starting transfers between devices, on_device(): from_right = lax.ppermute(left, 'gx', ring('gx', -1))  2.44 us
    ppermute x1, waiting for transfers between devices, on_device(): strip_above = lax.ppermute(strip_down, 'gy', ring('gy', -1))  1.86 us
  transfers between devices with their start and end apart: 8, of which 5 were waited for; matrix products, arithmetic and copies ran while one was open for 0% of the time, Pallas kernels for 0%

profile of v3, /device:TPU:6, one launch (start us, length us, event | category | flops | bytes accessed | tf_op | source)
XLA Modules:
  0.0 46.6 jit_solution(14352666095873729601)
XLA Ops:
  0.6 1.9 %shard_map.112 = (f32[14,16,128]{2,1,0:T(8,128)S(1)}, f32[14,16,128]{2,1,0:T(8,128)S(1)}, f32[54,8,128]{2,1,0:T(8,128)S(1)}, f32[54,8,128]{2,1,0:T(8,128)S(1)}, ...) custom-call(s32[8,16]{1,0:T(8,128)} %design_in.1, ...), custom_call_target="tpu_custom_call" | custom-call | tf_op jit(solution)/shard_map/pallas_call | solution.py:353
  2.5 16.2 %collective-permute-start = (f32[54,8,128]{2,1,0:T(8,128)S(1)}, f32[54,8,128]{2,1,0:T(8,128)S(1)}, u32[]{:S(2)}, u32[]{:S(2)}) collective-permute-start(f32[54,8,128]{2,1,0:T(8,128)S(1)} %get-tuple-element.29), channel_id=1, source_target_pairs={{0,63},{1,0},{2,1},{3,2},{4,3},{5,4},{6,5},{7,6},{8,7},{9,8},{10,9... | collective-permute-start | bytes 663560 | tf_op jit(solution)/shard_map/ppermute | solution.py:382
  18.7 0.0 collective-permute-start.1
  18.7 3.4 %collective-permute-start.2 = (f32[14,16,128]{2,1,0:T(8,128)S(1)}, f32[14,16,128]{2,1,0:T(8,128)S(1)}, u32[]{:S(2)}, u32[]{:S(2)}) collective-permute-start(f32[14,16,128]{2,1,0:T(8,128)S(1)} %get-tuple-element.31.own_right), channel_id=1, source_target_pairs={{0,64},{64,128},{128,192},{192,256},{256,320},{320,384},{384,448},... | collective-permute-start | bytes 344072 | tf_op jit(solution)/shard_map/ppermute | solution.py:379
  22.1 2.4 %collective-permute-start.3 = (f32[14,16,128]{2,1,0:T(8,128)S(1)}, f32[14,16,128]{2,1,0:T(8,128)S(1)}, u32[]{:S(2)}, u32[]{:S(2)}) collective-permute-start(f32[14,16,128]{2,1,0:T(8,128)S(1)} %get-tuple-element.32.own_left), channel_id=1, source_target_pairs={{0,960},{64,0},{128,64},{192,128},{256,192},{320,256},{384,320},{4... | collective-permute-start | bytes 344072 | tf_op jit(solution)/shard_map/ppermute | solution.py:380
  24.6 0.8 %collective-permute-done.2.from_left = f32[14,16,128]{2,1,0:T(8,128)S(1)} collective-permute-done((f32[14,16,128]{2,1,0:T(8,128)S(1)}, f32[14,16,128]{2,1,0:T(8,128)S(1)}, u32[]{:S(2)}, u32[]{:S(2)}) %collective-permute-start.2) | collective-permute-done | bytes 114720 | tf_op jit(solution)/shard_map/ppermute | solution.py:379
  25.4 5.5 %collective-permute-done.3.from_right = f32[14,16,128]{2,1,0:T(8,128)S(1)} collective-permute-done((f32[14,16,128]{2,1,0:T(8,128)S(1)}, f32[14,16,128]{2,1,0:T(8,128)S(1)}, u32[]{:S(2)}, u32[]{:S(2)}) %collective-permute-start.3) | collective-permute-done | bytes 114720 | tf_op jit(solution)/shard_map/ppermute | solution.py:380
  30.9 0.1 shard_map.113
  31.1 1.7 %collective-permute-start.4 = (f32[15,8,128]{2,1,0:T(8,128)S(1)}, f32[15,8,128]{2,1,0:T(8,128)S(1)}, u32[]{:S(2)}, u32[]{:S(2)}) collective-permute-start(f32[15,8,128]{2,1,0:T(8,128)S(1)} %get-tuple-element.35), channel_id=1, source_target_pairs={{0,63},{1,0},{2,1},{3,2},{4,3},{5,4},{6,5},{7,6},{8,7},{9,8},{10,9... | collective-permute-start | bytes 184328 | tf_op jit(solution)/shard_map/ppermute | solution.py:388
  32.8 0.0 collective-permute-start.5
  32.8 1.9 %collective-permute-done.4.strip_above = f32[15,8,128]{2,1,0:T(8,128)S(1)} collective-permute-done((f32[15,8,128]{2,1,0:T(8,128)S(1)}, f32[15,8,128]{2,1,0:T(8,128)S(1)}, u32[]{:S(2)}, u32[]{:S(2)}) %collective-permute-start.4) | collective-permute-done | bytes 61472 | tf_op jit(solution)/shard_map/ppermute | solution.py:388
  34.7 3.0 %collective-permute-done.5.strip_below = f32[15,8,128]{2,1,0:T(8,128)S(1)} collective-permute-done((f32[15,8,128]{2,1,0:T(8,128)S(1)}, f32[15,8,128]{2,1,0:T(8,128)S(1)}, u32[]{:S(2)}, u32[]{:S(2)}) %collective-permute-start.5) | collective-permute-done | bytes 61472 | tf_op jit(solution)/shard_map/ppermute | solution.py:387
  37.7 0.0 collective-permute-done.above
  37.7 0.0 collective-permute-done.1.below
  37.7 3.8 %shard_map.114 = (f32[3,8,16,128]{3,2,1,0:T(8,128)}, f32[3,8,16,128]{3,2,1,0:T(8,128)}, f32[8,256]{1,0:T(8,128)S(1)}, f32[8,256]{1,0:T(8,128)S(1)}) custom-call(f32[3,24,128]{2,1,0:T(8,128)S(1)} %get-tuple-element.22.gains, f32[3,8,16,128]{3,2,1,0:T(8,128)S(1)} %get-tuple-element.23.field, f32[3,8,16,128]{3,2,1,0:T(8,128)S(1)} %get-tuple-element.24.adjoint, ...), custom_call_target="tpu_custom_call" | custom-call | tf_op jit(solution)/shard_map/pallas_call | solution.py:353
  41.4 0.0 collective-permute-start.7
  41.4 3.0 %collective-permute-start.6 = (f32[8,256]{1,0:T(8,128)S(1)}, f32[8,256]{1,0:T(8,128)S(1)}, u32[]{:S(2)}, u32[]{:S(2)}) collective-permute-start(f32[8,256]{1,0:T(8,128)S(1)} %get-tuple-element.40.own_down), channel_id=1, source_target_pairs={{0,63},{1,0},{2,1},{3,2},{4,3},{5,4},{6,5},{7,6},{8,7},{9,8},{10,9... | collective-permute-start | bytes 24584 | tf_op jit(solution)/shard_map/ppermute | solution.py:401
  44.4 1.3 %collective-permute-done.7.below = f32[8,256]{1,0:T(8,128)S(1)} collective-permute-done((f32[8,256]{1,0:T(8,128)S(1)}, f32[8,256]{1,0:T(8,128)S(1)}, u32[]{:S(2)}, u32[]{:S(2)}) %collective-permute-start.7) | collective-permute-done | bytes 8224 | tf_op jit(solution)/shard_map/ppermute | solution.py:400
  45.7 0.0 collective-permute-done.6.above
  45.8 0.8 %shard_map.115 = f32[16,128]{1,0:T(8,128)} custom-call(f32[8,256]{1,0:T(8,128)S(1)} %get-tuple-element.39.own_up, f32[8,256]{1,0:T(8,128)S(1)} %get-tuple-element.40.own_down, f32[8,256]{1,0:T(8,128)S(1)} %collective-permute-done.6.above, f32[8,256]{1,0:T(8,128)S(1)} %collective-permute-done.7.below), custom_call_target="tpu_custom_call" | custom-call | tf_op jit(solution)/shard_map/pallas_call | solution.py:353
Async XLA Ops:
  2.5 35.1 %collective-permute-start = (f32[54,8,128]{2,1,0:T(8,128)S(1)}, f32[54,8,128]{2,1,0:T(8,128)S(1)}, u32[]{:S(2)}, u32[]{:S(2)}) collective-permute-start(f32[54,8,128]{2,1,0:T(8,128)S(1)} %get-tuple-element.29), channel_id=1, source_target_pairs={{0,63},{1,0},{2,1},{3,2},{4,3},{5,4},{6,5},{7,6},{8,7},{9,8},{10,9... | collective-permute-start | bytes 663560 | tf_op jit(solution)/shard_map/ppermute | solution.py:382
  18.7 18.9 %collective-permute-start.1 = (f32[54,8,128]{2,1,0:T(8,128)S(1)}, f32[54,8,128]{2,1,0:T(8,128)S(1)}, u32[]{:S(2)}, u32[]{:S(2)}) collective-permute-start(f32[54,8,128]{2,1,0:T(8,128)S(1)} %get-tuple-element.30), channel_id=1, source_target_pairs={{0,1},{1,2},{2,3},{3,4},{4,5},{5,6},{6,7},{7,8},{8,9},{9,10},{10,1... | collective-permute-start | bytes 663560 | tf_op jit(solution)/shard_map/ppermute | solution.py:381
  18.7 6.7 %collective-permute-start.2 = (f32[14,16,128]{2,1,0:T(8,128)S(1)}, f32[14,16,128]{2,1,0:T(8,128)S(1)}, u32[]{:S(2)}, u32[]{:S(2)}) collective-permute-start(f32[14,16,128]{2,1,0:T(8,128)S(1)} %get-tuple-element.31.own_right), channel_id=1, source_target_pairs={{0,64},{64,128},{128,192},{192,256},{256,320},{320,384},{384,448},... | collective-permute-start | bytes 344072 | tf_op jit(solution)/shard_map/ppermute | solution.py:379
  22.1 8.8 %collective-permute-start.3 = (f32[14,16,128]{2,1,0:T(8,128)S(1)}, f32[14,16,128]{2,1,0:T(8,128)S(1)}, u32[]{:S(2)}, u32[]{:S(2)}) collective-permute-start(f32[14,16,128]{2,1,0:T(8,128)S(1)} %get-tuple-element.32.own_left), channel_id=1, source_target_pairs={{0,960},{64,0},{128,64},{192,128},{256,192},{320,256},{384,320},{4... | collective-permute-start | bytes 344072 | tf_op jit(solution)/shard_map/ppermute | solution.py:380
  31.1 3.6 %collective-permute-start.4 = (f32[15,8,128]{2,1,0:T(8,128)S(1)}, f32[15,8,128]{2,1,0:T(8,128)S(1)}, u32[]{:S(2)}, u32[]{:S(2)}) collective-permute-start(f32[15,8,128]{2,1,0:T(8,128)S(1)} %get-tuple-element.35), channel_id=1, source_target_pairs={{0,63},{1,0},{2,1},{3,2},{4,3},{5,4},{6,5},{7,6},{8,7},{9,8},{10,9... | collective-permute-start | bytes 184328 | tf_op jit(solution)/shard_map/ppermute | solution.py:388
  32.8 4.9 %collective-permute-start.5 = (f32[15,8,128]{2,1,0:T(8,128)S(1)}, f32[15,8,128]{2,1,0:T(8,128)S(1)}, u32[]{:S(2)}, u32[]{:S(2)}) collective-permute-start(f32[15,8,128]{2,1,0:T(8,128)S(1)} %get-tuple-element.36), channel_id=1, source_target_pairs={{0,1},{1,2},{2,3},{3,4},{4,5},{5,6},{6,7},{7,8},{8,9},{9,10},{10,1... | collective-permute-start | bytes 184328 | tf_op jit(solution)/shard_map/ppermute | solution.py:387
  41.4 4.3 %collective-permute-start.7 = (f32[8,256]{1,0:T(8,128)S(1)}, f32[8,256]{1,0:T(8,128)S(1)}, u32[]{:S(2)}, u32[]{:S(2)}) collective-permute-start(f32[8,256]{1,0:T(8,128)S(1)} %get-tuple-element.39.own_up), channel_id=1, source_target_pairs={{0,1},{1,2},{2,3},{3,4},{4,5},{5,6},{6,7},{7,8},{8,9},{9,10},{10,1... | collective-permute-start | bytes 24584 | tf_op jit(solution)/shard_map/ppermute | solution.py:400
  41.4 4.3 %collective-permute-start.6 = (f32[8,256]{1,0:T(8,128)S(1)}, f32[8,256]{1,0:T(8,128)S(1)}, u32[]{:S(2)}, u32[]{:S(2)}) collective-permute-start(f32[8,256]{1,0:T(8,128)S(1)} %get-tuple-element.40.own_down), channel_id=1, source_target_pairs={{0,63},{1,0},{2,1},{3,2},{4,3},{5,4},{6,5},{7,6},{8,7},{9,8},{10,9... | collective-permute-start | bytes 24584 | tf_op jit(solution)/shard_map/ppermute | solution.py:401

commit v4 on v3

--- a/solution.py
+++ b/solution.py
@@ -64,7 +64,7 @@
 
 def pack_kernel(
     design_in, material_in, contrast_in, field_in, adjoint_in, source_in, adjoint_source_in, background_in, density_in,
-    right, left, up, down, gains, field, adjoint, source, adjoint_source, background, density,
+    first, second, own_right, own_left, up, down, gains, field, adjoint, source, adjoint_source, background, density,
     design, material, contrast, done,
 ):
     arrays = (
@@ -76,6 +76,7 @@
     for copy in copies:
         copy.start()
     lane = lanes_of(ROWS)
+    rightward = lax.axis_index("gx") % 2 == 0
     low = rows_of(8) < 4
     for g in range(GROUPS):
         if g % 3 == 0:
@@ -92,16 +93,18 @@
                 chosen = lane >= 16 * z
                 to_right = jnp.where(chosen, here_right, to_right)
                 to_left = jnp.where(chosen, here_left, to_left)
-        right[g] = to_right
-        left[g] = to_left
+        own_right[g] = to_right
+        own_left[g] = to_left
+        first[g] = jnp.where(rightward, to_right, to_left)
+        second[g] = jnp.where(rightward, to_left, to_right)
         for pair in range(Z // 2):
             k = g * (Z // 2) + pair
             down[k] = jnp.where(low, planes[2 * pair, 0:8], turn(planes[2 * pair + 1, 0:8], 4, 0))
             up[k] = jnp.where(low, turn(planes[2 * pair + 1, 8:16], 4, 0), planes[2 * pair, 8:16])
     for copy in copies[5:]:
         copy.wait()
-    right[GROUPS] = density[...]
-    left[GROUPS] = density[...]
+    first[GROUPS] = density[...]
+    second[GROUPS] = density[...]
     for part in range(2):
         up[4 * GROUPS + part] = density[8 * part : 8 * part + 8]
         down[4 * GROUPS + part] = density[8 * part : 8 * part + 8]
@@ -123,25 +126,32 @@
         gains[k] = jnp.where(row24 < 16, here, jnp.where(row24 < 20, up, down))
 
 
-def strip_kernel(own_right, own_left, from_left, from_right, strips, side, up, down):
+def strip_kernel(own_right, own_left, first_got, second_got, strips, side, up, down):
     col = lax.axis_index("gx")
+    rightward = col % 2 == 0
     first, last = col == 0, col == lax.axis_size("gx") - 1
     lane = lanes_of(ROWS)
     within = lane % 16
     half = lane % 32 < 16
     low = rows_of(8) < 4
+
+    def sides(g):
+        from_right = jnp.where(rightward, first_got[g], second_got[g])
+        from_left = jnp.where(rightward, second_got[g], first_got[g])
+        return jnp.where(last, 0.0, from_right), jnp.where(first, 0.0, from_left)
+
     for g in range(GROUPS):
-        here_right = jnp.where(within >= HALO, jnp.where(last, 0.0, from_right[g]), own_left[g])
-        here_left = jnp.where(within < 12, jnp.where(first, 0.0, from_left[g]), own_right[g])
+        from_right, from_left = sides(g)
+        here_right = jnp.where(within >= HALO, from_right, own_left[g])
+        here_left = jnp.where(within < 12, from_left, own_right[g])
         even = jnp.where(half, here_right, turn(here_left, 16, 1))
         odd = jnp.where(half, turn(here_right, -16, 1), here_left)
         strips[g, 0] = even
         strips[g, 1] = odd
         down[g] = jnp.where(low, even[0:8], turn(odd[0:8], 4, 0))
         up[g] = jnp.where(low, turn(odd[8:16], 4, 0), even[8:16])
-    beside = jnp.where(
-        lane < 64, jnp.where(last, 0.0, from_right[GROUPS]), jnp.where(first, 0.0, from_left[GROUPS])
-    )
+    from_right, from_left = sides(GROUPS)
+    beside = jnp.where(lane < 64, from_right, from_left)
     side[...] = beside
     for part in range(2):
         up[GROUPS + part] = beside[8 * part : 8 * part + 8]
@@ -339,6 +349,12 @@
     gradient[...] = cone(lambda a: wide[8 + a : 24 + a], ROWS)[:, :LANES]
 
 
+def swaps(axis, start):
+    size = lax.axis_size(axis)
+    pairs = [(i, i + 1) for i in range(start, size - 1, 2)]
+    return sorted(pairs + [(j, i) for i, j in pairs])
+
+
 def ring(axis, step):
     size = lax.axis_size(axis)
     return [(i, (i + step) % size) for i in range(size)]
@@ -370,20 +386,20 @@
     inner = (field_start, adjoint_start, source, adjoint_source, background, density)
     tiles = (design_tiles, material_tiles, contrast)
     edges, rows = shape(GROUPS + 1, ROWS, LANES), shape(4 * GROUPS + 2, 8, LANES)
-    right, left, up, down, gains, *inner = call(
+    first, second, own_right, own_left, up, down, gains, *inner = call(
         pack_kernel,
-        [edges, edges, rows, rows, shape(3, WRAP, LANES)] + [shape(*a.shape) for a in inner],
+        [edges, edges, edges, edges, rows, rows, shape(3, WRAP, LANES)] + [shape(*a.shape) for a in inner],
         space=pltpu.HBM,
         scratch=[pltpu.SMEM(a.shape, a.dtype) for a in tiles] + [pltpu.SemaphoreType.DMA((9,))],
     )(*[pltpu.with_memory_space_constraint(a, pltpu.HBM) for a in (*tiles, *inner)])
-    from_left = lax.ppermute(right, "gx", ring("gx", 1))
-    from_right = lax.ppermute(left, "gx", ring("gx", -1))
+    first_got = lax.ppermute(first, "gx", swaps("gx", 0))
+    second_got = lax.ppermute(second, "gx", swaps("gx", 1))
     below = lax.ppermute(up, "gy", ring("gy", 1))
     above = lax.ppermute(down, "gy", ring("gy", -1))
     corner = shape(GROUPS + 2, 8, LANES)
     strips, side, strip_up, strip_down = call(
         strip_kernel, [shape(GROUPS, 2, ROWS, LANES), shape(ROWS, LANES), corner, corner]
-    )(right, left, from_left, from_right)
+    )(own_right, own_left, first_got, second_got)
     strip_below = lax.ppermute(strip_up, "gy", ring("gy", 1))
     strip_above = lax.ppermute(strip_down, "gy", ring("gy", -1))
     block, part = shape(3, Z, ROWS, LANES), shape(8, 2 * LANES)

time: 46.8 us -> 46.8 us (level)
  the two profiles are of different devices: /device:TPU:6 before, /device:TPU:24 now
where the time goes in v4:
time: 46.8 us; the launch traced here: 46.6 us
  starting transfers between devices  28.5 us (61%)
  waiting for transfers between devices  10.8 us (23%)
  Pallas kernels  6.61 us (14%)
  between operations  0.68 us (1%)
    ppermute x1, starting transfers between devices, on_device(): above = lax.ppermute(down, 'gy', ring('gy', -1))  16.2 us
    pallas_call x4, Pallas kernels, run(): pl.pallas_call(kernel, out_shape=outs, in_specs=[pl.BlockSpec(memory_spac...  6.61 us
    ppermute x1, waiting for transfers between devices, on_device(): second_got = lax.ppermute(second, 'gx', swaps('gx', 1))  4.59 us
    ppermute x1, starting transfers between devices, on_device(): second_got = lax.ppermute(second, 'gx', swaps('gx', 1))  4.18 us
    ppermute x1, starting transfers between devices, on_device(): first_got = lax.ppermute(first, 'gx', swaps('gx', 0))  3.39 us
    ppermute x1, waiting for transfers between devices, on_device(): strip_below = lax.ppermute(strip_up, 'gy', ring('gy', 1))  2.99 us
    ppermute x1, starting transfers between devices, on_device(): local_above = lax.ppermute(local_down, 'gy', ring('gy', -1))  2.95 us
    ppermute x1, waiting for transfers between devices, on_device(): strip_above = lax.ppermute(strip_down, 'gy', ring('gy', -1))  1.86 us
  transfers between devices with their start and end apart: 8, of which 4 were waited for; matrix products, arithmetic and copies ran while one was open for 0% of the time, Pallas kernels for 0%

profile of v4, /device:TPU:24, one launch (start us, length us, event | category | flops | bytes accessed | tf_op | source)
XLA Modules:
  0.0 46.6 jit_solution(1476437491986128570)
XLA Ops:
  0.6 1.9 %shard_map.112 = (f32[14,16,128]{2,1,0:T(8,128)S(1)}, f32[14,16,128]{2,1,0:T(8,128)S(1)}, f32[14,16,128]{2,1,0:T(8,128)S(1)}, f32[14,16,128]{2,1,0:T(8,128)S(1)}...) custom-call(s32[8,16]{1,0:T(8,128)} %design_in.1, ...), custom_call_target="tpu_custom_call" | custom-call | tf_op jit(solution)/shard_map/pallas_call | solution.py:369
  2.5 16.2 %collective-permute-start = (f32[54,8,128]{2,1,0:T(8,128)S(1)}, f32[54,8,128]{2,1,0:T(8,128)S(1)}, u32[]{:S(2)}, u32[]{:S(2)}) collective-permute-start(f32[54,8,128]{2,1,0:T(8,128)S(1)} %get-tuple-element.31), channel_id=1, source_target_pairs={{0,63},{1,0},{2,1},{3,2},{4,3},{5,4},{6,5},{7,6},{8,7},{9,8},{10,9... | collective-permute-start | bytes 663560 | tf_op jit(solution)/shard_map/ppermute | solution.py:398
  18.7 0.0 collective-permute-start.1
  18.7 3.4 %collective-permute-start.2 = (f32[14,16,128]{2,1,0:T(8,128)S(1)}, f32[14,16,128]{2,1,0:T(8,128)S(1)}, u32[]{:S(2)}, u32[]{:S(2)}) collective-permute-start(f32[14,16,128]{2,1,0:T(8,128)S(1)} %get-tuple-element.35), channel_id=1, source_target_pairs={{0,64},{64,0},{128,192},{192,128},{256,320},{320,256},{384,448},{4... | collective-permute-start | bytes 344072 | tf_op jit(solution)/shard_map/ppermute | solution.py:395
  22.1 4.2 %collective-permute-start.3 = (f32[14,16,128]{2,1,0:T(8,128)S(1)}, f32[14,16,128]{2,1,0:T(8,128)S(1)}, u32[]{:S(2)}, u32[]{:S(2)}) collective-permute-start(f32[14,16,128]{2,1,0:T(8,128)S(1)} %get-tuple-element.36), channel_id=1, source_target_pairs={{64,128},{128,64},{192,256},{256,192},{320,384},{384,320},{448,512... | collective-permute-start | bytes 344072 | tf_op jit(solution)/shard_map/ppermute | solution.py:396
  26.3 0.0 collective-permute-done.2.first_got
  26.3 4.6 %collective-permute-done.3.second_got = f32[14,16,128]{2,1,0:T(8,128)S(1)} collective-permute-done((f32[14,16,128]{2,1,0:T(8,128)S(1)}, f32[14,16,128]{2,1,0:T(8,128)S(1)}, u32[]{:S(2)}, u32[]{:S(2)}) %collective-permute-start.3) | collective-permute-done | bytes 114720 | tf_op jit(solution)/shard_map/ppermute | solution.py:396
  30.9 0.1 shard_map.113
  31.1 1.7 %collective-permute-start.4 = (f32[15,8,128]{2,1,0:T(8,128)S(1)}, f32[15,8,128]{2,1,0:T(8,128)S(1)}, u32[]{:S(2)}, u32[]{:S(2)}) collective-permute-start(f32[15,8,128]{2,1,0:T(8,128)S(1)} %get-tuple-element.39), channel_id=1, source_target_pairs={{0,63},{1,0},{2,1},{3,2},{4,3},{5,4},{6,5},{7,6},{8,7},{9,8},{10,9... | collective-permute-start | bytes 184328 | tf_op jit(solution)/shard_map/ppermute | solution.py:404
  32.8 0.0 collective-permute-start.5
  32.8 1.9 %collective-permute-done.4.strip_above = f32[15,8,128]{2,1,0:T(8,128)S(1)} collective-permute-done((f32[15,8,128]{2,1,0:T(8,128)S(1)}, f32[15,8,128]{2,1,0:T(8,128)S(1)}, u32[]{:S(2)}, u32[]{:S(2)}) %collective-permute-start.4) | collective-permute-done | bytes 61472 | tf_op jit(solution)/shard_map/ppermute | solution.py:404
  34.7 3.0 %collective-permute-done.5.strip_below = f32[15,8,128]{2,1,0:T(8,128)S(1)} collective-permute-done((f32[15,8,128]{2,1,0:T(8,128)S(1)}, f32[15,8,128]{2,1,0:T(8,128)S(1)}, u32[]{:S(2)}, u32[]{:S(2)}) %collective-permute-start.5) | collective-permute-done | bytes 61472 | tf_op jit(solution)/shard_map/ppermute | solution.py:403
  37.7 0.0 collective-permute-done.above
  37.7 0.0 collective-permute-done.1.below
  37.7 3.8 %shard_map.114 = (f32[3,8,16,128]{3,2,1,0:T(8,128)}, f32[3,8,16,128]{3,2,1,0:T(8,128)}, f32[8,256]{1,0:T(8,128)S(1)}, f32[8,256]{1,0:T(8,128)S(1)}) custom-call(f32[3,24,128]{2,1,0:T(8,128)S(1)} %get-tuple-element.24.gains, f32[3,8,16,128]{3,2,1,0:T(8,128)S(1)} %get-tuple-element.25.field, f32[3,8,16,128]{3,2,1,0:T(8,128)S(1)} %get-tuple-element.26.adjoint, ...), custom_call_target="tpu_custom_call" | custom-call | tf_op jit(solution)/shard_map/pallas_call | solution.py:369
  41.4 0.0 collective-permute-start.7
  41.4 3.0 %collective-permute-start.6 = (f32[8,256]{1,0:T(8,128)S(1)}, f32[8,256]{1,0:T(8,128)S(1)}, u32[]{:S(2)}, u32[]{:S(2)}) collective-permute-start(f32[8,256]{1,0:T(8,128)S(1)} %get-tuple-element.44.own_down), channel_id=1, source_target_pairs={{0,63},{1,0},{2,1},{3,2},{4,3},{5,4},{6,5},{7,6},{8,7},{9,8},{10,9... | collective-permute-start | bytes 24584 | tf_op jit(solution)/shard_map/ppermute | solution.py:417
  44.4 1.3 %collective-permute-done.7.below = f32[8,256]{1,0:T(8,128)S(1)} collective-permute-done((f32[8,256]{1,0:T(8,128)S(1)}, f32[8,256]{1,0:T(8,128)S(1)}, u32[]{:S(2)}, u32[]{:S(2)}) %collective-permute-start.7) | collective-permute-done | bytes 8224 | tf_op jit(solution)/shard_map/ppermute | solution.py:416
  45.7 0.0 collective-permute-done.6.above
  45.8 0.8 %shard_map.115 = f32[16,128]{1,0:T(8,128)} custom-call(f32[8,256]{1,0:T(8,128)S(1)} %get-tuple-element.43.own_up, f32[8,256]{1,0:T(8,128)S(1)} %get-tuple-element.44.own_down, f32[8,256]{1,0:T(8,128)S(1)} %collective-permute-done.6.above, f32[8,256]{1,0:T(8,128)S(1)} %collective-permute-done.7.below), custom_call_target="tpu_custom_call" | custom-call | tf_op jit(solution)/shard_map/pallas_call | solution.py:369
Async XLA Ops:
  2.5 35.2 %collective-permute-start = (f32[54,8,128]{2,1,0:T(8,128)S(1)}, f32[54,8,128]{2,1,0:T(8,128)S(1)}, u32[]{:S(2)}, u32[]{:S(2)}) collective-permute-start(f32[54,8,128]{2,1,0:T(8,128)S(1)} %get-tuple-element.31), channel_id=1, source_target_pairs={{0,63},{1,0},{2,1},{3,2},{4,3},{5,4},{6,5},{7,6},{8,7},{9,8},{10,9... | collective-permute-start | bytes 663560 | tf_op jit(solution)/shard_map/ppermute | solution.py:398
  18.7 18.9 %collective-permute-start.1 = (f32[54,8,128]{2,1,0:T(8,128)S(1)}, f32[54,8,128]{2,1,0:T(8,128)S(1)}, u32[]{:S(2)}, u32[]{:S(2)}) collective-permute-start(f32[54,8,128]{2,1,0:T(8,128)S(1)} %get-tuple-element.32), channel_id=1, source_target_pairs={{0,1},{1,2},{2,3},{3,4},{4,5},{5,6},{6,7},{7,8},{8,9},{9,10},{10,1... | collective-permute-start | bytes 663560 | tf_op jit(solution)/shard_map/ppermute | solution.py:397
  18.7 7.6 %collective-permute-start.2 = (f32[14,16,128]{2,1,0:T(8,128)S(1)}, f32[14,16,128]{2,1,0:T(8,128)S(1)}, u32[]{:S(2)}, u32[]{:S(2)}) collective-permute-start(f32[14,16,128]{2,1,0:T(8,128)S(1)} %get-tuple-element.35), channel_id=1, source_target_pairs={{0,64},{64,0},{128,192},{192,128},{256,320},{320,256},{384,448},{4... | collective-permute-start | bytes 344072 | tf_op jit(solution)/shard_map/ppermute | solution.py:395
  22.1 8.8 %collective-permute-start.3 = (f32[14,16,128]{2,1,0:T(8,128)S(1)}, f32[14,16,128]{2,1,0:T(8,128)S(1)}, u32[]{:S(2)}, u32[]{:S(2)}) collective-permute-start(f32[14,16,128]{2,1,0:T(8,128)S(1)} %get-tuple-element.36), channel_id=1, source_target_pairs={{64,128},{128,64},{192,256},{256,192},{320,384},{384,320},{448,512... | collective-permute-start | bytes 344072 | tf_op jit(solution)/shard_map/ppermute | solution.py:396
  31.1 3.6 %collective-permute-start.4 = (f32[15,8,128]{2,1,0:T(8,128)S(1)}, f32[15,8,128]{2,1,0:T(8,128)S(1)}, u32[]{:S(2)}, u32[]{:S(2)}) collective-permute-start(f32[15,8,128]{2,1,0:T(8,128)S(1)} %get-tuple-element.39), channel_id=1, source_target_pairs={{0,63},{1,0},{2,1},{3,2},{4,3},{5,4},{6,5},{7,6},{8,7},{9,8},{10,9... | collective-permute-start | bytes 184328 | tf_op jit(solution)/shard_map/ppermute | solution.py:404
  32.8 4.9 %collective-permute-start.5 = (f32[15,8,128]{2,1,0:T(8,128)S(1)}, f32[15,8,128]{2,1,0:T(8,128)S(1)}, u32[]{:S(2)}, u32[]{:S(2)}) collective-permute-start(f32[15,8,128]{2,1,0:T(8,128)S(1)} %get-tuple-element.40), channel_id=1, source_target_pairs={{0,1},{1,2},{2,3},{3,4},{4,5},{5,6},{6,7},{7,8},{8,9},{9,10},{10,1... | collective-permute-start | bytes 184328 | tf_op jit(solution)/shard_map/ppermute | solution.py:403
  41.4 4.3 %collective-permute-start.7 = (f32[8,256]{1,0:T(8,128)S(1)}, f32[8,256]{1,0:T(8,128)S(1)}, u32[]{:S(2)}, u32[]{:S(2)}) collective-permute-start(f32[8,256]{1,0:T(8,128)S(1)} %get-tuple-element.43.own_up), channel_id=1, source_target_pairs={{0,1},{1,2},{2,3},{3,4},{4,5},{5,6},{6,7},{7,8},{8,9},{9,10},{10,1... | collective-permute-start | bytes 24584 | tf_op jit(solution)/shard_map/ppermute | solution.py:416
  41.4 4.3 %collective-permute-start.6 = (f32[8,256]{1,0:T(8,128)S(1)}, f32[8,256]{1,0:T(8,128)S(1)}, u32[]{:S(2)}, u32[]{:S(2)}) collective-permute-start(f32[8,256]{1,0:T(8,128)S(1)} %get-tuple-element.44.own_down), channel_id=1, source_target_pairs={{0,63},{1,0},{2,1},{3,2},{4,3},{5,4},{6,5},{7,6},{8,7},{9,8},{10,9... | collective-permute-start | bytes 24584 | tf_op jit(solution)/shard_map/ppermute | solution.py:417

commit v5 on v4

--- a/solution.py
+++ b/solution.py
@@ -76,7 +76,7 @@
     for copy in copies:
         copy.start()
     lane = lanes_of(ROWS)
-    rightward = lax.axis_index("gx") % 2 == 0
+    rightward = lax.axis_index("gx") % 2 == 1
     low = rows_of(8) < 4
     for g in range(GROUPS):
         if g % 3 == 0:
@@ -128,7 +128,7 @@
 
 def strip_kernel(own_right, own_left, first_got, second_got, strips, side, up, down):
     col = lax.axis_index("gx")
-    rightward = col % 2 == 0
+    rightward = col % 2 == 1
     first, last = col == 0, col == lax.axis_size("gx") - 1
     lane = lanes_of(ROWS)
     within = lane % 16
@@ -256,7 +256,7 @@
     def behind_x(value, strip, z):
         return jnp.where(at_first, turn(strip[z % 2], -(32 * (z // 2) + 27), 1), turn(value, 1, 1))
 
-    def sweep(_, carry):
+    def sweep():
         for f in range(2):
             ex, ey, ez = ([strip_fields[f, c, t] for t in range(2)] for c in range(3))
             for t in range(2):
@@ -308,9 +308,8 @@
                 fields[f, 0, z] = kept * ex + step * (sources[f, 0, z] - curl_x)
                 fields[f, 1, z] = kept * ey + step * (sources[f, 1, z] - curl_y)
                 fields[f, 2, z] = kept * ez + step * (sources[f, 2, z] - curl_z)
-        return carry
-
-    lax.fori_loop(0, ITERS, sweep, 0)
+    for _ in range(ITERS):
+        sweep()
 
     product = jnp.zeros((ROWS, LANES), jnp.float32)
     strip_product = jnp.zeros((ROWS, LANES), jnp.float32)
@@ -392,8 +391,8 @@
         space=pltpu.HBM,
         scratch=[pltpu.SMEM(a.shape, a.dtype) for a in tiles] + [pltpu.SemaphoreType.DMA((9,))],
     )(*[pltpu.with_memory_space_constraint(a, pltpu.HBM) for a in (*tiles, *inner)])
-    first_got = lax.ppermute(first, "gx", swaps("gx", 0))
-    second_got = lax.ppermute(second, "gx", swaps("gx", 1))
+    first_got = lax.ppermute(first, "gx", swaps("gx", 1))
+    second_got = lax.ppermute(second, "gx", swaps("gx", 0))
     below = lax.ppermute(up, "gy", ring("gy", 1))
     above = lax.ppermute(down, "gy", ring("gy", -1))
     corner = shape(GROUPS + 2, 8, LANES)

time: 46.8 us -> 45.7 us (0.976)
  starting transfers between devices: 28.5 us -> 27.7 us
    ppermute x2, starting transfers between devices: 7.57 us -> 6.79 us  [the longest x1 4.83 us: on_device(): first_got = lax.ppermute(first, 'gx', swaps('gx', 1))]
  transfers between devices with their start and end apart: 8 -> 8, of which waited for: 4 -> 5; matrix products, arithmetic and copies ran while one was open for 0% -> 0% of each run, Pallas kernels for 0% -> 0%
where the time goes in v5:
time: 45.7 us; the launch traced here: 45.5 us
  starting transfers between devices  27.7 us (61%)
  waiting for transfers between devices  11 us (24%)
  Pallas kernels  6.19 us (14%)
  between operations  0.67 us (1%)
    ppermute x1, starting transfers between devices, on_device(): above = lax.ppermute(down, 'gy', ring('gy', -1))  16.2 us
    pallas_call x4, Pallas kernels, run(): pl.pallas_call(kernel, out_shape=outs, in_specs=[pl.BlockSpec(memory_spac...  6.19 us
    ppermute x1, starting transfers between devices, on_device(): first_got = lax.ppermute(first, 'gx', swaps('gx', 1))  4.83 us
    ppermute x1, waiting for transfers between devices, on_device(): strip_below = lax.ppermute(strip_up, 'gy', ring('gy', 1))  2.99 us
    ppermute x1, starting transfers between devices, on_device(): local_above = lax.ppermute(local_down, 'gy', ring('gy', -1))  2.95 us
    ppermute x1, waiting for transfers between devices, on_device(): second_got = lax.ppermute(second, 'gx', swaps('gx', 0))  2.74 us
    ppermute x1, waiting for transfers between devices, on_device(): first_got = lax.ppermute(first, 'gx', swaps('gx', 1))  1.98 us
    ppermute x1, starting transfers between devices, on_device(): second_got = lax.ppermute(second, 'gx', swaps('gx', 0))  1.95 us
  transfers between devices with their start and end apart: 8, of which 5 were waited for; matrix products, arithmetic and copies ran while one was open for 0% of the time, Pallas kernels for 0%

profile of v5, /device:TPU:24, one launch (start us, length us, event | category | flops | bytes accessed | tf_op | source)
XLA Modules:
  0.0 45.5 jit_solution(11791325358395837542)
XLA Ops:
  0.6 1.9 %shard_map.112 = (f32[14,16,128]{2,1,0:T(8,128)S(1)}, f32[14,16,128]{2,1,0:T(8,128)S(1)}, f32[14,16,128]{2,1,0:T(8,128)S(1)}, f32[14,16,128]{2,1,0:T(8,128)S(1)}...) custom-call(s32[8,16]{1,0:T(8,128)} %design_in.1, ...), custom_call_target="tpu_custom_call" | custom-call | tf_op jit(solution)/shard_map/pallas_call | solution.py:368
  2.5 16.2 %collective-permute-start = (f32[54,8,128]{2,1,0:T(8,128)S(1)}, f32[54,8,128]{2,1,0:T(8,128)S(1)}, u32[]{:S(2)}, u32[]{:S(2)}) collective-permute-start(f32[54,8,128]{2,1,0:T(8,128)S(1)} %get-tuple-element.31), channel_id=1, source_target_pairs={{0,63},{1,0},{2,1},{3,2},{4,3},{5,4},{6,5},{7,6},{8,7},{9,8},{10,9... | collective-permute-start | bytes 663560 | tf_op jit(solution)/shard_map/ppermute | solution.py:397
  18.7 0.0 collective-permute-start.1
  18.7 4.8 %collective-permute-start.2 = (f32[14,16,128]{2,1,0:T(8,128)S(1)}, f32[14,16,128]{2,1,0:T(8,128)S(1)}, u32[]{:S(2)}, u32[]{:S(2)}) collective-permute-start(f32[14,16,128]{2,1,0:T(8,128)S(1)} %get-tuple-element.35), channel_id=1, source_target_pairs={{64,128},{128,64},{192,256},{256,192},{320,384},{384,320},{448,512... | collective-permute-start | bytes 344072 | tf_op jit(solution)/shard_map/ppermute | solution.py:394
  23.6 2.0 %collective-permute-start.3 = (f32[14,16,128]{2,1,0:T(8,128)S(1)}, f32[14,16,128]{2,1,0:T(8,128)S(1)}, u32[]{:S(2)}, u32[]{:S(2)}) collective-permute-start(f32[14,16,128]{2,1,0:T(8,128)S(1)} %get-tuple-element.36), channel_id=1, source_target_pairs={{0,64},{64,0},{128,192},{192,128},{256,320},{320,256},{384,448},{4... | collective-permute-start | bytes 344072 | tf_op jit(solution)/shard_map/ppermute | solution.py:395
  25.5 2.0 %collective-permute-done.2.first_got = f32[14,16,128]{2,1,0:T(8,128)S(1)} collective-permute-done((f32[14,16,128]{2,1,0:T(8,128)S(1)}, f32[14,16,128]{2,1,0:T(8,128)S(1)}, u32[]{:S(2)}, u32[]{:S(2)}) %collective-permute-start.2) | collective-permute-done | bytes 114720 | tf_op jit(solution)/shard_map/ppermute | solution.py:394
  27.5 2.7 %collective-permute-done.3.second_got = f32[14,16,128]{2,1,0:T(8,128)S(1)} collective-permute-done((f32[14,16,128]{2,1,0:T(8,128)S(1)}, f32[14,16,128]{2,1,0:T(8,128)S(1)}, u32[]{:S(2)}, u32[]{:S(2)}) %collective-permute-start.3) | collective-permute-done | bytes 114720 | tf_op jit(solution)/shard_map/ppermute | solution.py:395
  30.3 0.1 shard_map.113
  30.4 1.7 %collective-permute-start.4 = (f32[15,8,128]{2,1,0:T(8,128)S(1)}, f32[15,8,128]{2,1,0:T(8,128)S(1)}, u32[]{:S(2)}, u32[]{:S(2)}) collective-permute-start(f32[15,8,128]{2,1,0:T(8,128)S(1)} %get-tuple-element.39), channel_id=1, source_target_pairs={{0,63},{1,0},{2,1},{3,2},{4,3},{5,4},{6,5},{7,6},{8,7},{9,8},{10,9... | collective-permute-start | bytes 184328 | tf_op jit(solution)/shard_map/ppermute | solution.py:403
  32.2 0.0 collective-permute-start.5
  32.2 1.9 %collective-permute-done.4.strip_above = f32[15,8,128]{2,1,0:T(8,128)S(1)} collective-permute-done((f32[15,8,128]{2,1,0:T(8,128)S(1)}, f32[15,8,128]{2,1,0:T(8,128)S(1)}, u32[]{:S(2)}, u32[]{:S(2)}) %collective-permute-start.4) | collective-permute-done | bytes 61472 | tf_op jit(solution)/shard_map/ppermute | solution.py:403
  34.0 3.0 %collective-permute-done.5.strip_below = f32[15,8,128]{2,1,0:T(8,128)S(1)} collective-permute-done((f32[15,8,128]{2,1,0:T(8,128)S(1)}, f32[15,8,128]{2,1,0:T(8,128)S(1)}, u32[]{:S(2)}, u32[]{:S(2)}) %collective-permute-start.5) | collective-permute-done | bytes 61472 | tf_op jit(solution)/shard_map/ppermute | solution.py:402
  37.0 0.0 collective-permute-done.above
  37.0 0.0 collective-permute-done.1.below
  37.0 3.3 %shard_map.114 = (f32[3,8,16,128]{3,2,1,0:T(8,128)}, f32[3,8,16,128]{3,2,1,0:T(8,128)}, f32[8,256]{1,0:T(8,128)S(1)}, f32[8,256]{1,0:T(8,128)S(1)}) custom-call(f32[3,24,128]{2,1,0:T(8,128)S(1)} %get-tuple-element.24.gains, f32[3,8,16,128]{3,2,1,0:T(8,128)S(1)} %get-tuple-element.25.field, f32[3,8,16,128]{3,2,1,0:T(8,128)S(1)} %get-tuple-element.26.adjoint, ...), custom_call_target="tpu_custom_call" | custom-call | tf_op jit(solution)/shard_map/pallas_call | solution.py:368
  40.4 0.0 collective-permute-start.7
  40.4 3.0 %collective-permute-start.6 = (f32[8,256]{1,0:T(8,128)S(1)}, f32[8,256]{1,0:T(8,128)S(1)}, u32[]{:S(2)}, u32[]{:S(2)}) collective-permute-start(f32[8,256]{1,0:T(8,128)S(1)} %get-tuple-element.44.own_down), channel_id=1, source_target_pairs={{0,63},{1,0},{2,1},{3,2},{4,3},{5,4},{6,5},{7,6},{8,7},{9,8},{10,9... | collective-permute-start | bytes 24584 | tf_op jit(solution)/shard_map/ppermute | solution.py:416
  43.3 1.3 %collective-permute-done.7.below = f32[8,256]{1,0:T(8,128)S(1)} collective-permute-done((f32[8,256]{1,0:T(8,128)S(1)}, f32[8,256]{1,0:T(8,128)S(1)}, u32[]{:S(2)}, u32[]{:S(2)}) %collective-permute-start.7) | collective-permute-done | bytes 8224 | tf_op jit(solution)/shard_map/ppermute | solution.py:415
  44.6 0.0 collective-permute-done.6.above
  44.7 0.8 %shard_map.115 = f32[16,128]{1,0:T(8,128)} custom-call(f32[8,256]{1,0:T(8,128)S(1)} %get-tuple-element.43.own_up, f32[8,256]{1,0:T(8,128)S(1)} %get-tuple-element.44.own_down, f32[8,256]{1,0:T(8,128)S(1)} %collective-permute-done.6.above, f32[8,256]{1,0:T(8,128)S(1)} %collective-permute-done.7.below), custom_call_target="tpu_custom_call" | custom-call | tf_op jit(solution)/shard_map/pallas_call | solution.py:368
Async XLA Ops:
  2.5 34.5 %collective-permute-start = (f32[54,8,128]{2,1,0:T(8,128)S(1)}, f32[54,8,128]{2,1,0:T(8,128)S(1)}, u32[]{:S(2)}, u32[]{:S(2)}) collective-permute-start(f32[54,8,128]{2,1,0:T(8,128)S(1)} %get-tuple-element.31), channel_id=1, source_target_pairs={{0,63},{1,0},{2,1},{3,2},{4,3},{5,4},{6,5},{7,6},{8,7},{9,8},{10,9... | collective-permute-start | bytes 663560 | tf_op jit(solution)/shard_map/ppermute | solution.py:397
  18.7 18.3 %collective-permute-start.1 = (f32[54,8,128]{2,1,0:T(8,128)S(1)}, f32[54,8,128]{2,1,0:T(8,128)S(1)}, u32[]{:S(2)}, u32[]{:S(2)}) collective-permute-start(f32[54,8,128]{2,1,0:T(8,128)S(1)} %get-tuple-element.32), channel_id=1, source_target_pairs={{0,1},{1,2},{2,3},{3,4},{4,5},{5,6},{6,7},{7,8},{8,9},{9,10},{10,1... | collective-permute-start | bytes 663560 | tf_op jit(solution)/shard_map/ppermute | solution.py:396
  18.7 8.8 %collective-permute-start.2 = (f32[14,16,128]{2,1,0:T(8,128)S(1)}, f32[14,16,128]{2,1,0:T(8,128)S(1)}, u32[]{:S(2)}, u32[]{:S(2)}) collective-permute-start(f32[14,16,128]{2,1,0:T(8,128)S(1)} %get-tuple-element.35), channel_id=1, source_target_pairs={{64,128},{128,64},{192,256},{256,192},{320,384},{384,320},{448,512... | collective-permute-start | bytes 344072 | tf_op jit(solution)/shard_map/ppermute | solution.py:394
  23.6 6.7 %collective-permute-start.3 = (f32[14,16,128]{2,1,0:T(8,128)S(1)}, f32[14,16,128]{2,1,0:T(8,128)S(1)}, u32[]{:S(2)}, u32[]{:S(2)}) collective-permute-start(f32[14,16,128]{2,1,0:T(8,128)S(1)} %get-tuple-element.36), channel_id=1, source_target_pairs={{0,64},{64,0},{128,192},{192,128},{256,320},{320,256},{384,448},{4... | collective-permute-start | bytes 344072 | tf_op jit(solution)/shard_map/ppermute | solution.py:395
  30.4 3.6 %collective-permute-start.4 = (f32[15,8,128]{2,1,0:T(8,128)S(1)}, f32[15,8,128]{2,1,0:T(8,128)S(1)}, u32[]{:S(2)}, u32[]{:S(2)}) collective-permute-start(f32[15,8,128]{2,1,0:T(8,128)S(1)} %get-tuple-element.39), channel_id=1, source_target_pairs={{0,63},{1,0},{2,1},{3,2},{4,3},{5,4},{6,5},{7,6},{8,7},{9,8},{10,9... | collective-permute-start | bytes 184328 | tf_op jit(solution)/shard_map/ppermute | solution.py:403
  32.2 4.9 %collective-permute-start.5 = (f32[15,8,128]{2,1,0:T(8,128)S(1)}, f32[15,8,128]{2,1,0:T(8,128)S(1)}, u32[]{:S(2)}, u32[]{:S(2)}) collective-permute-start(f32[15,8,128]{2,1,0:T(8,128)S(1)} %get-tuple-element.40), channel_id=1, source_target_pairs={{0,1},{1,2},{2,3},{3,4},{4,5},{5,6},{6,7},{7,8},{8,9},{9,10},{10,1... | collective-permute-start | bytes 184328 | tf_op jit(solution)/shard_map/ppermute | solution.py:402
  40.4 4.3 %collective-permute-start.7 = (f32[8,256]{1,0:T(8,128)S(1)}, f32[8,256]{1,0:T(8,128)S(1)}, u32[]{:S(2)}, u32[]{:S(2)}) collective-permute-start(f32[8,256]{1,0:T(8,128)S(1)} %get-tuple-element.43.own_up), channel_id=1, source_target_pairs={{0,1},{1,2},{2,3},{3,4},{4,5},{5,6},{6,7},{7,8},{8,9},{9,10},{10,1... | collective-permute-start | bytes 24584 | tf_op jit(solution)/shard_map/ppermute | solution.py:415
  40.4 4.3 %collective-permute-start.6 = (f32[8,256]{1,0:T(8,128)S(1)}, f32[8,256]{1,0:T(8,128)S(1)}, u32[]{:S(2)}, u32[]{:S(2)}) collective-permute-start(f32[8,256]{1,0:T(8,128)S(1)} %get-tuple-element.44.own_down), channel_id=1, source_target_pairs={{0,63},{1,0},{2,1},{3,2},{4,3},{5,4},{6,5},{7,6},{8,7},{9,8},{10,9... | collective-permute-start | bytes 24584 | tf_op jit(solution)/shard_map/ppermute | solution.py:416

commit v6 on v5

--- a/solution.py
+++ b/solution.py
@@ -64,7 +64,7 @@
 
 def pack_kernel(
     design_in, material_in, contrast_in, field_in, adjoint_in, source_in, adjoint_source_in, background_in, density_in,
-    first, second, own_right, own_left, up, down, gains, field, adjoint, source, adjoint_source, background, density,
+    first, second, own_right, own_left, far, near, gains, field, adjoint, source, adjoint_source, background, density,
     design, material, contrast, done,
 ):
     arrays = (
@@ -77,6 +77,7 @@
         copy.start()
     lane = lanes_of(ROWS)
     rightward = lax.axis_index("gx") % 2 == 1
+    upward = lax.axis_index("gy") % 2 == 1
     low = rows_of(8) < 4
     for g in range(GROUPS):
         if g % 3 == 0:
@@ -99,15 +100,17 @@
         second[g] = jnp.where(rightward, to_left, to_right)
         for pair in range(Z // 2):
             k = g * (Z // 2) + pair
-            down[k] = jnp.where(low, planes[2 * pair, 0:8], turn(planes[2 * pair + 1, 0:8], 4, 0))
-            up[k] = jnp.where(low, turn(planes[2 * pair + 1, 8:16], 4, 0), planes[2 * pair, 8:16])
+            down = jnp.where(low, planes[2 * pair, 0:8], turn(planes[2 * pair + 1, 0:8], 4, 0))
+            up = jnp.where(low, turn(planes[2 * pair + 1, 8:16], 4, 0), planes[2 * pair, 8:16])
+            far[k] = jnp.where(upward, up, down)
+            near[k] = jnp.where(upward, down, up)
     for copy in copies[5:]:
         copy.wait()
     first[GROUPS] = density[...]
     second[GROUPS] = density[...]
     for part in range(2):
-        up[4 * GROUPS + part] = density[8 * part : 8 * part + 8]
-        down[4 * GROUPS + part] = density[8 * part : 8 * part + 8]
+        far[4 * GROUPS + part] = density[8 * part : 8 * part + 8]
+        near[4 * GROUPS + part] = density[8 * part : 8 * part + 8]
 
     col, row = lax.axis_index("gx"), lax.axis_index("gy")
     row24 = rows_of(WRAP)
@@ -126,9 +129,10 @@
         gains[k] = jnp.where(row24 < 16, here, jnp.where(row24 < 20, up, down))
 
 
-def strip_kernel(own_right, own_left, first_got, second_got, strips, side, up, down):
+def strip_kernel(own_right, own_left, first_got, second_got, strips, side, far, near):
     col = lax.axis_index("gx")
     rightward = col % 2 == 1
+    upward = lax.axis_index("gy") % 2 == 1
     first, last = col == 0, col == lax.axis_size("gx") - 1
     lane = lanes_of(ROWS)
     within = lane % 16
@@ -148,32 +152,36 @@
         odd = jnp.where(half, turn(here_right, -16, 1), here_left)
         strips[g, 0] = even
         strips[g, 1] = odd
-        down[g] = jnp.where(low, even[0:8], turn(odd[0:8], 4, 0))
-        up[g] = jnp.where(low, turn(odd[8:16], 4, 0), even[8:16])
+        down = jnp.where(low, even[0:8], turn(odd[0:8], 4, 0))
+        up = jnp.where(low, turn(odd[8:16], 4, 0), even[8:16])
+        far[g] = jnp.where(upward, up, down)
+        near[g] = jnp.where(upward, down, up)
     from_right, from_left = sides(GROUPS)
     beside = jnp.where(lane < 64, from_right, from_left)
     side[...] = beside
     for part in range(2):
-        up[GROUPS + part] = beside[8 * part : 8 * part + 8]
-        down[GROUPS + part] = beside[8 * part : 8 * part + 8]
-
-
-def unpack(above, below, low, odd):
-    if odd:
-        return turn(jnp.where(low, below, above), 4, 0)
-    return jnp.where(low, above, below)
+        far[GROUPS + part] = beside[8 * part : 8 * part + 8]
+        near[GROUPS + part] = beside[8 * part : 8 * part + 8]
+
+
+def unpack(far, near, pick, second):
+    if second:
+        return turn(jnp.where(pick, near, far), 4, 0)
+    return jnp.where(pick, far, near)
 
 
 def main_kernel(
     gains, field, adjoint, source, adjoint_source, background, density,
-    above, below, strips, side, strip_above, strip_below,
-    field_out, adjoint_out, local_up, local_down,
+    far, near, strips, side, strip_far, strip_near,
+    field_out, adjoint_out, local_far, local_near,
     fields, sources, curls, rate, keep, strip_fields, strip_sources, strip_curls, strip_rate, strip_keep, wide,
 ):
     col, row = lax.axis_index("gx"), lax.axis_index("gy")
     cols, rows = lax.axis_size("gx"), lax.axis_size("gy")
     first_row, last_row = row == 0, row == rows - 1
     low = rows_of(8) < 4
+    upward = row % 2 == 1
+    pick = jnp.where(upward, rows_of(8), 7 - rows_of(8)) < 4
     lane24, row24 = lanes_of(WRAP), rows_of(WRAP)
     outside8 = (low & last_row) | (jnp.logical_not(low) & first_row)
     outside = ((row24 >= 16) & (row24 < 20) & last_row) | ((row24 >= 20) & first_row)
@@ -181,16 +189,17 @@
     outside_strip = outside | ((j >= HALO) & (j < 16) & (col == cols - 1)) | ((j >= 16) & (j < 28) & (col == 0))
     gain_main, gain_right, gain_left = gains[0], gains[1], gains[2]
 
-    wide[0:8, 0:LANES] = jnp.where(first_row, 0.0, below[52])
-    wide[8:16, 0:LANES] = jnp.where(first_row, 0.0, below[53])
-    wide[0:8, LANES : 2 * LANES] = jnp.where(first_row, 0.0, strip_below[13])
-    wide[8:16, LANES : 2 * LANES] = jnp.where(first_row, 0.0, strip_below[14])
     wide[16:32, 0:LANES] = density[...]
     wide[16:32, LANES : 2 * LANES] = side[...]
-    wide[32:40, 0:LANES] = jnp.where(last_row, 0.0, above[52])
-    wide[40:48, 0:LANES] = jnp.where(last_row, 0.0, above[53])
-    wide[32:40, LANES : 2 * LANES] = jnp.where(last_row, 0.0, strip_above[13])
-    wide[40:48, LANES : 2 * LANES] = jnp.where(last_row, 0.0, strip_above[14])
+    for part in range(2):
+        k, rows8 = 4 * GROUPS + part, slice(8 * part, 8 * part + 8)
+        wide[rows8, 0:LANES] = jnp.where(first_row, 0.0, jnp.where(upward, near[k], far[k]))
+        rows8 = slice(32 + 8 * part, 40 + 8 * part)
+        wide[rows8, 0:LANES] = jnp.where(last_row, 0.0, jnp.where(upward, far[k], near[k]))
+        k, rows8 = GROUPS + part, slice(8 * part, 8 * part + 8)
+        wide[rows8, LANES : 2 * LANES] = jnp.where(first_row, 0.0, jnp.where(upward, strip_near[k], strip_far[k]))
+        rows8 = slice(32 + 8 * part, 40 + 8 * part)
+        wide[rows8, LANES : 2 * LANES] = jnp.where(last_row, 0.0, jnp.where(upward, strip_far[k], strip_near[k]))
     filtered = cone(lambda a: wide[8 + a : 40 + a], 32)
     low2 = lax.broadcasted_iota(jnp.int32, (8, 2 * LANES), 0) < 4
     filtered = jnp.concatenate(
@@ -212,13 +221,13 @@
 
     for z in range(Z):
         k = 48 + z // 2
-        halo = unpack(above[k], below[k], low, z % 2)
+        halo = unpack(far[k], near[k], pick, z % 2)
         step = 0.5 / (4.0 + 0.5 * (whole(background[z], halo) + design_main))
         step = jnp.where(outside, 0.0, step)
         rate[z] = step
         keep[z] = 0.5 + 4.0 * step
     for t in range(2):
-        halo = unpack(strip_above[12], strip_below[12], low, t)
+        halo = unpack(strip_far[12], strip_near[12], pick, t)
         step = 0.5 / (4.0 + 0.5 * (whole(strips[12, t], halo) + design_strip))
         step = jnp.where(outside_strip, 0.0, step)
         strip_rate[t] = step
@@ -230,13 +239,13 @@
             g = 3 * f + c
             for z in range(Z):
                 k = 4 * g + z // 2
-                halo = unpack(above[k], below[k], low, z % 2)
+                halo = unpack(far[k], near[k], pick, z % 2)
                 if f < 2:
                     fields[f, c, z] = whole(starts[f][c, z], jnp.where(outside8, 0.0, halo))
                 else:
                     sources[f - 2, c, z] = whole(starts[f][c, z], halo)
             for t in range(2):
-                halo = unpack(strip_above[g], strip_below[g], low, t)
+                halo = unpack(strip_far[g], strip_near[g], pick, t)
                 if f < 2:
                     strip_fields[f, c, t] = whole(strips[g, t], jnp.where(outside8, 0.0, halo))
                 else:
@@ -329,22 +338,22 @@
         lane < 64, turn(strip_product, -4, 1) * (-0.5 * gain_right[0:ROWS]),
         turn(strip_product, 100, 1) * (-0.5 * gain_left[0:ROWS]),
     )
-    local_down[:, 0:LANES] = local[0:8]
-    local_down[:, LANES : 2 * LANES] = local_side[0:8]
-    local_up[:, 0:LANES] = local[8:16]
-    local_up[:, LANES : 2 * LANES] = local_side[8:16]
+    for out, value in ((slice(0, LANES), local), (slice(LANES, 2 * LANES), local_side)):
+        local_far[:, out] = jnp.where(upward, value[8:16], value[0:8])
+        local_near[:, out] = jnp.where(upward, value[0:8], value[8:16])
 
 
 def turn_edges(right_side, left_side, lane):
     return jnp.where(lane < 16, right_side, left_side)
 
 
-def gradient_kernel(own_up, own_down, above, below, gradient, wide):
+def gradient_kernel(own_far, own_near, far, near, gradient, wide):
     row = lax.axis_index("gy")
-    wide[0:8] = jnp.where(row == 0, 0.0, below[...])
-    wide[8:16] = own_down[...]
-    wide[16:24] = own_up[...]
-    wide[24:32] = jnp.where(row == lax.axis_size("gy") - 1, 0.0, above[...])
+    upward = row % 2 == 1
+    wide[0:8] = jnp.where(row == 0, 0.0, jnp.where(upward, near[...], far[...]))
+    wide[8:16] = jnp.where(upward, own_near[...], own_far[...])
+    wide[16:24] = jnp.where(upward, own_far[...], own_near[...])
+    wide[24:32] = jnp.where(row == lax.axis_size("gy") - 1, 0.0, jnp.where(upward, far[...], near[...]))
     gradient[...] = cone(lambda a: wide[8 + a : 24 + a], ROWS)[:, :LANES]
 
 
@@ -354,9 +363,8 @@
     return sorted(pairs + [(j, i) for i, j in pairs])
 
 
-def ring(axis, step):
-    size = lax.axis_size(axis)
-    return [(i, (i + step) % size) for i in range(size)]
+def swap_rows(far, near):
+    return lax.ppermute(far, "gy", swaps("gy", 1)), lax.ppermute(near, "gy", swaps("gy", 0))
 
 
 def shape(*dims):
@@ -385,7 +393,7 @@
     inner = (field_start, adjoint_start, source, adjoint_source, background, density)
     tiles = (design_tiles, material_tiles, contrast)
     edges, rows = shape(GROUPS + 1, ROWS, LANES), shape(4 * GROUPS + 2, 8, LANES)
-    first, second, own_right, own_left, up, down, gains, *inner = call(
+    first, second, own_right, own_left, far, near, gains, *inner = call(
         pack_kernel,
         [edges, edges, edges, edges, rows, rows, shape(3, WRAP, LANES)] + [shape(*a.shape) for a in inner],
         space=pltpu.HBM,
@@ -393,17 +401,15 @@
     )(*[pltpu.with_memory_space_constraint(a, pltpu.HBM) for a in (*tiles, *inner)])
     first_got = lax.ppermute(first, "gx", swaps("gx", 1))
     second_got = lax.ppermute(second, "gx", swaps("gx", 0))
-    below = lax.ppermute(up, "gy", ring("gy", 1))
-    above = lax.ppermute(down, "gy", ring("gy", -1))
+    far_got, near_got = swap_rows(far, near)
     corner = shape(GROUPS + 2, 8, LANES)
-    strips, side, strip_up, strip_down = call(
+    strips, side, strip_far, strip_near = call(
         strip_kernel, [shape(GROUPS, 2, ROWS, LANES), shape(ROWS, LANES), corner, corner]
     )(own_right, own_left, first_got, second_got)
-    strip_below = lax.ppermute(strip_up, "gy", ring("gy", 1))
-    strip_above = lax.ppermute(strip_down, "gy", ring("gy", -1))
+    strip_far_got, strip_near_got = swap_rows(strip_far, strip_near)
     block, part = shape(3, Z, ROWS, LANES), shape(8, 2 * LANES)
     planes, sheets = (2, 3, Z, WRAP, LANES), (2, 3, 2, WRAP, LANES)
-    field, adjoint, local_up, local_down = call(
+    field, adjoint, local_far, local_near = call(
         main_kernel,
         [block, block, part, part],
         scratch=[
@@ -411,11 +417,10 @@
             room(*sheets), room(*sheets), room(*sheets), room(2, WRAP, LANES), room(2, WRAP, LANES),
             room(48, 2 * LANES),
         ],
-    )(gains, *inner, above, below, strips, side, strip_above, strip_below)
-    local_below = lax.ppermute(local_up, "gy", ring("gy", 1))
-    local_above = lax.ppermute(local_down, "gy", ring("gy", -1))
+    )(gains, *inner, far_got, near_got, strips, side, strip_far_got, strip_near_got)
+    local_far_got, local_near_got = swap_rows(local_far, local_near)
     gradient = call(gradient_kernel, shape(ROWS, LANES), scratch=[room(32, 2 * LANES)])(
-        local_up, local_down, local_above, local_below
+        local_far, local_near, local_far_got, local_near_got
     )
     return (field, adjoint, gradient)
 

time: 45.7 us -> 43.1 us (0.943)
  the two profiles are of different devices: /device:TPU:24 before, /device:TPU:1 now
where the time goes in v6:
time: 43.1 us; the launch traced here: 42.7 us
  starting transfers between devices  28.2 us (65%)
  waiting for transfers between devices  7.54 us (17%)
  Pallas kernels  6.21 us (14%)
  between operations  0.74 us (2%)
    ppermute x3, starting transfers between devices, swap_rows(): lax.ppermute(near, 'gy', swaps('gy', 0))  15.6 us
    ppermute x3, starting transfers between devices, swap_rows(): lax.ppermute(far, 'gy', swaps('gy', 1))  10 us
    pallas_call x4, Pallas kernels, run(): pl.pallas_call(kernel, out_shape=outs, in_specs=[pl.BlockSpec(memory_spac...  6.21 us
    ppermute x1, waiting for transfers between devices, on_device(): second_got = lax.ppermute(second, 'gx', swaps('gx', 0))  4.72 us
    ppermute x1, starting transfers between devices, on_device(): second_got = lax.ppermute(second, 'gx', swaps('gx', 0))  1.92 us
    ppermute x3, waiting for transfers between devices, swap_rows(): lax.ppermute(far, 'gy', swaps('gy', 1))  1.69 us
    ppermute x3, waiting for transfers between devices, swap_rows(): lax.ppermute(near, 'gy', swaps('gy', 0))  1.13 us
  transfers between devices with their start and end apart: 8, of which 3 were waited for; matrix products, arithmetic and copies ran while one was open for 0% of the time, Pallas kernels for 0%

profile of v6, /device:TPU:1, one launch (start us, length us, event | category | flops | bytes accessed | tf_op | source)
XLA Modules:
  0.0 42.7 jit_solution(7682210180498128825)
XLA Ops:
  0.6 1.9 %shard_map.112 = (f32[14,16,128]{2,1,0:T(8,128)S(1)}, f32[14,16,128]{2,1,0:T(8,128)S(1)}, f32[14,16,128]{2,1,0:T(8,128)S(1)}, f32[14,16,128]{2,1,0:T(8,128)S(1)}...) custom-call(s32[8,16]{1,0:T(8,128)} %design_in.1, ...), custom_call_target="tpu_custom_call" | custom-call | tf_op jit(solution)/shard_map/pallas_call | solution.py:376
  2.5 4.9 %collective-permute-start = (f32[54,8,128]{2,1,0:T(8,128)S(1)}, f32[54,8,128]{2,1,0:T(8,128)S(1)}, u32[]{:S(2)}, u32[]{:S(2)}) collective-permute-start(f32[54,8,128]{2,1,0:T(8,128)S(1)} %get-tuple-element.31), channel_id=1, source_target_pairs={{1,2},{2,1},{3,4},{4,3},{5,6},{6,5},{7,8},{8,7},{9,10},{10,9},{11,... | collective-permute-start | bytes 663560 | tf_op jit(solution)/shard_map/ppermute | solution.py:367
  7.5 11.8 %collective-permute-start.1 = (f32[54,8,128]{2,1,0:T(8,128)S(1)}, f32[54,8,128]{2,1,0:T(8,128)S(1)}, u32[]{:S(2)}, u32[]{:S(2)}) collective-permute-start(f32[54,8,128]{2,1,0:T(8,128)S(1)} %get-tuple-element.32), channel_id=1, source_target_pairs={{0,1},{1,0},{2,3},{3,2},{4,5},{5,4},{6,7},{7,6},{8,9},{9,8},{10,11... | collective-permute-start | bytes 663560 | tf_op jit(solution)/shard_map/ppermute | solution.py:367
  19.3 0.7 %collective-permute-start.2 = (f32[14,16,128]{2,1,0:T(8,128)S(1)}, f32[14,16,128]{2,1,0:T(8,128)S(1)}, u32[]{:S(2)}, u32[]{:S(2)}) collective-permute-start(f32[14,16,128]{2,1,0:T(8,128)S(1)} %get-tuple-element.35), channel_id=1, source_target_pairs={{64,128},{128,64},{192,256},{256,192},{320,384},{384,320},{448,512... | collective-permute-start | bytes 344072 | tf_op jit(solution)/shard_map/ppermute | solution.py:402
  19.9 1.9 %collective-permute-start.3 = (f32[14,16,128]{2,1,0:T(8,128)S(1)}, f32[14,16,128]{2,1,0:T(8,128)S(1)}, u32[]{:S(2)}, u32[]{:S(2)}) collective-permute-start(f32[14,16,128]{2,1,0:T(8,128)S(1)} %get-tuple-element.36), channel_id=1, source_target_pairs={{0,64},{64,0},{128,192},{192,128},{256,320},{320,256},{384,448},{4... | collective-permute-start | bytes 344072 | tf_op jit(solution)/shard_map/ppermute | solution.py:403
  21.9 0.0 collective-permute-done.2.first_got
  21.9 4.7 %collective-permute-done.3.second_got = f32[14,16,128]{2,1,0:T(8,128)S(1)} collective-permute-done((f32[14,16,128]{2,1,0:T(8,128)S(1)}, f32[14,16,128]{2,1,0:T(8,128)S(1)}, u32[]{:S(2)}, u32[]{:S(2)}) %collective-permute-start.3) | collective-permute-done | bytes 114720 | tf_op jit(solution)/shard_map/ppermute | solution.py:403
  26.6 0.1 shard_map.113
  26.8 1.9 %collective-permute-start.4 = (f32[15,8,128]{2,1,0:T(8,128)S(1)}, f32[15,8,128]{2,1,0:T(8,128)S(1)}, u32[]{:S(2)}, u32[]{:S(2)}) collective-permute-start(f32[15,8,128]{2,1,0:T(8,128)S(1)} %get-tuple-element.39), channel_id=1, source_target_pairs={{1,2},{2,1},{3,4},{4,3},{5,6},{6,5},{7,8},{8,7},{9,10},{10,9},{11,... | collective-permute-start | bytes 184328 | tf_op jit(solution)/shard_map/ppermute | solution.py:367
  28.7 1.9 %collective-permute-start.5 = (f32[15,8,128]{2,1,0:T(8,128)S(1)}, f32[15,8,128]{2,1,0:T(8,128)S(1)}, u32[]{:S(2)}, u32[]{:S(2)}) collective-permute-start(f32[15,8,128]{2,1,0:T(8,128)S(1)} %get-tuple-element.40), channel_id=1, source_target_pairs={{0,1},{1,0},{2,3},{3,2},{4,5},{5,4},{6,7},{7,6},{8,9},{9,8},{10,11... | collective-permute-start | bytes 184328 | tf_op jit(solution)/shard_map/ppermute | solution.py:367
  30.6 1.7 %collective-permute-done.4.strip_far = f32[15,8,128]{2,1,0:T(8,128)S(1)} collective-permute-done((f32[15,8,128]{2,1,0:T(8,128)S(1)}, f32[15,8,128]{2,1,0:T(8,128)S(1)}, u32[]{:S(2)}, u32[]{:S(2)}) %collective-permute-start.4) | collective-permute-done | bytes 61472 | tf_op jit(solution)/shard_map/ppermute | solution.py:367
  32.3 0.0 collective-permute-done.5.strip_near
  32.3 0.0 collective-permute-done.far
  32.3 0.0 collective-permute-done.1.near
  32.3 3.4 %shard_map.114 = (f32[3,8,16,128]{3,2,1,0:T(8,128)}, f32[3,8,16,128]{3,2,1,0:T(8,128)}, f32[8,256]{1,0:T(8,128)S(1)}, f32[8,256]{1,0:T(8,128)S(1)}) custom-call(f32[3,24,128]{2,1,0:T(8,128)S(1)} %get-tuple-element.24.gains, f32[3,8,16,128]{3,2,1,0:T(8,128)S(1)} %get-tuple-element.25.field, f32[3,8,16,128]{3,2,1,0:T(8,128)S(1)} %get-tuple-element.26.adjoint, ...), custom_call_target="tpu_custom_call" | custom-call | tf_op jit(solution)/shard_map/pallas_call | solution.py:376
  35.7 3.1 %collective-permute-start.6 = (f32[8,256]{1,0:T(8,128)S(1)}, f32[8,256]{1,0:T(8,128)S(1)}, u32[]{:S(2)}, u32[]{:S(2)}) collective-permute-start(f32[8,256]{1,0:T(8,128)S(1)} %get-tuple-element.43.own_far), channel_id=1, source_target_pairs={{1,2},{2,1},{3,4},{4,3},{5,6},{6,5},{7,8},{8,7},{9,10},{10,9},{11,... | collective-permute-start | bytes 24584 | tf_op jit(solution)/shard_map/ppermute | solution.py:367
  38.8 1.9 %collective-permute-start.7 = (f32[8,256]{1,0:T(8,128)S(1)}, f32[8,256]{1,0:T(8,128)S(1)}, u32[]{:S(2)}, u32[]{:S(2)}) collective-permute-start(f32[8,256]{1,0:T(8,128)S(1)} %get-tuple-element.44.own_near), channel_id=1, source_target_pairs={{0,1},{1,0},{2,3},{3,2},{4,5},{5,4},{6,7},{7,6},{8,9},{9,8},{10,11... | collective-permute-start | bytes 24584 | tf_op jit(solution)/shard_map/ppermute | solution.py:367
  40.7 0.0 collective-permute-done.6.far
  40.8 1.1 %collective-permute-done.7.near = f32[8,256]{1,0:T(8,128)S(1)} collective-permute-done((f32[8,256]{1,0:T(8,128)S(1)}, f32[8,256]{1,0:T(8,128)S(1)}, u32[]{:S(2)}, u32[]{:S(2)}) %collective-permute-start.7) | collective-permute-done | bytes 8224 | tf_op jit(solution)/shard_map/ppermute | solution.py:367
  41.9 0.8 %shard_map.115 = f32[16,128]{1,0:T(8,128)} custom-call(f32[8,256]{1,0:T(8,128)S(1)} %get-tuple-element.43.own_far, f32[8,256]{1,0:T(8,128)S(1)} %get-tuple-element.44.own_near, f32[8,256]{1,0:T(8,128)S(1)} %collective-permute-done.6.far, f32[8,256]{1,0:T(8,128)S(1)} %collective-permute-done.7.near), custom_call_target="tpu_custom_call" | custom-call | tf_op jit(solution)/shard_map/pallas_call | solution.py:376
Async XLA Ops:
  2.5 29.8 %collective-permute-start = (f32[54,8,128]{2,1,0:T(8,128)S(1)}, f32[54,8,128]{2,1,0:T(8,128)S(1)}, u32[]{:S(2)}, u32[]{:S(2)}) collective-permute-start(f32[54,8,128]{2,1,0:T(8,128)S(1)} %get-tuple-element.31), channel_id=1, source_target_pairs={{1,2},{2,1},{3,4},{4,3},{5,6},{6,5},{7,8},{8,7},{9,10},{10,9},{11,... | collective-permute-start | bytes 663560 | tf_op jit(solution)/shard_map/ppermute | solution.py:367
  7.5 24.8 %collective-permute-start.1 = (f32[54,8,128]{2,1,0:T(8,128)S(1)}, f32[54,8,128]{2,1,0:T(8,128)S(1)}, u32[]{:S(2)}, u32[]{:S(2)}) collective-permute-start(f32[54,8,128]{2,1,0:T(8,128)S(1)} %get-tuple-element.32), channel_id=1, source_target_pairs={{0,1},{1,0},{2,3},{3,2},{4,5},{5,4},{6,7},{7,6},{8,9},{9,8},{10,11... | collective-permute-start | bytes 663560 | tf_op jit(solution)/shard_map/ppermute | solution.py:367
  19.3 2.6 %collective-permute-start.2 = (f32[14,16,128]{2,1,0:T(8,128)S(1)}, f32[14,16,128]{2,1,0:T(8,128)S(1)}, u32[]{:S(2)}, u32[]{:S(2)}) collective-permute-start(f32[14,16,128]{2,1,0:T(8,128)S(1)} %get-tuple-element.35), channel_id=1, source_target_pairs={{64,128},{128,64},{192,256},{256,192},{320,384},{384,320},{448,512... | collective-permute-start | bytes 344072 | tf_op jit(solution)/shard_map/ppermute | solution.py:402
  19.9 6.7 %collective-permute-start.3 = (f32[14,16,128]{2,1,0:T(8,128)S(1)}, f32[14,16,128]{2,1,0:T(8,128)S(1)}, u32[]{:S(2)}, u32[]{:S(2)}) collective-permute-start(f32[14,16,128]{2,1,0:T(8,128)S(1)} %get-tuple-element.36), channel_id=1, source_target_pairs={{0,64},{64,0},{128,192},{192,128},{256,320},{320,256},{384,448},{4... | collective-permute-start | bytes 344072 | tf_op jit(solution)/shard_map/ppermute | solution.py:403
  26.8 5.5 %collective-permute-start.4 = (f32[15,8,128]{2,1,0:T(8,128)S(1)}, f32[15,8,128]{2,1,0:T(8,128)S(1)}, u32[]{:S(2)}, u32[]{:S(2)}) collective-permute-start(f32[15,8,128]{2,1,0:T(8,128)S(1)} %get-tuple-element.39), channel_id=1, source_target_pairs={{1,2},{2,1},{3,4},{4,3},{5,6},{6,5},{7,8},{8,7},{9,10},{10,9},{11,... | collective-permute-start | bytes 184328 | tf_op jit(solution)/shard_map/ppermute | solution.py:367
  28.7 3.6 %collective-permute-start.5 = (f32[15,8,128]{2,1,0:T(8,128)S(1)}, f32[15,8,128]{2,1,0:T(8,128)S(1)}, u32[]{:S(2)}, u32[]{:S(2)}) collective-permute-start(f32[15,8,128]{2,1,0:T(8,128)S(1)} %get-tuple-element.40), channel_id=1, source_target_pairs={{0,1},{1,0},{2,3},{3,2},{4,5},{5,4},{6,7},{7,6},{8,9},{9,8},{10,11... | collective-permute-start | bytes 184328 | tf_op jit(solution)/shard_map/ppermute | solution.py:367
  35.7 5.1 %collective-permute-start.6 = (f32[8,256]{1,0:T(8,128)S(1)}, f32[8,256]{1,0:T(8,128)S(1)}, u32[]{:S(2)}, u32[]{:S(2)}) collective-permute-start(f32[8,256]{1,0:T(8,128)S(1)} %get-tuple-element.43.own_far), channel_id=1, source_target_pairs={{1,2},{2,1},{3,4},{4,3},{5,6},{6,5},{7,8},{8,7},{9,10},{10,9},{11,... | collective-permute-start | bytes 24584 | tf_op jit(solution)/shard_map/ppermute | solution.py:367
  38.8 3.1 %collective-permute-start.7 = (f32[8,256]{1,0:T(8,128)S(1)}, f32[8,256]{1,0:T(8,128)S(1)}, u32[]{:S(2)}, u32[]{:S(2)}) collective-permute-start(f32[8,256]{1,0:T(8,128)S(1)} %get-tuple-element.44.own_near), channel_id=1, source_target_pairs={{0,1},{1,0},{2,3},{3,2},{4,5},{5,4},{6,7},{7,6},{8,9},{9,8},{10,11... | collective-permute-start | bytes 24584 | tf_op jit(solution)/shard_map/ppermute | solution.py:367

commit v7 on v6

--- a/solution.py
+++ b/solution.py
@@ -17,6 +17,7 @@
 HALO = 4
 WRAP = ROWS + 8
 GROUPS = 13
+PACKED = 4 * GROUPS + 2
 VMEM = pltpu.VMEM
 LIMIT = 48 * 1024 * 1024
 
@@ -129,7 +130,7 @@
         gains[k] = jnp.where(row24 < 16, here, jnp.where(row24 < 20, up, down))
 
 
-def strip_kernel(own_right, own_left, first_got, second_got, strips, side, far, near):
+def strip_kernel(own_right, own_left, far_rows, near_rows, first_got, second_got, strips, side, far, near):
     col = lax.axis_index("gx")
     rightward = col % 2 == 1
     upward = lax.axis_index("gy") % 2 == 1
@@ -138,6 +139,9 @@
     within = lane % 16
     half = lane % 32 < 16
     low = rows_of(8) < 4
+
+    far[0:PACKED] = far_rows[...]
+    near[0:PACKED] = near_rows[...]
 
     def sides(g):
         from_right = jnp.where(rightward, first_got[g], second_got[g])
@@ -154,14 +158,14 @@
         strips[g, 1] = odd
         down = jnp.where(low, even[0:8], turn(odd[0:8], 4, 0))
         up = jnp.where(low, turn(odd[8:16], 4, 0), even[8:16])
-        far[g] = jnp.where(upward, up, down)
-        near[g] = jnp.where(upward, down, up)
+        far[PACKED + g] = jnp.where(upward, up, down)
+        near[PACKED + g] = jnp.where(upward, down, up)
     from_right, from_left = sides(GROUPS)
     beside = jnp.where(lane < 64, from_right, from_left)
     side[...] = beside
     for part in range(2):
-        far[GROUPS + part] = beside[8 * part : 8 * part + 8]
-        near[GROUPS + part] = beside[8 * part : 8 * part + 8]
+        far[PACKED + GROUPS + part] = beside[8 * part : 8 * part + 8]
+        near[PACKED + GROUPS + part] = beside[8 * part : 8 * part + 8]
 
 
 def unpack(far, near, pick, second):
@@ -172,7 +176,7 @@
 
 def main_kernel(
     gains, field, adjoint, source, adjoint_source, background, density,
-    far, near, strips, side, strip_far, strip_near,
+    far, near, strips, side,
     field_out, adjoint_out, local_far, local_near,
     fields, sources, curls, rate, keep, strip_fields, strip_sources, strip_curls, strip_rate, strip_keep, wide,
 ):
@@ -196,10 +200,10 @@
         wide[rows8, 0:LANES] = jnp.where(first_row, 0.0, jnp.where(upward, near[k], far[k]))
         rows8 = slice(32 + 8 * part, 40 + 8 * part)
         wide[rows8, 0:LANES] = jnp.where(last_row, 0.0, jnp.where(upward, far[k], near[k]))
-        k, rows8 = GROUPS + part, slice(8 * part, 8 * part + 8)
-        wide[rows8, LANES : 2 * LANES] = jnp.where(first_row, 0.0, jnp.where(upward, strip_near[k], strip_far[k]))
+        k, rows8 = PACKED + GROUPS + part, slice(8 * part, 8 * part + 8)
+        wide[rows8, LANES : 2 * LANES] = jnp.where(first_row, 0.0, jnp.where(upward, near[k], far[k]))
         rows8 = slice(32 + 8 * part, 40 + 8 * part)
-        wide[rows8, LANES : 2 * LANES] = jnp.where(last_row, 0.0, jnp.where(upward, strip_far[k], strip_near[k]))
+        wide[rows8, LANES : 2 * LANES] = jnp.where(last_row, 0.0, jnp.where(upward, far[k], near[k]))
     filtered = cone(lambda a: wide[8 + a : 40 + a], 32)
     low2 = lax.broadcasted_iota(jnp.int32, (8, 2 * LANES), 0) < 4
     filtered = jnp.concatenate(
@@ -227,7 +231,7 @@
         rate[z] = step
         keep[z] = 0.5 + 4.0 * step
     for t in range(2):
-        halo = unpack(strip_far[12], strip_near[12], pick, t)
+        halo = unpack(far[PACKED + 12], near[PACKED + 12], pick, t)
         step = 0.5 / (4.0 + 0.5 * (whole(strips[12, t], halo) + design_strip))
         step = jnp.where(outside_strip, 0.0, step)
         strip_rate[t] = step
@@ -245,7 +249,7 @@
                 else:
                     sources[f - 2, c, z] = whole(starts[f][c, z], halo)
             for t in range(2):
-                halo = unpack(strip_far[g], strip_near[g], pick, t)
+                halo = unpack(far[PACKED + g], near[PACKED + g], pick, t)
                 if f < 2:
                     strip_fields[f, c, t] = whole(strips[g, t], jnp.where(outside8, 0.0, halo))
                 else:
@@ -392,7 +396,7 @@
 def on_device(background, density, design_tiles, material_tiles, contrast, source, adjoint_source, field_start, adjoint_start):
     inner = (field_start, adjoint_start, source, adjoint_source, background, density)
     tiles = (design_tiles, material_tiles, contrast)
-    edges, rows = shape(GROUPS + 1, ROWS, LANES), shape(4 * GROUPS + 2, 8, LANES)
+    edges, rows, packed = shape(GROUPS + 1, ROWS, LANES), shape(PACKED, 8, LANES), shape(PACKED + GROUPS + 2, 8, LANES)
     first, second, own_right, own_left, far, near, gains, *inner = call(
         pack_kernel,
         [edges, edges, edges, edges, rows, rows, shape(3, WRAP, LANES)] + [shape(*a.shape) for a in inner],
@@ -401,12 +405,10 @@
     )(*[pltpu.with_memory_space_constraint(a, pltpu.HBM) for a in (*tiles, *inner)])
     first_got = lax.ppermute(first, "gx", swaps("gx", 1))
     second_got = lax.ppermute(second, "gx", swaps("gx", 0))
+    strips, side, far, near = call(strip_kernel, [shape(GROUPS, 2, ROWS, LANES), shape(ROWS, LANES), packed, packed])(
+        own_right, own_left, far, near, first_got, second_got
+    )
     far_got, near_got = swap_rows(far, near)
-    corner = shape(GROUPS + 2, 8, LANES)
-    strips, side, strip_far, strip_near = call(
-        strip_kernel, [shape(GROUPS, 2, ROWS, LANES), shape(ROWS, LANES), corner, corner]
-    )(own_right, own_left, first_got, second_got)
-    strip_far_got, strip_near_got = swap_rows(strip_far, strip_near)
     block, part = shape(3, Z, ROWS, LANES), shape(8, 2 * LANES)
     planes, sheets = (2, 3, Z, WRAP, LANES), (2, 3, 2, WRAP, LANES)
     field, adjoint, local_far, local_near = call(
@@ -417,7 +419,7 @@
             room(*sheets), room(*sheets), room(*sheets), room(2, WRAP, LANES), room(2, WRAP, LANES),
             room(48, 2 * LANES),
         ],
-    )(gains, *inner, far_got, near_got, strips, side, strip_far_got, strip_near_got)
+    )(gains, *inner, far_got, near_got, strips, side)
     local_far_got, local_near_got = swap_rows(local_far, local_near)
     gradient = call(gradient_kernel, shape(ROWS, LANES), scratch=[room(32, 2 * LANES)])(
         local_far, local_near, local_far_got, local_near_got

time: 43.1 us -> 37.4 us (0.87)
  waiting for transfers between devices: 7.54 us -> 4.46 us
  starting transfers between devices: 28.2 us -> 25.8 us
    ppermute x1, starting transfers between devices: 1.92 us -> 6.4 us  [on_device(): second_got = lax.ppermute(second, 'gx', swaps('gx', 0))]
    ppermute x3 -> x2, starting transfers between devices: 15.6 us -> 11.4 us  [swap_rows(): lax.ppermute(near, 'gy', swaps('gy', 0))]
    ppermute x3 -> x2, starting transfers between devices: 10 us -> 7.26 us  [swap_rows(): lax.ppermute(far, 'gy', swaps('gy', 1))]
    ppermute x1, waiting for transfers between devices: 4.72 us -> 2.16 us  [on_device(): second_got = lax.ppermute(second, 'gx', swaps('gx', 0))]
    ppermute x3 -> x2, waiting for transfers between devices: 1.69 us -> 1.12 us  [swap_rows(): lax.ppermute(far, 'gy', swaps('gy', 1))]
    ppermute x3 -> x2, waiting for transfers between devices: 1.13 us -> 1.18 us  [swap_rows(): lax.ppermute(near, 'gy', swaps('gy', 0))]
  transfers between devices with their start and end apart: 8 -> 6, of which waited for: 3 -> 3; matrix products, arithmetic and copies ran while one was open for 0% -> 0% of each run, Pallas kernels for 0% -> 0%
where the time goes in v7:
time: 37.4 us; the launch traced here: 37.1 us
  starting transfers between devices  25.8 us (69%)
  Pallas kernels  6.19 us (17%)
  waiting for transfers between devices  4.46 us (12%)
  between operations  0.72 us (2%)
    ppermute x2, starting transfers between devices, swap_rows(): lax.ppermute(near, 'gy', swaps('gy', 0))  11.4 us
    ppermute x2, starting transfers between devices, swap_rows(): lax.ppermute(far, 'gy', swaps('gy', 1))  7.26 us
    ppermute x1, starting transfers between devices, on_device(): second_got = lax.ppermute(second, 'gx', swaps('gx', 0))  6.4 us
    pallas_call x4, Pallas kernels, run(): pl.pallas_call(kernel, out_shape=outs, in_specs=[pl.BlockSpec(memory_spac...  6.19 us
    ppermute x1, waiting for transfers between devices, on_device(): second_got = lax.ppermute(second, 'gx', swaps('gx', 0))  2.16 us
    ppermute x2, waiting for transfers between devices, swap_rows(): lax.ppermute(near, 'gy', swaps('gy', 0))  1.18 us
    ppermute x2, waiting for transfers between devices, swap_rows(): lax.ppermute(far, 'gy', swaps('gy', 1))  1.12 us
  transfers between devices with their start and end apart: 6, of which 3 were waited for; matrix products, arithmetic and copies ran while one was open for 0% of the time, Pallas kernels for 0%

profile of v7, /device:TPU:1, one launch (start us, length us, event | category | flops | bytes accessed | tf_op | source)
XLA Modules:
  0.0 37.1 jit_solution(7385054185926318486)
XLA Ops:
  0.6 1.9 %shard_map.112 = (f32[14,16,128]{2,1,0:T(8,128)S(1)}, f32[14,16,128]{2,1,0:T(8,128)S(1)}, f32[14,16,128]{2,1,0:T(8,128)S(1)}, f32[14,16,128]{2,1,0:T(8,128)S(1)}...) custom-call(s32[8,16]{1,0:T(8,128)} %design_in.1, ...), custom_call_target="tpu_custom_call" | custom-call | tf_op jit(solution)/shard_map/pallas_call | solution.py:380
  2.5 0.7 %collective-permute-start = (f32[14,16,128]{2,1,0:T(8,128)S(1)}, f32[14,16,128]{2,1,0:T(8,128)S(1)}, u32[]{:S(2)}, u32[]{:S(2)}) collective-permute-start(f32[14,16,128]{2,1,0:T(8,128)S(1)} %get-tuple-element.35), channel_id=1, source_target_pairs={{64,128},{128,64},{192,256},{256,192},{320,384},{384,320},{448,512... | collective-permute-start | bytes 344072 | tf_op jit(solution)/shard_map/ppermute | solution.py:406
  3.2 6.4 %collective-permute-start.1 = (f32[14,16,128]{2,1,0:T(8,128)S(1)}, f32[14,16,128]{2,1,0:T(8,128)S(1)}, u32[]{:S(2)}, u32[]{:S(2)}) collective-permute-start(f32[14,16,128]{2,1,0:T(8,128)S(1)} %get-tuple-element.36), channel_id=1, source_target_pairs={{0,64},{64,0},{128,192},{192,128},{256,320},{320,256},{384,448},{4... | collective-permute-start | bytes 344072 | tf_op jit(solution)/shard_map/ppermute | solution.py:407
  9.6 0.0 collective-permute-done.first_got
  9.6 2.2 %collective-permute-done.1.second_got = f32[14,16,128]{2,1,0:T(8,128)S(1)} collective-permute-done((f32[14,16,128]{2,1,0:T(8,128)S(1)}, f32[14,16,128]{2,1,0:T(8,128)S(1)}, u32[]{:S(2)}, u32[]{:S(2)}) %collective-permute-start.1) | collective-permute-done | bytes 114720 | tf_op jit(solution)/shard_map/ppermute | solution.py:407
  11.8 0.1 shard_map.113
  11.9 5.3 %collective-permute-start.2 = (f32[69,8,128]{2,1,0:T(8,128)S(1)}, f32[69,8,128]{2,1,0:T(8,128)S(1)}, u32[]{:S(2)}, u32[]{:S(2)}) collective-permute-start(f32[69,8,128]{2,1,0:T(8,128)S(1)} %get-tuple-element.37), channel_id=1, source_target_pairs={{1,2},{2,1},{3,4},{4,3},{5,6},{6,5},{7,8},{8,7},{9,10},{10,9},{11,... | collective-permute-start | bytes 847880 | tf_op jit(solution)/shard_map/ppermute | solution.py:371
  17.3 9.5 %collective-permute-start.3 = (f32[69,8,128]{2,1,0:T(8,128)S(1)}, f32[69,8,128]{2,1,0:T(8,128)S(1)}, u32[]{:S(2)}, u32[]{:S(2)}) collective-permute-start(f32[69,8,128]{2,1,0:T(8,128)S(1)} %get-tuple-element.38), channel_id=1, source_target_pairs={{0,1},{1,0},{2,3},{3,2},{4,5},{5,4},{6,7},{7,6},{8,9},{9,8},{10,11... | collective-permute-start | bytes 847880 | tf_op jit(solution)/shard_map/ppermute | solution.py:371
  26.8 0.0 collective-permute-done.2.far
  26.8 1.2 %collective-permute-done.3.near = f32[69,8,128]{2,1,0:T(8,128)S(1)} collective-permute-done((f32[69,8,128]{2,1,0:T(8,128)S(1)}, f32[69,8,128]{2,1,0:T(8,128)S(1)}, u32[]{:S(2)}, u32[]{:S(2)}) %collective-permute-start.3) | collective-permute-done | bytes 282656 | tf_op jit(solution)/shard_map/ppermute | solution.py:371
  28.0 3.3 %shard_map.114 = (f32[3,8,16,128]{3,2,1,0:T(8,128)}, f32[3,8,16,128]{3,2,1,0:T(8,128)}, f32[8,256]{1,0:T(8,128)S(1)}, f32[8,256]{1,0:T(8,128)S(1)}) custom-call(f32[3,24,128]{2,1,0:T(8,128)S(1)} %get-tuple-element.24.gains, f32[3,8,16,128]{3,2,1,0:T(8,128)S(1)} %get-tuple-element.25.field, f32[3,8,16,128]{3,2,1,0:T(8,128)S(1)} %get-tuple-element.26.adjoint, ...), custom_call_target="tpu_custom_call" | custom-call | tf_op jit(solution)/shard_map/pallas_call | solution.py:380
  31.3 1.9 %collective-permute-start.4 = (f32[8,256]{1,0:T(8,128)S(1)}, f32[8,256]{1,0:T(8,128)S(1)}, u32[]{:S(2)}, u32[]{:S(2)}) collective-permute-start(f32[8,256]{1,0:T(8,128)S(1)} %get-tuple-element.43.own_far), channel_id=1, source_target_pairs={{1,2},{2,1},{3,4},{4,3},{5,6},{6,5},{7,8},{8,7},{9,10},{10,9},{11,... | collective-permute-start | bytes 24584 | tf_op jit(solution)/shard_map/ppermute | solution.py:371
  33.2 1.9 %collective-permute-start.5 = (f32[8,256]{1,0:T(8,128)S(1)}, f32[8,256]{1,0:T(8,128)S(1)}, u32[]{:S(2)}, u32[]{:S(2)}) collective-permute-start(f32[8,256]{1,0:T(8,128)S(1)} %get-tuple-element.44.own_near), channel_id=1, source_target_pairs={{0,1},{1,0},{2,3},{3,2},{4,5},{5,4},{6,7},{7,6},{8,9},{9,8},{10,11... | collective-permute-start | bytes 24584 | tf_op jit(solution)/shard_map/ppermute | solution.py:371
  35.1 1.1 %collective-permute-done.4.far = f32[8,256]{1,0:T(8,128)S(1)} collective-permute-done((f32[8,256]{1,0:T(8,128)S(1)}, f32[8,256]{1,0:T(8,128)S(1)}, u32[]{:S(2)}, u32[]{:S(2)}) %collective-permute-start.4) | collective-permute-done | bytes 8224 | tf_op jit(solution)/shard_map/ppermute | solution.py:371
  36.2 0.0 collective-permute-done.5.near
  36.3 0.8 %shard_map.115 = f32[16,128]{1,0:T(8,128)} custom-call(f32[8,256]{1,0:T(8,128)S(1)} %get-tuple-element.43.own_far, f32[8,256]{1,0:T(8,128)S(1)} %get-tuple-element.44.own_near, f32[8,256]{1,0:T(8,128)S(1)} %collective-permute-done.4.far, f32[8,256]{1,0:T(8,128)S(1)} %collective-permute-done.5.near), custom_call_target="tpu_custom_call" | custom-call | tf_op jit(solution)/shard_map/pallas_call | solution.py:380
Async XLA Ops:
  2.5 7.1 %collective-permute-start = (f32[14,16,128]{2,1,0:T(8,128)S(1)}, f32[14,16,128]{2,1,0:T(8,128)S(1)}, u32[]{:S(2)}, u32[]{:S(2)}) collective-permute-start(f32[14,16,128]{2,1,0:T(8,128)S(1)} %get-tuple-element.35), channel_id=1, source_target_pairs={{64,128},{128,64},{192,256},{256,192},{320,384},{384,320},{448,512... | collective-permute-start | bytes 344072 | tf_op jit(solution)/shard_map/ppermute | solution.py:406
  3.2 8.6 %collective-permute-start.1 = (f32[14,16,128]{2,1,0:T(8,128)S(1)}, f32[14,16,128]{2,1,0:T(8,128)S(1)}, u32[]{:S(2)}, u32[]{:S(2)}) collective-permute-start(f32[14,16,128]{2,1,0:T(8,128)S(1)} %get-tuple-element.36), channel_id=1, source_target_pairs={{0,64},{64,0},{128,192},{192,128},{256,320},{320,256},{384,448},{4... | collective-permute-start | bytes 344072 | tf_op jit(solution)/shard_map/ppermute | solution.py:407
  11.9 14.9 %collective-permute-start.2 = (f32[69,8,128]{2,1,0:T(8,128)S(1)}, f32[69,8,128]{2,1,0:T(8,128)S(1)}, u32[]{:S(2)}, u32[]{:S(2)}) collective-permute-start(f32[69,8,128]{2,1,0:T(8,128)S(1)} %get-tuple-element.37), channel_id=1, source_target_pairs={{1,2},{2,1},{3,4},{4,3},{5,6},{6,5},{7,8},{8,7},{9,10},{10,9},{11,... | collective-permute-start | bytes 847880 | tf_op jit(solution)/shard_map/ppermute | solution.py:371
  17.3 10.7 %collective-permute-start.3 = (f32[69,8,128]{2,1,0:T(8,128)S(1)}, f32[69,8,128]{2,1,0:T(8,128)S(1)}, u32[]{:S(2)}, u32[]{:S(2)}) collective-permute-start(f32[69,8,128]{2,1,0:T(8,128)S(1)} %get-tuple-element.38), channel_id=1, source_target_pairs={{0,1},{1,0},{2,3},{3,2},{4,5},{5,4},{6,7},{7,6},{8,9},{9,8},{10,11... | collective-permute-start | bytes 847880 | tf_op jit(solution)/shard_map/ppermute | solution.py:371
  31.3 5.0 %collective-permute-start.4 = (f32[8,256]{1,0:T(8,128)S(1)}, f32[8,256]{1,0:T(8,128)S(1)}, u32[]{:S(2)}, u32[]{:S(2)}) collective-permute-start(f32[8,256]{1,0:T(8,128)S(1)} %get-tuple-element.43.own_far), channel_id=1, source_target_pairs={{1,2},{2,1},{3,4},{4,3},{5,6},{6,5},{7,8},{8,7},{9,10},{10,9},{11,... | collective-permute-start | bytes 24584 | tf_op jit(solution)/shard_map/ppermute | solution.py:371
  33.2 3.1 %collective-permute-start.5 = (f32[8,256]{1,0:T(8,128)S(1)}, f32[8,256]{1,0:T(8,128)S(1)}, u32[]{:S(2)}, u32[]{:S(2)}) collective-permute-start(f32[8,256]{1,0:T(8,128)S(1)} %get-tuple-element.44.own_near), channel_id=1, source_target_pairs={{0,1},{1,0},{2,3},{3,2},{4,5},{5,4},{6,7},{7,6},{8,9},{9,8},{10,11... | collective-permute-start | bytes 24584 | tf_op jit(solution)/shard_map/ppermute | solution.py:371

commit v8 on v7

--- a/solution.py
+++ b/solution.py
@@ -84,17 +84,16 @@
         if g % 3 == 0:
             copies[g // 3].wait()
         planes = background if g == 12 else (field, adjoint, source, adjoint_source)[g // 3].at[g % 3]
-        to_right = to_left = None
-        for z in range(Z):
-            plane = planes[z]
-            here_right = turn(plane, 16 * z + 12, 1)
-            here_left = turn(plane, 16 * z + 4, 1)
-            if z == 0:
-                to_right, to_left = here_right, here_left
-            else:
-                chosen = lane >= 16 * z
-                to_right = jnp.where(chosen, here_right, to_right)
-                to_left = jnp.where(chosen, here_left, to_left)
+        windows = []
+        for t in range(2):
+            window = None
+            for q in range(Z // 2):
+                here = turn(planes[2 * q + t], 32 * q + 12, 1)
+                window = here if q == 0 else jnp.where(lane >= 32 * q, here, window)
+            windows.append(window)
+        half = lane % 32 < 16
+        to_right = jnp.where(half, windows[0], turn(windows[1], 16, 1))
+        to_left = jnp.where(half, turn(windows[0], -8, 1), turn(windows[1], 8, 1))
         own_right[g] = to_right
         own_left[g] = to_left
         first[g] = jnp.where(rightward, to_right, to_left)
@@ -177,8 +176,8 @@
 def main_kernel(
     gains, field, adjoint, source, adjoint_source, background, density,
     far, near, strips, side,
-    field_out, adjoint_out, local_far, local_near,
-    fields, sources, curls, rate, keep, strip_fields, strip_sources, strip_curls, strip_rate, strip_keep, wide,
+    fields, local_far, local_near,
+    sources, curls, rate, keep, strip_fields, strip_sources, strip_curls, strip_rate, strip_keep, wide,
 ):
     col, row = lax.axis_index("gx"), lax.axis_index("gy")
     cols, rows = lax.axis_size("gx"), lax.axis_size("gy")
@@ -269,7 +268,7 @@
     def behind_x(value, strip, z):
         return jnp.where(at_first, turn(strip[z % 2], -(32 * (z // 2) + 27), 1), turn(value, 1, 1))
 
-    def sweep():
+    def sweep(kept_rows):
         for f in range(2):
             ex, ey, ez = ([strip_fields[f, c, t] for t in range(2)] for c in range(3))
             for t in range(2):
@@ -318,20 +317,17 @@
                 curl_y = (hx - hx_z) - (hz - behind_x(hz, strip_curls.at[f, 2], z))
                 curl_z = (hy - behind_x(hy, strip_curls.at[f, 1], z)) - (hx - behind_y(hx))
                 step, kept = rate[z], keep[z]
-                fields[f, 0, z] = kept * ex + step * (sources[f, 0, z] - curl_x)
-                fields[f, 1, z] = kept * ey + step * (sources[f, 1, z] - curl_y)
-                fields[f, 2, z] = kept * ez + step * (sources[f, 2, z] - curl_z)
-    for _ in range(ITERS):
-        sweep()
+                fields[f, 0, z, 0:kept_rows] = (kept * ex + step * (sources[f, 0, z] - curl_x))[0:kept_rows]
+                fields[f, 1, z, 0:kept_rows] = (kept * ey + step * (sources[f, 1, z] - curl_y))[0:kept_rows]
+                fields[f, 2, z, 0:kept_rows] = (kept * ez + step * (sources[f, 2, z] - curl_z))[0:kept_rows]
+    for number in range(ITERS):
+        sweep(WRAP if number < ITERS - 1 else ROWS)
 
     product = jnp.zeros((ROWS, LANES), jnp.float32)
     strip_product = jnp.zeros((ROWS, LANES), jnp.float32)
     for c in range(3):
         for z in range(Z):
-            forward, backward = fields[0, c, z, 0:ROWS], fields[1, c, z, 0:ROWS]
-            field_out[c, z] = forward
-            adjoint_out[c, z] = backward
-            product = product + forward * backward
+            product = product + fields[0, c, z, 0:ROWS] * fields[1, c, z, 0:ROWS]
         for t in range(2):
             strip_product = strip_product + strip_fields[0, c, t, 0:ROWS] * strip_fields[1, c, t, 0:ROWS]
     strip_product = strip_product + turn(strip_product, 64, 1)
@@ -351,7 +347,13 @@
     return jnp.where(lane < 16, right_side, left_side)
 
 
-def gradient_kernel(own_far, own_near, far, near, gradient, wide):
+def last_kernel(fields, own_far, own_near, far, near, field, adjoint, gradient, wide, done):
+    copies = [
+        pltpu.make_async_copy(fields.at[f, :, :, pl.ds(0, ROWS)], out, done.at[f])
+        for f, out in enumerate((field, adjoint))
+    ]
+    for copy in copies:
+        copy.start()
     row = lax.axis_index("gy")
     upward = row % 2 == 1
     wide[0:8] = jnp.where(row == 0, 0.0, jnp.where(upward, near[...], far[...]))
@@ -359,6 +361,8 @@
     wide[16:24] = jnp.where(upward, own_far[...], own_near[...])
     wide[24:32] = jnp.where(row == lax.axis_size("gy") - 1, 0.0, jnp.where(upward, far[...], near[...]))
     gradient[...] = cone(lambda a: wide[8 + a : 24 + a], ROWS)[:, :LANES]
+    for copy in copies:
+        copy.wait()
 
 
 def swaps(axis, start):
@@ -375,13 +379,13 @@
     return jax.ShapeDtypeStruct(dims, jnp.float32)
 
 
-def call(kernel, outs, space=VMEM, scratch=()):
+def call(kernel, outs, space=VMEM, scratch=(), places=None):
     def run(*operands):
         return pl.pallas_call(
             kernel,
             out_shape=outs,
             in_specs=[pl.BlockSpec(memory_space=space)] * len(operands),
-            out_specs=jax.tree.map(lambda _: pl.BlockSpec(memory_space=VMEM), outs),
+            out_specs=[pl.BlockSpec(memory_space=place) for place in places or [VMEM] * len(outs)],
             scratch_shapes=scratch,
             compiler_params=pltpu.CompilerParams(vmem_limit_bytes=LIMIT),
         )(*operands)
@@ -411,19 +415,22 @@
     far_got, near_got = swap_rows(far, near)
     block, part = shape(3, Z, ROWS, LANES), shape(8, 2 * LANES)
     planes, sheets = (2, 3, Z, WRAP, LANES), (2, 3, 2, WRAP, LANES)
-    field, adjoint, local_far, local_near = call(
+    fields, local_far, local_near = call(
         main_kernel,
-        [block, block, part, part],
+        [room(*planes), part, part],
         scratch=[
-            room(*planes), room(*planes), room(*planes), room(Z, WRAP, LANES), room(Z, WRAP, LANES),
+            room(*planes), room(*planes), room(Z, WRAP, LANES), room(Z, WRAP, LANES),
             room(*sheets), room(*sheets), room(*sheets), room(2, WRAP, LANES), room(2, WRAP, LANES),
             room(48, 2 * LANES),
         ],
     )(gains, *inner, far_got, near_got, strips, side)
     local_far_got, local_near_got = swap_rows(local_far, local_near)
-    gradient = call(gradient_kernel, shape(ROWS, LANES), scratch=[room(32, 2 * LANES)])(
-        local_far, local_near, local_far_got, local_near_got
-    )
+    field, adjoint, gradient = call(
+        last_kernel,
+        [block, block, shape(ROWS, LANES)],
+        places=(pltpu.HBM, pltpu.HBM, VMEM),
+        scratch=[room(32, 2 * LANES), pltpu.SemaphoreType.DMA((2,))],
+    )(fields, local_far, local_near, local_far_got, local_near_got)
     return (field, adjoint, gradient)
 
 

time: 37.4 us -> 37.4 us (level)
  no operation moved by 1% of the time
where the time goes in v8:
time: 37.4 us; the launch traced here: 37.1 us
  starting transfers between devices  25.8 us (69%)
  Pallas kernels  6.2 us (17%)
  waiting for transfers between devices  4.46 us (12%)
  between operations  0.72 us (2%)
    ppermute x2, starting transfers between devices, swap_rows(): lax.ppermute(near, 'gy', swaps('gy', 0))  11.4 us
    ppermute x2, starting transfers between devices, swap_rows(): lax.ppermute(far, 'gy', swaps('gy', 1))  7.27 us
    ppermute x1, starting transfers between devices, on_device(): second_got = lax.ppermute(second, 'gx', swaps('gx', 0))  6.4 us
    pallas_call x4, Pallas kernels, run(): pl.pallas_call(kernel, out_shape=outs, in_specs=[pl.BlockSpec(memory_spac...  6.2 us
    ppermute x1, waiting for transfers between devices, on_device(): second_got = lax.ppermute(second, 'gx', swaps('gx', 0))  2.16 us
    ppermute x2, waiting for transfers between devices, swap_rows(): lax.ppermute(near, 'gy', swaps('gy', 0))  1.18 us
    ppermute x2, waiting for transfers between devices, swap_rows(): lax.ppermute(far, 'gy', swaps('gy', 1))  1.12 us
  transfers between devices with their start and end apart: 6, of which 3 were waited for; matrix products, arithmetic and copies ran while one was open for 0% of the time, Pallas kernels for 0%

profile of v8, /device:TPU:1, one launch (start us, length us, event | category | flops | bytes accessed | tf_op | source)
XLA Modules:
  0.0 37.1 jit_solution(4235116800850595334)
XLA Ops:
  0.6 2.0 %shard_map.112 = (f32[14,16,128]{2,1,0:T(8,128)S(1)}, f32[14,16,128]{2,1,0:T(8,128)S(1)}, f32[14,16,128]{2,1,0:T(8,128)S(1)}, f32[14,16,128]{2,1,0:T(8,128)S(1)}...) custom-call(s32[8,16]{1,0:T(8,128)} %design_in.1, ...), custom_call_target="tpu_custom_call" | custom-call | tf_op jit(solution)/shard_map/pallas_call | solution.py:384
  2.7 0.7 %collective-permute-start = (f32[14,16,128]{2,1,0:T(8,128)S(1)}, f32[14,16,128]{2,1,0:T(8,128)S(1)}, u32[]{:S(2)}, u32[]{:S(2)}) collective-permute-start(f32[14,16,128]{2,1,0:T(8,128)S(1)} %get-tuple-element.34), channel_id=1, source_target_pairs={{64,128},{128,64},{192,256},{256,192},{320,384},{384,320},{448,512... | collective-permute-start | bytes 344072 | tf_op jit(solution)/shard_map/ppermute | solution.py:410
  3.3 6.4 %collective-permute-start.1 = (f32[14,16,128]{2,1,0:T(8,128)S(1)}, f32[14,16,128]{2,1,0:T(8,128)S(1)}, u32[]{:S(2)}, u32[]{:S(2)}) collective-permute-start(f32[14,16,128]{2,1,0:T(8,128)S(1)} %get-tuple-element.35), channel_id=1, source_target_pairs={{0,64},{64,0},{128,192},{192,128},{256,320},{320,256},{384,448},{4... | collective-permute-start | bytes 344072 | tf_op jit(solution)/shard_map/ppermute | solution.py:411
  9.8 0.0 collective-permute-done.first_got
  9.8 2.2 %collective-permute-done.1.second_got = f32[14,16,128]{2,1,0:T(8,128)S(1)} collective-permute-done((f32[14,16,128]{2,1,0:T(8,128)S(1)}, f32[14,16,128]{2,1,0:T(8,128)S(1)}, u32[]{:S(2)}, u32[]{:S(2)}) %collective-permute-start.1) | collective-permute-done | bytes 114720 | tf_op jit(solution)/shard_map/ppermute | solution.py:411
  11.9 0.1 shard_map.113
  12.1 5.3 %collective-permute-start.2 = (f32[69,8,128]{2,1,0:T(8,128)S(1)}, f32[69,8,128]{2,1,0:T(8,128)S(1)}, u32[]{:S(2)}, u32[]{:S(2)}) collective-permute-start(f32[69,8,128]{2,1,0:T(8,128)S(1)} %get-tuple-element.36), channel_id=1, source_target_pairs={{1,2},{2,1},{3,4},{4,3},{5,6},{6,5},{7,8},{8,7},{9,10},{10,9},{11,... | collective-permute-start | bytes 847880 | tf_op jit(solution)/shard_map/ppermute | solution.py:375
  17.4 9.5 %collective-permute-start.3 = (f32[69,8,128]{2,1,0:T(8,128)S(1)}, f32[69,8,128]{2,1,0:T(8,128)S(1)}, u32[]{:S(2)}, u32[]{:S(2)}) collective-permute-start(f32[69,8,128]{2,1,0:T(8,128)S(1)} %get-tuple-element.37), channel_id=1, source_target_pairs={{0,1},{1,0},{2,3},{3,2},{4,5},{5,4},{6,7},{7,6},{8,9},{9,8},{10,11... | collective-permute-start | bytes 847880 | tf_op jit(solution)/shard_map/ppermute | solution.py:375
  26.9 0.0 collective-permute-done.2.far
  27.0 1.2 %collective-permute-done.3.near = f32[69,8,128]{2,1,0:T(8,128)S(1)} collective-permute-done((f32[69,8,128]{2,1,0:T(8,128)S(1)}, f32[69,8,128]{2,1,0:T(8,128)S(1)}, u32[]{:S(2)}, u32[]{:S(2)}) %collective-permute-start.3) | collective-permute-done | bytes 282656 | tf_op jit(solution)/shard_map/ppermute | solution.py:375
  28.1 2.6 %shard_map.114 = (f32[2,3,8,24,128]{4,3,2,1,0:T(8,128)S(1)}, f32[8,256]{1,0:T(8,128)S(1)}, f32[8,256]{1,0:T(8,128)S(1)}) custom-call(f32[3,24,128]{2,1,0:T(8,128)S(1)} %get-tuple-element.23.gains, f32[3,8,16,128]{3,2,1,0:T(8,128)S(1)} %get-tuple-element.24.field, f32[3,8,16,128]{3,2,1,0:T(8,128)S(1)} %get-tuple-element.25.adjoint, ...), custom_call_target="tpu_custom_call" | custom-call | tf_op jit(solution)/shard_map/pallas_call | solution.py:384
  30.7 1.9 %collective-permute-start.4 = (f32[8,256]{1,0:T(8,128)S(1)}, f32[8,256]{1,0:T(8,128)S(1)}, u32[]{:S(2)}, u32[]{:S(2)}) collective-permute-start(f32[8,256]{1,0:T(8,128)S(1)} %get-tuple-element.41.own_far), channel_id=1, source_target_pairs={{1,2},{2,1},{3,4},{4,3},{5,6},{6,5},{7,8},{8,7},{9,10},{10,9},{11,... | collective-permute-start | bytes 24584 | tf_op jit(solution)/shard_map/ppermute | solution.py:375
  32.6 1.9 %collective-permute-start.5 = (f32[8,256]{1,0:T(8,128)S(1)}, f32[8,256]{1,0:T(8,128)S(1)}, u32[]{:S(2)}, u32[]{:S(2)}) collective-permute-start(f32[8,256]{1,0:T(8,128)S(1)} %get-tuple-element.42.own_near), channel_id=1, source_target_pairs={{0,1},{1,0},{2,3},{3,2},{4,5},{5,4},{6,7},{7,6},{8,9},{9,8},{10,11... | collective-permute-start | bytes 24584 | tf_op jit(solution)/shard_map/ppermute | solution.py:375
  34.6 1.1 %collective-permute-done.4.far = f32[8,256]{1,0:T(8,128)S(1)} collective-permute-done((f32[8,256]{1,0:T(8,128)S(1)}, f32[8,256]{1,0:T(8,128)S(1)}, u32[]{:S(2)}, u32[]{:S(2)}) %collective-permute-start.4) | collective-permute-done | bytes 8224 | tf_op jit(solution)/shard_map/ppermute | solution.py:375
  35.7 0.0 collective-permute-done.5.near
  35.7 1.4 %shard_map.115 = (f32[3,8,16,128]{3,2,1,0:T(8,128)}, f32[3,8,16,128]{3,2,1,0:T(8,128)}, f32[16,128]{1,0:T(8,128)}) custom-call(f32[2,3,8,24,128]{4,3,2,1,0:T(8,128)S(1)} %get-tuple-element.40.fields, f32[8,256]{1,0:T(8,128)S(1)} %get-tuple-element.41.own_far, f32[8,256]{1,0:T(8,128)S(1)} %get-tuple-element.42.own_near, ...), custom_call_target="tpu_custom_call" | custom-call | tf_op jit(solution)/shard_map/pallas_call | solution.py:384
Async XLA Ops:
  2.7 7.1 %collective-permute-start = (f32[14,16,128]{2,1,0:T(8,128)S(1)}, f32[14,16,128]{2,1,0:T(8,128)S(1)}, u32[]{:S(2)}, u32[]{:S(2)}) collective-permute-start(f32[14,16,128]{2,1,0:T(8,128)S(1)} %get-tuple-element.34), channel_id=1, source_target_pairs={{64,128},{128,64},{192,256},{256,192},{320,384},{384,320},{448,512... | collective-permute-start | bytes 344072 | tf_op jit(solution)/shard_map/ppermute | solution.py:410
  3.3 8.6 %collective-permute-start.1 = (f32[14,16,128]{2,1,0:T(8,128)S(1)}, f32[14,16,128]{2,1,0:T(8,128)S(1)}, u32[]{:S(2)}, u32[]{:S(2)}) collective-permute-start(f32[14,16,128]{2,1,0:T(8,128)S(1)} %get-tuple-element.35), channel_id=1, source_target_pairs={{0,64},{64,0},{128,192},{192,128},{256,320},{320,256},{384,448},{4... | collective-permute-start | bytes 344072 | tf_op jit(solution)/shard_map/ppermute | solution.py:411
  12.1 14.9 %collective-permute-start.2 = (f32[69,8,128]{2,1,0:T(8,128)S(1)}, f32[69,8,128]{2,1,0:T(8,128)S(1)}, u32[]{:S(2)}, u32[]{:S(2)}) collective-permute-start(f32[69,8,128]{2,1,0:T(8,128)S(1)} %get-tuple-element.36), channel_id=1, source_target_pairs={{1,2},{2,1},{3,4},{4,3},{5,6},{6,5},{7,8},{8,7},{9,10},{10,9},{11,... | collective-permute-start | bytes 847880 | tf_op jit(solution)/shard_map/ppermute | solution.py:375
  17.4 10.7 %collective-permute-start.3 = (f32[69,8,128]{2,1,0:T(8,128)S(1)}, f32[69,8,128]{2,1,0:T(8,128)S(1)}, u32[]{:S(2)}, u32[]{:S(2)}) collective-permute-start(f32[69,8,128]{2,1,0:T(8,128)S(1)} %get-tuple-element.37), channel_id=1, source_target_pairs={{0,1},{1,0},{2,3},{3,2},{4,5},{5,4},{6,7},{7,6},{8,9},{9,8},{10,11... | collective-permute-start | bytes 847880 | tf_op jit(solution)/shard_map/ppermute | solution.py:375
  30.7 5.0 %collective-permute-start.4 = (f32[8,256]{1,0:T(8,128)S(1)}, f32[8,256]{1,0:T(8,128)S(1)}, u32[]{:S(2)}, u32[]{:S(2)}) collective-permute-start(f32[8,256]{1,0:T(8,128)S(1)} %get-tuple-element.41.own_far), channel_id=1, source_target_pairs={{1,2},{2,1},{3,4},{4,3},{5,6},{6,5},{7,8},{8,7},{9,10},{10,9},{11,... | collective-permute-start | bytes 24584 | tf_op jit(solution)/shard_map/ppermute | solution.py:375
  32.6 3.1 %collective-permute-start.5 = (f32[8,256]{1,0:T(8,128)S(1)}, f32[8,256]{1,0:T(8,128)S(1)}, u32[]{:S(2)}, u32[]{:S(2)}) collective-permute-start(f32[8,256]{1,0:T(8,128)S(1)} %get-tuple-element.42.own_near), channel_id=1, source_target_pairs={{0,1},{1,0},{2,3},{3,2},{4,5},{5,4},{6,7},{7,6},{8,9},{9,8},{10,11... | collective-permute-start | bytes 24584 | tf_op jit(solution)/shard_map/ppermute | solution.py:375

commit v9 on v8

--- a/solution.py
+++ b/solution.py
@@ -77,7 +77,7 @@
     for copy in copies:
         copy.start()
     lane = lanes_of(ROWS)
-    rightward = lax.axis_index("gx") % 2 == 1
+    rightward = lax.axis_index("gx") % 2 == 0
     upward = lax.axis_index("gy") % 2 == 1
     low = rows_of(8) < 4
     for g in range(GROUPS):
@@ -131,7 +131,7 @@
 
 def strip_kernel(own_right, own_left, far_rows, near_rows, first_got, second_got, strips, side, far, near):
     col = lax.axis_index("gx")
-    rightward = col % 2 == 1
+    rightward = col % 2 == 0
     upward = lax.axis_index("gy") % 2 == 1
     first, last = col == 0, col == lax.axis_size("gx") - 1
     lane = lanes_of(ROWS)
@@ -347,7 +347,7 @@
     return jnp.where(lane < 16, right_side, left_side)
 
 
-def last_kernel(fields, own_far, own_near, far, near, field, adjoint, gradient, wide, done):
+def last_kernel(fields, own_far, own_near, far, near, field, adjoint, gradient, wide, result, done):
     copies = [
         pltpu.make_async_copy(fields.at[f, :, :, pl.ds(0, ROWS)], out, done.at[f])
         for f, out in enumerate((field, adjoint))
@@ -360,7 +360,9 @@
     wide[8:16] = jnp.where(upward, own_near[...], own_far[...])
     wide[16:24] = jnp.where(upward, own_far[...], own_near[...])
     wide[24:32] = jnp.where(row == lax.axis_size("gy") - 1, 0.0, jnp.where(upward, far[...], near[...]))
-    gradient[...] = cone(lambda a: wide[8 + a : 24 + a], ROWS)[:, :LANES]
+    result[...] = cone(lambda a: wide[8 + a : 24 + a], ROWS)[:, :LANES]
+    copies.append(pltpu.make_async_copy(result, gradient, done.at[2]))
+    copies[2].start()
     for copy in copies:
         copy.wait()
 
@@ -407,8 +409,8 @@
         space=pltpu.HBM,
         scratch=[pltpu.SMEM(a.shape, a.dtype) for a in tiles] + [pltpu.SemaphoreType.DMA((9,))],
     )(*[pltpu.with_memory_space_constraint(a, pltpu.HBM) for a in (*tiles, *inner)])
-    first_got = lax.ppermute(first, "gx", swaps("gx", 1))
-    second_got = lax.ppermute(second, "gx", swaps("gx", 0))
+    first_got = lax.ppermute(first, "gx", swaps("gx", 0))
+    second_got = lax.ppermute(second, "gx", swaps("gx", 1))
     strips, side, far, near = call(strip_kernel, [shape(GROUPS, 2, ROWS, LANES), shape(ROWS, LANES), packed, packed])(
         own_right, own_left, far, near, first_got, second_got
     )
@@ -428,8 +430,8 @@
     field, adjoint, gradient = call(
         last_kernel,
         [block, block, shape(ROWS, LANES)],
-        places=(pltpu.HBM, pltpu.HBM, VMEM),
-        scratch=[room(32, 2 * LANES), pltpu.SemaphoreType.DMA((2,))],
+        places=(pltpu.HBM,) * 3,
+        scratch=[room(32, 2 * LANES), room(ROWS, LANES), pltpu.SemaphoreType.DMA((3,))],
     )(fields, local_far, local_near, local_far_got, local_near_got)
     return (field, adjoint, gradient)
 

time: 37.4 us -> 37.8 us (1.011)
  the two profiles are of different devices: /device:TPU:1 before, /device:TPU:3 now
where the time goes in v9:
time: 37.8 us; the launch traced here: 37.5 us
  starting transfers between devices  26.7 us (71%)
  Pallas kernels  5.64 us (15%)
  waiting for transfers between devices  4.46 us (12%)
  between operations  0.72 us (2%)
    ppermute x2, starting transfers between devices, swap_rows(): lax.ppermute(near, 'gy', swaps('gy', 0))  13.5 us
    ppermute x2, starting transfers between devices, swap_rows(): lax.ppermute(far, 'gy', swaps('gy', 1))  7.27 us
    pallas_call x4, Pallas kernels, run(): pl.pallas_call(kernel, out_shape=outs, in_specs=[pl.BlockSpec(memory_spac...  5.64 us
    ppermute x1, starting transfers between devices, on_device(): second_got = lax.ppermute(second, 'gx', swaps('gx', 1))  4.02 us
    ppermute x1, waiting for transfers between devices, on_device(): second_got = lax.ppermute(second, 'gx', swaps('gx', 1))  2.16 us
    ppermute x1, starting transfers between devices, on_device(): first_got = lax.ppermute(first, 'gx', swaps('gx', 0))  1.92 us
    ppermute x2, waiting for transfers between devices, swap_rows(): lax.ppermute(near, 'gy', swaps('gy', 0))  1.18 us
    ppermute x2, waiting for transfers between devices, swap_rows(): lax.ppermute(far, 'gy', swaps('gy', 1))  1.12 us
  transfers between devices with their start and end apart: 6, of which 3 were waited for; matrix products, arithmetic and copies ran while one was open for 0% of the time, Pallas kernels for 0%

profile of v9, /device:TPU:3, one launch (start us, length us, event | category | flops | bytes accessed | tf_op | source)
XLA Modules:
  0.0 37.5 jit_solution(4529339754993863027)
XLA Ops:
  0.6 2.0 %shard_map.112 = (f32[14,16,128]{2,1,0:T(8,128)S(1)}, f32[14,16,128]{2,1,0:T(8,128)S(1)}, f32[14,16,128]{2,1,0:T(8,128)S(1)}, f32[14,16,128]{2,1,0:T(8,128)S(1)}...) custom-call(s32[8,16]{1,0:T(8,128)} %design_in.1, ...), custom_call_target="tpu_custom_call" | custom-call | tf_op jit(solution)/shard_map/pallas_call | solution.py:386
  2.7 1.9 %collective-permute-start = (f32[14,16,128]{2,1,0:T(8,128)S(1)}, f32[14,16,128]{2,1,0:T(8,128)S(1)}, u32[]{:S(2)}, u32[]{:S(2)}) collective-permute-start(f32[14,16,128]{2,1,0:T(8,128)S(1)} %get-tuple-element.34), channel_id=1, source_target_pairs={{0,64},{64,0},{128,192},{192,128},{256,320},{320,256},{384,448},{4... | collective-permute-start | bytes 344072 | tf_op jit(solution)/shard_map/ppermute | solution.py:412
  4.6 4.0 %collective-permute-start.1 = (f32[14,16,128]{2,1,0:T(8,128)S(1)}, f32[14,16,128]{2,1,0:T(8,128)S(1)}, u32[]{:S(2)}, u32[]{:S(2)}) collective-permute-start(f32[14,16,128]{2,1,0:T(8,128)S(1)} %get-tuple-element.35), channel_id=1, source_target_pairs={{64,128},{128,64},{192,256},{256,192},{320,384},{384,320},{448,512... | collective-permute-start | bytes 344072 | tf_op jit(solution)/shard_map/ppermute | solution.py:413
  8.6 0.0 collective-permute-done.first_got
  8.6 2.2 %collective-permute-done.1.second_got = f32[14,16,128]{2,1,0:T(8,128)S(1)} collective-permute-done((f32[14,16,128]{2,1,0:T(8,128)S(1)}, f32[14,16,128]{2,1,0:T(8,128)S(1)}, u32[]{:S(2)}, u32[]{:S(2)}) %collective-permute-start.1) | collective-permute-done | bytes 114720 | tf_op jit(solution)/shard_map/ppermute | solution.py:413
  10.8 0.1 shard_map.113
  11.0 5.3 %collective-permute-start.2 = (f32[69,8,128]{2,1,0:T(8,128)S(1)}, f32[69,8,128]{2,1,0:T(8,128)S(1)}, u32[]{:S(2)}, u32[]{:S(2)}) collective-permute-start(f32[69,8,128]{2,1,0:T(8,128)S(1)} %get-tuple-element.36), channel_id=1, source_target_pairs={{1,2},{2,1},{3,4},{4,3},{5,6},{6,5},{7,8},{8,7},{9,10},{10,9},{11,... | collective-permute-start | bytes 847880 | tf_op jit(solution)/shard_map/ppermute | solution.py:377
  16.3 11.6 %collective-permute-start.3 = (f32[69,8,128]{2,1,0:T(8,128)S(1)}, f32[69,8,128]{2,1,0:T(8,128)S(1)}, u32[]{:S(2)}, u32[]{:S(2)}) collective-permute-start(f32[69,8,128]{2,1,0:T(8,128)S(1)} %get-tuple-element.37), channel_id=1, source_target_pairs={{0,1},{1,0},{2,3},{3,2},{4,5},{5,4},{6,7},{7,6},{8,9},{9,8},{10,11... | collective-permute-start | bytes 847880 | tf_op jit(solution)/shard_map/ppermute | solution.py:377
  27.9 0.0 collective-permute-done.2.far
  27.9 1.2 %collective-permute-done.3.near = f32[69,8,128]{2,1,0:T(8,128)S(1)} collective-permute-done((f32[69,8,128]{2,1,0:T(8,128)S(1)}, f32[69,8,128]{2,1,0:T(8,128)S(1)}, u32[]{:S(2)}, u32[]{:S(2)}) %collective-permute-start.3) | collective-permute-done | bytes 282656 | tf_op jit(solution)/shard_map/ppermute | solution.py:377
  29.1 2.6 %shard_map.114 = (f32[2,3,8,24,128]{4,3,2,1,0:T(8,128)S(1)}, f32[8,256]{1,0:T(8,128)S(1)}, f32[8,256]{1,0:T(8,128)S(1)}) custom-call(f32[3,24,128]{2,1,0:T(8,128)S(1)} %get-tuple-element.23.gains, f32[3,8,16,128]{3,2,1,0:T(8,128)S(1)} %get-tuple-element.24.field, f32[3,8,16,128]{3,2,1,0:T(8,128)S(1)} %get-tuple-element.25.adjoint, ...), custom_call_target="tpu_custom_call" | custom-call | tf_op jit(solution)/shard_map/pallas_call | solution.py:386
  31.7 1.9 %collective-permute-start.4 = (f32[8,256]{1,0:T(8,128)S(1)}, f32[8,256]{1,0:T(8,128)S(1)}, u32[]{:S(2)}, u32[]{:S(2)}) collective-permute-start(f32[8,256]{1,0:T(8,128)S(1)} %get-tuple-element.41.own_far), channel_id=1, source_target_pairs={{1,2},{2,1},{3,4},{4,3},{5,6},{6,5},{7,8},{8,7},{9,10},{10,9},{11,... | collective-permute-start | bytes 24584 | tf_op jit(solution)/shard_map/ppermute | solution.py:377
  33.6 1.9 %collective-permute-start.5 = (f32[8,256]{1,0:T(8,128)S(1)}, f32[8,256]{1,0:T(8,128)S(1)}, u32[]{:S(2)}, u32[]{:S(2)}) collective-permute-start(f32[8,256]{1,0:T(8,128)S(1)} %get-tuple-element.42.own_near), channel_id=1, source_target_pairs={{0,1},{1,0},{2,3},{3,2},{4,5},{5,4},{6,7},{7,6},{8,9},{9,8},{10,11... | collective-permute-start | bytes 24584 | tf_op jit(solution)/shard_map/ppermute | solution.py:377
  35.5 1.1 %collective-permute-done.4.far = f32[8,256]{1,0:T(8,128)S(1)} collective-permute-done((f32[8,256]{1,0:T(8,128)S(1)}, f32[8,256]{1,0:T(8,128)S(1)}, u32[]{:S(2)}, u32[]{:S(2)}) %collective-permute-start.4) | collective-permute-done | bytes 8224 | tf_op jit(solution)/shard_map/ppermute | solution.py:377
  36.6 0.0 collective-permute-done.5.near
  36.7 0.9 %shard_map.115 = (f32[3,8,16,128]{3,2,1,0:T(8,128)}, f32[3,8,16,128]{3,2,1,0:T(8,128)}, f32[16,128]{1,0:T(8,128)}) custom-call(f32[2,3,8,24,128]{4,3,2,1,0:T(8,128)S(1)} %get-tuple-element.40.fields, f32[8,256]{1,0:T(8,128)S(1)} %get-tuple-element.41.own_far, f32[8,256]{1,0:T(8,128)S(1)} %get-tuple-element.42.own_near, ...), custom_call_target="tpu_custom_call" | custom-call | tf_op jit(solution)/shard_map/pallas_call | solution.py:386
Async XLA Ops:
  2.7 6.0 %collective-permute-start = (f32[14,16,128]{2,1,0:T(8,128)S(1)}, f32[14,16,128]{2,1,0:T(8,128)S(1)}, u32[]{:S(2)}, u32[]{:S(2)}) collective-permute-start(f32[14,16,128]{2,1,0:T(8,128)S(1)} %get-tuple-element.34), channel_id=1, source_target_pairs={{0,64},{64,0},{128,192},{192,128},{256,320},{320,256},{384,448},{4... | collective-permute-start | bytes 344072 | tf_op jit(solution)/shard_map/ppermute | solution.py:412
  4.6 6.2 %collective-permute-start.1 = (f32[14,16,128]{2,1,0:T(8,128)S(1)}, f32[14,16,128]{2,1,0:T(8,128)S(1)}, u32[]{:S(2)}, u32[]{:S(2)}) collective-permute-start(f32[14,16,128]{2,1,0:T(8,128)S(1)} %get-tuple-element.35), channel_id=1, source_target_pairs={{64,128},{128,64},{192,256},{256,192},{320,384},{384,320},{448,512... | collective-permute-start | bytes 344072 | tf_op jit(solution)/shard_map/ppermute | solution.py:413
  11.0 16.9 %collective-permute-start.2 = (f32[69,8,128]{2,1,0:T(8,128)S(1)}, f32[69,8,128]{2,1,0:T(8,128)S(1)}, u32[]{:S(2)}, u32[]{:S(2)}) collective-permute-start(f32[69,8,128]{2,1,0:T(8,128)S(1)} %get-tuple-element.36), channel_id=1, source_target_pairs={{1,2},{2,1},{3,4},{4,3},{5,6},{6,5},{7,8},{8,7},{9,10},{10,9},{11,... | collective-permute-start | bytes 847880 | tf_op jit(solution)/shard_map/ppermute | solution.py:377
  16.3 12.7 %collective-permute-start.3 = (f32[69,8,128]{2,1,0:T(8,128)S(1)}, f32[69,8,128]{2,1,0:T(8,128)S(1)}, u32[]{:S(2)}, u32[]{:S(2)}) collective-permute-start(f32[69,8,128]{2,1,0:T(8,128)S(1)} %get-tuple-element.37), channel_id=1, source_target_pairs={{0,1},{1,0},{2,3},{3,2},{4,5},{5,4},{6,7},{7,6},{8,9},{9,8},{10,11... | collective-permute-start | bytes 847880 | tf_op jit(solution)/shard_map/ppermute | solution.py:377
  31.7 5.0 %collective-permute-start.4 = (f32[8,256]{1,0:T(8,128)S(1)}, f32[8,256]{1,0:T(8,128)S(1)}, u32[]{:S(2)}, u32[]{:S(2)}) collective-permute-start(f32[8,256]{1,0:T(8,128)S(1)} %get-tuple-element.41.own_far), channel_id=1, source_target_pairs={{1,2},{2,1},{3,4},{4,3},{5,6},{6,5},{7,8},{8,7},{9,10},{10,9},{11,... | collective-permute-start | bytes 24584 | tf_op jit(solution)/shard_map/ppermute | solution.py:377
  33.6 3.1 %collective-permute-start.5 = (f32[8,256]{1,0:T(8,128)S(1)}, f32[8,256]{1,0:T(8,128)S(1)}, u32[]{:S(2)}, u32[]{:S(2)}) collective-permute-start(f32[8,256]{1,0:T(8,128)S(1)} %get-tuple-element.42.own_near), channel_id=1, source_target_pairs={{0,1},{1,0},{2,3},{3,2},{4,5},{5,4},{6,7},{7,6},{8,9},{9,8},{10,11... | collective-permute-start | bytes 24584 | tf_op jit(solution)/shard_map/ppermute | solution.py:377

commit v10 on v9

--- a/solution.py
+++ b/solution.py
@@ -77,7 +77,7 @@
     for copy in copies:
         copy.start()
     lane = lanes_of(ROWS)
-    rightward = lax.axis_index("gx") % 2 == 0
+    rightward = lax.axis_index("gx") % 2 == 1
     upward = lax.axis_index("gy") % 2 == 1
     low = rows_of(8) < 4
     for g in range(GROUPS):
@@ -131,7 +131,7 @@
 
 def strip_kernel(own_right, own_left, far_rows, near_rows, first_got, second_got, strips, side, far, near):
     col = lax.axis_index("gx")
-    rightward = col % 2 == 0
+    rightward = col % 2 == 1
     upward = lax.axis_index("gy") % 2 == 1
     first, last = col == 0, col == lax.axis_size("gx") - 1
     lane = lanes_of(ROWS)
@@ -409,8 +409,8 @@
         space=pltpu.HBM,
         scratch=[pltpu.SMEM(a.shape, a.dtype) for a in tiles] + [pltpu.SemaphoreType.DMA((9,))],
     )(*[pltpu.with_memory_space_constraint(a, pltpu.HBM) for a in (*tiles, *inner)])
-    first_got = lax.ppermute(first, "gx", swaps("gx", 0))
-    second_got = lax.ppermute(second, "gx", swaps("gx", 1))
+    first_got = lax.ppermute(first, "gx", swaps("gx", 1))
+    second_got = lax.ppermute(second, "gx", swaps("gx", 0))
     strips, side, far, near = call(strip_kernel, [shape(GROUPS, 2, ROWS, LANES), shape(ROWS, LANES), packed, packed])(
         own_right, own_left, far, near, first_got, second_got
     )

time: 37.8 us -> 36.9 us (0.976)
  the two profiles are of different devices: /device:TPU:3 before, /device:TPU:1 now
where the time goes in v10:
time: 36.9 us; the launch traced here: 36.6 us
  starting transfers between devices  25.8 us (70%)
  Pallas kernels  5.64 us (15%)
  waiting for transfers between devices  4.46 us (12%)
  between operations  0.72 us (2%)
    ppermute x2, starting transfers between devices, swap_rows(): lax.ppermute(near, 'gy', swaps('gy', 0))  11.4 us
    ppermute x2, starting transfers between devices, swap_rows(): lax.ppermute(far, 'gy', swaps('gy', 1))  7.27 us
    ppermute x1, starting transfers between devices, on_device(): second_got = lax.ppermute(second, 'gx', swaps('gx', 0))  6.4 us
    pallas_call x4, Pallas kernels, run(): pl.pallas_call(kernel, out_shape=outs, in_specs=[pl.BlockSpec(memory_spac...  5.64 us
    ppermute x1, waiting for transfers between devices, on_device(): second_got = lax.ppermute(second, 'gx', swaps('gx', 0))  2.16 us
    ppermute x2, waiting for transfers between devices, swap_rows(): lax.ppermute(near, 'gy', swaps('gy', 0))  1.18 us
    ppermute x2, waiting for transfers between devices, swap_rows(): lax.ppermute(far, 'gy', swaps('gy', 1))  1.12 us
  transfers between devices with their start and end apart: 6, of which 3 were waited for; matrix products, arithmetic and copies ran while one was open for 0% of the time, Pallas kernels for 0%

profile of v10, /device:TPU:1, one launch (start us, length us, event | category | flops | bytes accessed | tf_op | source)
XLA Modules:
  0.0 36.6 jit_solution(3687699056810784053)
XLA Ops:
  0.6 2.0 %shard_map.112 = (f32[14,16,128]{2,1,0:T(8,128)S(1)}, f32[14,16,128]{2,1,0:T(8,128)S(1)}, f32[14,16,128]{2,1,0:T(8,128)S(1)}, f32[14,16,128]{2,1,0:T(8,128)S(1)}...) custom-call(s32[8,16]{1,0:T(8,128)} %design_in.1, ...), custom_call_target="tpu_custom_call" | custom-call | tf_op jit(solution)/shard_map/pallas_call | solution.py:386
  2.7 0.7 %collective-permute-start = (f32[14,16,128]{2,1,0:T(8,128)S(1)}, f32[14,16,128]{2,1,0:T(8,128)S(1)}, u32[]{:S(2)}, u32[]{:S(2)}) collective-permute-start(f32[14,16,128]{2,1,0:T(8,128)S(1)} %get-tuple-element.34), channel_id=1, source_target_pairs={{64,128},{128,64},{192,256},{256,192},{320,384},{384,320},{448,512... | collective-permute-start | bytes 344072 | tf_op jit(solution)/shard_map/ppermute | solution.py:412
  3.3 6.4 %collective-permute-start.1 = (f32[14,16,128]{2,1,0:T(8,128)S(1)}, f32[14,16,128]{2,1,0:T(8,128)S(1)}, u32[]{:S(2)}, u32[]{:S(2)}) collective-permute-start(f32[14,16,128]{2,1,0:T(8,128)S(1)} %get-tuple-element.35), channel_id=1, source_target_pairs={{0,64},{64,0},{128,192},{192,128},{256,320},{320,256},{384,448},{4... | collective-permute-start | bytes 344072 | tf_op jit(solution)/shard_map/ppermute | solution.py:413
  9.8 0.0 collective-permute-done.first_got
  9.8 2.2 %collective-permute-done.1.second_got = f32[14,16,128]{2,1,0:T(8,128)S(1)} collective-permute-done((f32[14,16,128]{2,1,0:T(8,128)S(1)}, f32[14,16,128]{2,1,0:T(8,128)S(1)}, u32[]{:S(2)}, u32[]{:S(2)}) %collective-permute-start.1) | collective-permute-done | bytes 114720 | tf_op jit(solution)/shard_map/ppermute | solution.py:413
  11.9 0.1 shard_map.113
  12.1 5.3 %collective-permute-start.2 = (f32[69,8,128]{2,1,0:T(8,128)S(1)}, f32[69,8,128]{2,1,0:T(8,128)S(1)}, u32[]{:S(2)}, u32[]{:S(2)}) collective-permute-start(f32[69,8,128]{2,1,0:T(8,128)S(1)} %get-tuple-element.36), channel_id=1, source_target_pairs={{1,2},{2,1},{3,4},{4,3},{5,6},{6,5},{7,8},{8,7},{9,10},{10,9},{11,... | collective-permute-start | bytes 847880 | tf_op jit(solution)/shard_map/ppermute | solution.py:377
  17.4 9.5 %collective-permute-start.3 = (f32[69,8,128]{2,1,0:T(8,128)S(1)}, f32[69,8,128]{2,1,0:T(8,128)S(1)}, u32[]{:S(2)}, u32[]{:S(2)}) collective-permute-start(f32[69,8,128]{2,1,0:T(8,128)S(1)} %get-tuple-element.37), channel_id=1, source_target_pairs={{0,1},{1,0},{2,3},{3,2},{4,5},{5,4},{6,7},{7,6},{8,9},{9,8},{10,11... | collective-permute-start | bytes 847880 | tf_op jit(solution)/shard_map/ppermute | solution.py:377
  26.9 0.0 collective-permute-done.2.far
  27.0 1.2 %collective-permute-done.3.near = f32[69,8,128]{2,1,0:T(8,128)S(1)} collective-permute-done((f32[69,8,128]{2,1,0:T(8,128)S(1)}, f32[69,8,128]{2,1,0:T(8,128)S(1)}, u32[]{:S(2)}, u32[]{:S(2)}) %collective-permute-start.3) | collective-permute-done | bytes 282656 | tf_op jit(solution)/shard_map/ppermute | solution.py:377
  28.1 2.6 %shard_map.114 = (f32[2,3,8,24,128]{4,3,2,1,0:T(8,128)S(1)}, f32[8,256]{1,0:T(8,128)S(1)}, f32[8,256]{1,0:T(8,128)S(1)}) custom-call(f32[3,24,128]{2,1,0:T(8,128)S(1)} %get-tuple-element.23.gains, f32[3,8,16,128]{3,2,1,0:T(8,128)S(1)} %get-tuple-element.24.field, f32[3,8,16,128]{3,2,1,0:T(8,128)S(1)} %get-tuple-element.25.adjoint, ...), custom_call_target="tpu_custom_call" | custom-call | tf_op jit(solution)/shard_map/pallas_call | solution.py:386
  30.7 1.9 %collective-permute-start.4 = (f32[8,256]{1,0:T(8,128)S(1)}, f32[8,256]{1,0:T(8,128)S(1)}, u32[]{:S(2)}, u32[]{:S(2)}) collective-permute-start(f32[8,256]{1,0:T(8,128)S(1)} %get-tuple-element.41.own_far), channel_id=1, source_target_pairs={{1,2},{2,1},{3,4},{4,3},{5,6},{6,5},{7,8},{8,7},{9,10},{10,9},{11,... | collective-permute-start | bytes 24584 | tf_op jit(solution)/shard_map/ppermute | solution.py:377
  32.6 1.9 %collective-permute-start.5 = (f32[8,256]{1,0:T(8,128)S(1)}, f32[8,256]{1,0:T(8,128)S(1)}, u32[]{:S(2)}, u32[]{:S(2)}) collective-permute-start(f32[8,256]{1,0:T(8,128)S(1)} %get-tuple-element.42.own_near), channel_id=1, source_target_pairs={{0,1},{1,0},{2,3},{3,2},{4,5},{5,4},{6,7},{7,6},{8,9},{9,8},{10,11... | collective-permute-start | bytes 24584 | tf_op jit(solution)/shard_map/ppermute | solution.py:377
  34.6 1.1 %collective-permute-done.4.far = f32[8,256]{1,0:T(8,128)S(1)} collective-permute-done((f32[8,256]{1,0:T(8,128)S(1)}, f32[8,256]{1,0:T(8,128)S(1)}, u32[]{:S(2)}, u32[]{:S(2)}) %collective-permute-start.4) | collective-permute-done | bytes 8224 | tf_op jit(solution)/shard_map/ppermute | solution.py:377
  35.7 0.0 collective-permute-done.5.near
  35.7 0.9 %shard_map.115 = (f32[3,8,16,128]{3,2,1,0:T(8,128)}, f32[3,8,16,128]{3,2,1,0:T(8,128)}, f32[16,128]{1,0:T(8,128)}) custom-call(f32[2,3,8,24,128]{4,3,2,1,0:T(8,128)S(1)} %get-tuple-element.40.fields, f32[8,256]{1,0:T(8,128)S(1)} %get-tuple-element.41.own_far, f32[8,256]{1,0:T(8,128)S(1)} %get-tuple-element.42.own_near, ...), custom_call_target="tpu_custom_call" | custom-call | tf_op jit(solution)/shard_map/pallas_call | solution.py:386
Async XLA Ops:
  2.7 7.1 %collective-permute-start = (f32[14,16,128]{2,1,0:T(8,128)S(1)}, f32[14,16,128]{2,1,0:T(8,128)S(1)}, u32[]{:S(2)}, u32[]{:S(2)}) collective-permute-start(f32[14,16,128]{2,1,0:T(8,128)S(1)} %get-tuple-element.34), channel_id=1, source_target_pairs={{64,128},{128,64},{192,256},{256,192},{320,384},{384,320},{448,512... | collective-permute-start | bytes 344072 | tf_op jit(solution)/shard_map/ppermute | solution.py:412
  3.3 8.6 %collective-permute-start.1 = (f32[14,16,128]{2,1,0:T(8,128)S(1)}, f32[14,16,128]{2,1,0:T(8,128)S(1)}, u32[]{:S(2)}, u32[]{:S(2)}) collective-permute-start(f32[14,16,128]{2,1,0:T(8,128)S(1)} %get-tuple-element.35), channel_id=1, source_target_pairs={{0,64},{64,0},{128,192},{192,128},{256,320},{320,256},{384,448},{4... | collective-permute-start | bytes 344072 | tf_op jit(solution)/shard_map/ppermute | solution.py:413
  12.1 14.9 %collective-permute-start.2 = (f32[69,8,128]{2,1,0:T(8,128)S(1)}, f32[69,8,128]{2,1,0:T(8,128)S(1)}, u32[]{:S(2)}, u32[]{:S(2)}) collective-permute-start(f32[69,8,128]{2,1,0:T(8,128)S(1)} %get-tuple-element.36), channel_id=1, source_target_pairs={{1,2},{2,1},{3,4},{4,3},{5,6},{6,5},{7,8},{8,7},{9,10},{10,9},{11,... | collective-permute-start | bytes 847880 | tf_op jit(solution)/shard_map/ppermute | solution.py:377
  17.4 10.7 %collective-permute-start.3 = (f32[69,8,128]{2,1,0:T(8,128)S(1)}, f32[69,8,128]{2,1,0:T(8,128)S(1)}, u32[]{:S(2)}, u32[]{:S(2)}) collective-permute-start(f32[69,8,128]{2,1,0:T(8,128)S(1)} %get-tuple-element.37), channel_id=1, source_target_pairs={{0,1},{1,0},{2,3},{3,2},{4,5},{5,4},{6,7},{7,6},{8,9},{9,8},{10,11... | collective-permute-start | bytes 847880 | tf_op jit(solution)/shard_map/ppermute | solution.py:377
  30.7 5.0 %collective-permute-start.4 = (f32[8,256]{1,0:T(8,128)S(1)}, f32[8,256]{1,0:T(8,128)S(1)}, u32[]{:S(2)}, u32[]{:S(2)}) collective-permute-start(f32[8,256]{1,0:T(8,128)S(1)} %get-tuple-element.41.own_far), channel_id=1, source_target_pairs={{1,2},{2,1},{3,4},{4,3},{5,6},{6,5},{7,8},{8,7},{9,10},{10,9},{11,... | collective-permute-start | bytes 24584 | tf_op jit(solution)/shard_map/ppermute | solution.py:377
  32.6 3.1 %collective-permute-start.5 = (f32[8,256]{1,0:T(8,128)S(1)}, f32[8,256]{1,0:T(8,128)S(1)}, u32[]{:S(2)}, u32[]{:S(2)}) collective-permute-start(f32[8,256]{1,0:T(8,128)S(1)} %get-tuple-element.42.own_near), channel_id=1, source_target_pairs={{0,1},{1,0},{2,3},{3,2},{4,5},{5,4},{6,7},{7,6},{8,9},{9,8},{10,11... | collective-permute-start | bytes 24584 | tf_op jit(solution)/shard_map/ppermute | solution.py:377

commit v11 on v10

--- a/solution.py
+++ b/solution.py
@@ -64,14 +64,13 @@
 
 
 def pack_kernel(
-    design_in, material_in, contrast_in, field_in, adjoint_in, source_in, adjoint_source_in, background_in, density_in,
-    first, second, own_right, own_left, far, near, gains, field, adjoint, source, adjoint_source, background, density,
-    design, material, contrast, done,
+    field_in, adjoint_in, source_in, adjoint_source_in, background_in, density_in,
+    first, second, own_right, own_left, far, near, field, adjoint, source, adjoint_source, background, density,
+    done,
 ):
     arrays = (
         (field_in, field), (adjoint_in, adjoint), (source_in, source), (adjoint_source_in, adjoint_source),
         (background_in, background), (density_in, density),
-        (design_in, design), (material_in, material), (contrast_in, contrast),
     )
     copies = [pltpu.make_async_copy(here, there, done.at[i]) for i, (here, there) in enumerate(arrays)]
     for copy in copies:
@@ -112,21 +111,20 @@
         far[4 * GROUPS + part] = density[8 * part : 8 * part + 8]
         near[4 * GROUPS + part] = density[8 * part : 8 * part + 8]
 
-    col, row = lax.axis_index("gx"), lax.axis_index("gy")
-    row24 = rows_of(WRAP)
+
+def gain_planes(design, material, contrast):
+    chosen = material[:, :, None] == jnp.arange(contrast.shape[0], dtype=jnp.int32)
+    tile_gain = design.astype(jnp.float32) * jnp.sum(jnp.where(chosen, contrast, 0.0), axis=2)
     tiles_y, tiles_x = design.shape
-
-    def gain_at(first, tile_x):
-        tile_y = jnp.clip(first, 0, tiles_y * TILE - 1) // TILE
-        tile_x = jnp.clip(tile_x, 0, tiles_x - 1)
-        return design[tile_y, tile_x].astype(jnp.float32) * contrast[material[tile_y, tile_x]]
-
-    for k in range(3):
-        tile_x = col + (0, 1, -1)[k]
-        here = gain_at(row * ROWS, tile_x)
-        up = gain_at(row * ROWS + ROWS, tile_x)
-        down = gain_at(row * ROWS - HALO, tile_x)
-        gains[k] = jnp.where(row24 < 16, here, jnp.where(row24 < 20, up, down))
+    place = jnp.arange(WRAP, dtype=jnp.int32)
+    place = lax.axis_index("gy") * ROWS + jnp.where(place < 20, place, place - WRAP)
+    tile_y = jnp.clip(place, 0, tiles_y * TILE - 1) // TILE
+    tile_x = jnp.clip(lax.axis_index("gx") + jnp.array([0, 1, -1], jnp.int32), 0, tiles_x - 1)
+    by_row = tile_y[:, None] == jnp.arange(tiles_y, dtype=jnp.int32)
+    by_col = tile_x[:, None] == jnp.arange(tiles_x, dtype=jnp.int32)
+    picked = by_row[None, :, :, None] & by_col[:, None, None, :]
+    gains = jnp.sum(jnp.where(picked, tile_gain[None, None], 0.0), axis=(2, 3))
+    return jnp.broadcast_to(gains[:, :, None], (3, WRAP, LANES))
 
 
 def strip_kernel(own_right, own_left, far_rows, near_rows, first_got, second_got, strips, side, far, near):
@@ -401,14 +399,14 @@
 
 def on_device(background, density, design_tiles, material_tiles, contrast, source, adjoint_source, field_start, adjoint_start):
     inner = (field_start, adjoint_start, source, adjoint_source, background, density)
-    tiles = (design_tiles, material_tiles, contrast)
+    gains = gain_planes(design_tiles, material_tiles, contrast)
     edges, rows, packed = shape(GROUPS + 1, ROWS, LANES), shape(PACKED, 8, LANES), shape(PACKED + GROUPS + 2, 8, LANES)
-    first, second, own_right, own_left, far, near, gains, *inner = call(
+    first, second, own_right, own_left, far, near, *inner = call(
         pack_kernel,
-        [edges, edges, edges, edges, rows, rows, shape(3, WRAP, LANES)] + [shape(*a.shape) for a in inner],
+        [edges, edges, edges, edges, rows, rows] + [shape(*a.shape) for a in inner],
         space=pltpu.HBM,
-        scratch=[pltpu.SMEM(a.shape, a.dtype) for a in tiles] + [pltpu.SemaphoreType.DMA((9,))],
-    )(*[pltpu.with_memory_space_constraint(a, pltpu.HBM) for a in (*tiles, *inner)])
+        scratch=[pltpu.SemaphoreType.DMA((6,))],
+    )(*[pltpu.with_memory_space_constraint(a, pltpu.HBM) for a in inner])
     first_got = lax.ppermute(first, "gx", swaps("gx", 1))
     second_got = lax.ppermute(second, "gx", swaps("gx", 0))
     strips, side, far, near = call(strip_kernel, [shape(GROUPS, 2, ROWS, LANES), shape(ROWS, LANES), packed, packed])(

time: 36.9 us -> 36.9 us (level)
  waiting for transfers between devices: 4.46 us -> 2.2 us
  local copies, waits for them, and re-layouts: 0 us -> 1.99 us
    ppermute x1, waiting for transfers between devices: 2.16 us -> 0.1 us  [on_device(): second_got = lax.ppermute(second, 'gx', swaps('gx', 0))]
    unnamed x0 -> x8, local copies, waits for them, and re-layouts: none -> 1.92 us
  transfers between devices with their start and end apart: 6 -> 6, of which waited for: 3 -> 3; matrix products, arithmetic and copies ran while one was open for 0% -> 1% of each run, Pallas kernels for 0% -> 0%
where the time goes in v11:
time: 36.9 us; the launch traced here: 36.6 us
  starting transfers between devices  25.8 us (70%)
  Pallas kernels  5.56 us (15%)
  waiting for transfers between devices  2.2 us (6%)
  local copies, waits for them, and re-layouts  1.99 us (5%)
  between operations  0.76 us (2%)
    ppermute x2, starting transfers between devices, swap_rows(): lax.ppermute(near, 'gy', swaps('gy', 0))  11.4 us
    ppermute x2, starting transfers between devices, swap_rows(): lax.ppermute(far, 'gy', swaps('gy', 1))  7.27 us
    ppermute x1, starting transfers between devices, on_device(): second_got = lax.ppermute(second, 'gx', swaps('gx', 0))  6.4 us
    pallas_call x4, Pallas kernels, run(): pl.pallas_call(kernel, out_shape=outs, in_specs=[pl.BlockSpec(memory_spac...  5.56 us
    unnamed x8, local copies, waits for them, and re-layouts  1.92 us
    ppermute x2, waiting for transfers between devices, swap_rows(): lax.ppermute(far, 'gy', swaps('gy', 1))  1.12 us
    ppermute x2, waiting for transfers between devices, swap_rows(): lax.ppermute(near, 'gy', swaps('gy', 0))  0.99 us
  transfers between devices with their start and end apart: 6, of which 3 were waited for; matrix products, arithmetic and copies ran while one was open for 1% of the time, Pallas kernels for 0%

profile of v11, /device:TPU:1, one launch (start us, length us, event | category | flops | bytes accessed | tf_op | source)
XLA Modules:
  0.0 36.6 jit_solution(1305147067202920625)
XLA Ops:
  0.6 1.9 %shard_map.121 = (f32[14,16,128]{2,1,0:T(8,128)S(1)}, f32[14,16,128]{2,1,0:T(8,128)S(1)}, f32[14,16,128]{2,1,0:T(8,128)S(1)}, f32[14,16,128]{2,1,0:T(8,128)S(1)}...) custom-call(f32[3,8,16,128]{3,2,1,0:T(8,128)} %field_in.1, ...), custom_call_target="tpu_custom_call" | custom-call | tf_op jit(solution)/shard_map/pallas_call | solution.py:384
  2.6 0.7 %collective-permute-start = (f32[14,16,128]{2,1,0:T(8,128)S(1)}, f32[14,16,128]{2,1,0:T(8,128)S(1)}, u32[]{:S(2)}, u32[]{:S(2)}) collective-permute-start(f32[14,16,128]{2,1,0:T(8,128)S(1)} %get-tuple-element.32), channel_id=1, source_target_pairs={{64,128},{128,64},{192,256},{256,192},{320,384},{384,320},{448,512... | collective-permute-start | bytes 344072 | tf_op jit(solution)/shard_map/ppermute | solution.py:410
  3.3 6.4 %collective-permute-start.1 = (f32[14,16,128]{2,1,0:T(8,128)S(1)}, f32[14,16,128]{2,1,0:T(8,128)S(1)}, u32[]{:S(2)}, u32[]{:S(2)}) collective-permute-start(f32[14,16,128]{2,1,0:T(8,128)S(1)} %get-tuple-element.33), channel_id=1, source_target_pairs={{0,64},{64,0},{128,192},{192,128},{256,320},{320,256},{384,448},{4... | collective-permute-start | bytes 344072 | tf_op jit(solution)/shard_map/ppermute | solution.py:411
  9.7 0.0 copy-start.1
  9.7 0.0 copy-start.2
  9.7 0.6 %copy-done.1 = s32[8,16]{1,0:T(8,128)S(1)} copy-done((s32[8,16]{1,0:T(8,128)S(1)}, s32[8,16]{1,0:T(8,128)}, u32[]{:S(2)}) %copy-start.1) | copy-done | bytes 536
  10.4 0.0 copy-done.2
  10.4 0.0 copy-start
  10.4 0.1 select_reduce_fusion.1
  10.5 0.6 %copy-done = s32[8,16]{1,0:T(8,128)S(1)} copy-done((s32[8,16]{1,0:T(8,128)S(1)}, s32[8,16]{1,0:T(8,128)}, u32[]{:S(2)}) %copy-start) | copy-done | bytes 536
  11.1 0.0 copy-start.3
  11.1 0.6 %copy-done.3 = s32[3]{0:T(128)S(1)} copy-done((s32[3]{0:T(128)S(1)}, s32[3]{0:T(128)}, u32[]{:S(2)}) %copy-start.3) | copy-done | bytes 36
  11.7 0.0 collective-permute-done.first_got
  11.7 0.1 collective-permute-done.1.second_got
  11.8 0.1 shard_map.122
  12.0 5.3 %collective-permute-start.2 = (f32[69,8,128]{2,1,0:T(8,128)S(1)}, f32[69,8,128]{2,1,0:T(8,128)S(1)}, u32[]{:S(2)}, u32[]{:S(2)}) collective-permute-start(f32[69,8,128]{2,1,0:T(8,128)S(1)} %get-tuple-element.34), channel_id=1, source_target_pairs={{1,2},{2,1},{3,4},{4,3},{5,6},{6,5},{7,8},{8,7},{9,10},{10,9},{11,... | collective-permute-start | bytes 847880 | tf_op jit(solution)/shard_map/ppermute | solution.py:375
  17.3 9.5 %collective-permute-start.3 = (f32[69,8,128]{2,1,0:T(8,128)S(1)}, f32[69,8,128]{2,1,0:T(8,128)S(1)}, u32[]{:S(2)}, u32[]{:S(2)}) collective-permute-start(f32[69,8,128]{2,1,0:T(8,128)S(1)} %get-tuple-element.35), channel_id=1, source_target_pairs={{0,1},{1,0},{2,3},{3,2},{4,5},{5,4},{6,7},{7,6},{8,9},{9,8},{10,11... | collective-permute-start | bytes 847880 | tf_op jit(solution)/shard_map/ppermute | solution.py:375
  26.9 0.1 iota_compare_fusion.2
  26.9 0.1 select_reduce_fusion
  27.0 0.0 collective-permute-done.2.far
  27.1 1.0 %collective-permute-done.3.near = f32[69,8,128]{2,1,0:T(8,128)S(1)} collective-permute-done((f32[69,8,128]{2,1,0:T(8,128)S(1)}, f32[69,8,128]{2,1,0:T(8,128)S(1)}, u32[]{:S(2)}, u32[]{:S(2)}) %collective-permute-start.3) | collective-permute-done | bytes 282656 | tf_op jit(solution)/shard_map/ppermute | solution.py:375
  28.0 0.1 broadcast_in_dim.39.gains
  28.1 2.6 %shard_map.123 = (f32[2,3,8,24,128]{4,3,2,1,0:T(8,128)S(1)}, f32[8,256]{1,0:T(8,128)S(1)}, f32[8,256]{1,0:T(8,128)S(1)}) custom-call(f32[3,24,128]{2,1,0:T(8,128)S(1)} %broadcast_in_dim.39.gains, f32[3,8,16,128]{3,2,1,0:T(8,128)S(1)} %get-tuple-element.22.field, f32[3,8,16,128]{3,2,1,0:T(8,128)S(1)} %get-tuple-element.23.adjoint, ...), custom_call_target="tpu_custom_call" | custom-call | tf_op jit(solution)/shard_map/pallas_call | solution.py:384
  30.7 1.9 %collective-permute-start.4 = (f32[8,256]{1,0:T(8,128)S(1)}, f32[8,256]{1,0:T(8,128)S(1)}, u32[]{:S(2)}, u32[]{:S(2)}) collective-permute-start(f32[8,256]{1,0:T(8,128)S(1)} %get-tuple-element.39.own_far), channel_id=1, source_target_pairs={{1,2},{2,1},{3,4},{4,3},{5,6},{6,5},{7,8},{8,7},{9,10},{10,9},{11,... | collective-permute-start | bytes 24584 | tf_op jit(solution)/shard_map/ppermute | solution.py:375
  32.6 1.9 %collective-permute-start.5 = (f32[8,256]{1,0:T(8,128)S(1)}, f32[8,256]{1,0:T(8,128)S(1)}, u32[]{:S(2)}, u32[]{:S(2)}) collective-permute-start(f32[8,256]{1,0:T(8,128)S(1)} %get-tuple-element.40.own_near), channel_id=1, source_target_pairs={{0,1},{1,0},{2,3},{3,2},{4,5},{5,4},{6,7},{7,6},{8,9},{9,8},{10,11... | collective-permute-start | bytes 24584 | tf_op jit(solution)/shard_map/ppermute | solution.py:375
  34.6 1.1 %collective-permute-done.4.far = f32[8,256]{1,0:T(8,128)S(1)} collective-permute-done((f32[8,256]{1,0:T(8,128)S(1)}, f32[8,256]{1,0:T(8,128)S(1)}, u32[]{:S(2)}, u32[]{:S(2)}) %collective-permute-start.4) | collective-permute-done | bytes 8224 | tf_op jit(solution)/shard_map/ppermute | solution.py:375
  35.7 0.0 collective-permute-done.5.near
  35.7 0.9 %shard_map.124 = (f32[3,8,16,128]{3,2,1,0:T(8,128)}, f32[3,8,16,128]{3,2,1,0:T(8,128)}, f32[16,128]{1,0:T(8,128)}) custom-call(f32[2,3,8,24,128]{4,3,2,1,0:T(8,128)S(1)} %get-tuple-element.38.fields, f32[8,256]{1,0:T(8,128)S(1)} %get-tuple-element.39.own_far, f32[8,256]{1,0:T(8,128)S(1)} %get-tuple-element.40.own_near, ...), custom_call_target="tpu_custom_call" | custom-call | tf_op jit(solution)/shard_map/pallas_call | solution.py:384
  (4 shorter events, 0.0 us)
Async XLA Ops:
  2.6 9.2 %collective-permute-start = (f32[14,16,128]{2,1,0:T(8,128)S(1)}, f32[14,16,128]{2,1,0:T(8,128)S(1)}, u32[]{:S(2)}, u32[]{:S(2)}) collective-permute-start(f32[14,16,128]{2,1,0:T(8,128)S(1)} %get-tuple-element.32), channel_id=1, source_target_pairs={{64,128},{128,64},{192,256},{256,192},{320,384},{384,320},{448,512... | collective-permute-start | bytes 344072 | tf_op jit(solution)/shard_map/ppermute | solution.py:410
  3.3 8.6 %collective-permute-start.1 = (f32[14,16,128]{2,1,0:T(8,128)S(1)}, f32[14,16,128]{2,1,0:T(8,128)S(1)}, u32[]{:S(2)}, u32[]{:S(2)}) collective-permute-start(f32[14,16,128]{2,1,0:T(8,128)S(1)} %get-tuple-element.33), channel_id=1, source_target_pairs={{0,64},{64,0},{128,192},{192,128},{256,320},{320,256},{384,448},{4... | collective-permute-start | bytes 344072 | tf_op jit(solution)/shard_map/ppermute | solution.py:411
  9.7 0.7 %copy-start.1 = (s32[8,16]{1,0:T(8,128)S(1)}, s32[8,16]{1,0:T(8,128)}, u32[]{:S(2)}) copy-start(s32[8,16]{1,0:T(8,128)} %param.13) | copy-start | bytes 1540
  9.7 0.7 %copy-start.2 = (f32[4]{0:T(128)S(1)}, f32[4]{0:T(128)}, u32[]{:S(2)}) copy-start(f32[4]{0:T(128)} %param.14) | copy-start | bytes 52
  10.4 0.7 %copy-start = (s32[8,16]{1,0:T(8,128)S(1)}, s32[8,16]{1,0:T(8,128)}, u32[]{:S(2)}) copy-start(s32[8,16]{1,0:T(8,128)} %param.12) | copy-start | bytes 1540
  11.1 0.7 %copy-start.3 = (s32[3]{0:T(128)S(1)}, s32[3]{0:T(128)}, u32[]{:S(2)}) copy-start(s32[3]{0:T(128)} %constant.41.clone) | copy-start | bytes 40
  12.0 15.1 %collective-permute-start.2 = (f32[69,8,128]{2,1,0:T(8,128)S(1)}, f32[69,8,128]{2,1,0:T(8,128)S(1)}, u32[]{:S(2)}, u32[]{:S(2)}) collective-permute-start(f32[69,8,128]{2,1,0:T(8,128)S(1)} %get-tuple-element.34), channel_id=1, source_target_pairs={{1,2},{2,1},{3,4},{4,3},{5,6},{6,5},{7,8},{8,7},{9,10},{10,9},{11,... | collective-permute-start | bytes 847880 | tf_op jit(solution)/shard_map/ppermute | solution.py:375
  17.3 10.7 %collective-permute-start.3 = (f32[69,8,128]{2,1,0:T(8,128)S(1)}, f32[69,8,128]{2,1,0:T(8,128)S(1)}, u32[]{:S(2)}, u32[]{:S(2)}) collective-permute-start(f32[69,8,128]{2,1,0:T(8,128)S(1)} %get-tuple-element.35), channel_id=1, source_target_pairs={{0,1},{1,0},{2,3},{3,2},{4,5},{5,4},{6,7},{7,6},{8,9},{9,8},{10,11... | collective-permute-start | bytes 847880 | tf_op jit(solution)/shard_map/ppermute | solution.py:375
  30.7 5.0 %collective-permute-start.4 = (f32[8,256]{1,0:T(8,128)S(1)}, f32[8,256]{1,0:T(8,128)S(1)}, u32[]{:S(2)}, u32[]{:S(2)}) collective-permute-start(f32[8,256]{1,0:T(8,128)S(1)} %get-tuple-element.39.own_far), channel_id=1, source_target_pairs={{1,2},{2,1},{3,4},{4,3},{5,6},{6,5},{7,8},{8,7},{9,10},{10,9},{11,... | collective-permute-start | bytes 24584 | tf_op jit(solution)/shard_map/ppermute | solution.py:375
  32.6 3.1 %collective-permute-start.5 = (f32[8,256]{1,0:T(8,128)S(1)}, f32[8,256]{1,0:T(8,128)S(1)}, u32[]{:S(2)}, u32[]{:S(2)}) collective-permute-start(f32[8,256]{1,0:T(8,128)S(1)} %get-tuple-element.40.own_near), channel_id=1, source_target_pairs={{0,1},{1,0},{2,3},{3,2},{4,5},{5,4},{6,7},{7,6},{8,9},{9,8},{10,11... | collective-permute-start | bytes 24584 | tf_op jit(solution)/shard_map/ppermute | solution.py:375
